TPU v7x, 32 devices: a whole 2x2x4 slice. The times are simulated.
32 devices in a mesh: ctx: 2 (over y), tp: 16 (over z, x, core).
Axes of the slice: x: 2, y: 2, z: 4, core: 2. Of those that a mesh axis runs over, the one named last changes fastest.
Arguments:
- streams: bfloat16 [3, 1, 768, 8192], P(None, None, 'ctx', 'tp'), may hold values from -6 to 6
- taps: float32 [3, 7, 8192], P(None, None, 'tp'), may hold values from -2.4 to 2.4
- decay: float32 [16, 8192], P(None, 'tp'), may hold values from 0.96 to 1, as said below
- residues: float32 [16, 8192], P(None, 'tp'), may hold values from -0.12 to 0.12
- init_state: float32 [1, 16, 8192], P(None, None, 'tp'), may hold values from -48 to 48
- out_weight: bfloat16 [8192, 8192], P('tp'), may hold values from -0.09375 to 0.09375
Outputs:
- mixed: bfloat16 [1, 768, 8192], P(None, 'ctx', 'tp')
Inputs may be any that keep to these rules, and one draw needn't show every extreme that they name: `decay`: each pole's factor lies strictly between 0 and 1.
All inputs are finite; a program needn't handle non-finite values.
Results may differ from a plain program's by a relative error of at most 0.0049.
Values may be sent and summed in bfloat16 or wider, within the bound.
No kernel may reach another device: no remote copies, remote signals or barrier semaphores. Data moves between devices by JAX's collectives and lax.ppermute only.
A program may use at most 128 MiB of HBM per device.

v0:
```python
import jax
import jax.numpy as jnp
from jax import lax
from jax.sharding import PartitionSpec as P


def passed_along(x, axis, by):
    peers = lax.axis_size(axis)
    pairs = [(i, i + by) for i in range(peers) if 0 <= i + by < peers]
    return lax.ppermute(x, axis, pairs)


def prefix(value, axis, join, neutral):
    count, mine = (lax.axis_size(axis), lax.axis_index(axis))
    pieces = jax.tree.map(lambda part: lax.all_gather(part, axis), value)
    total = jax.tree.map(
        lambda part, zero: jnp.full_like(part, 0) + jnp.asarray(zero, part.dtype), value, neutral
    )

    def step(position, total):
        longer = join(total, jax.tree.map(lambda part: part[position], pieces))
        return jax.tree.map(lambda new, old: jnp.where(position < mine, new, old), longer, total)

    return lax.fori_loop(0, count - 1, step, total)


def per_device(streams, taps, decay, residues, init_state, out_weight):
    highest = lax.Precision.HIGHEST
    tap_count = taps.shape[1]
    tap_lag = tap_count - 1
    length = streams.shape[2]
    rim_rows = passed_along(streams[:, :, length - tap_lag :, :], "ctx", 1)
    joined = jnp.concatenate([rim_rows, streams], axis=2).astype(jnp.float32)
    featured = jnp.zeros(streams.shape, jnp.float32)
    for tap_index in range(tap_count):
        featured = (
            featured
            + taps[:, tap_index][:, None, None, :]
            * joined[:, :, tap_lag - tap_index : tap_lag - tap_index + length, :]
        )
    queries = featured[0]
    driven = featured[1] * featured[2]
    seq_count = driven.shape[0]
    channels = driven.shape[2]
    block_len = min(128, length)
    block_count = length // block_len
    log_decay = jnp.log(decay)
    positions = jnp.arange(block_len).astype(jnp.float32)
    powers = jnp.exp(positions[:, None, None] * log_decay[None])
    kernel = jnp.einsum("tnc,nc->tc", powers, residues, precision=highest)
    offset = jnp.arange(block_len)[:, None] - jnp.arange(block_len)[None, :]
    toeplitz = jnp.where(
        (offset >= 0)[:, :, None], kernel[jnp.maximum(offset, 0)], jnp.float32(0.0)
    )
    blocked = driven.reshape(seq_count, block_count, block_len, channels)
    within = jnp.einsum("tjc,sbjc->sbtc", toeplitz, blocked, precision=highest)
    tail_pow = jnp.exp((block_len - 1 - positions)[:, None, None] * log_decay[None])
    block_end = jnp.einsum("sbjc,jnc->sbnc", blocked, tail_pow, precision=highest)
    block_decay = jnp.exp(block_len * log_decay)

    def advance(running, block_state):
        return (block_decay[None] * running + block_state, running)

    end_local, entry_local = lax.scan(
        advance, jnp.zeros(init_state.shape, jnp.float32), jnp.moveaxis(block_end, 1, 0)
    )
    shard_decay = jnp.exp(length * log_decay)

    def chain_join(earlier, later_part):
        return (earlier[0] * later_part[0], later_part[0][None] * earlier[1] + later_part[1])

    prefix_decay, prefix_state = prefix(
        (shard_decay, end_local),
        "ctx",
        chain_join,
        (jnp.ones_like(shard_decay), jnp.zeros_like(end_local)),
    )
    incoming = prefix_decay[None] * init_state + prefix_state
    block_starts = jnp.exp(
        (block_len * jnp.arange(block_count).astype(jnp.float32))[:, None, None] * log_decay[None]
    )
    entries = entry_local + block_starts[:, None] * incoming[None]
    lead_pow = jnp.exp((positions + 1.0)[:, None, None] * log_decay[None]) * residues[None]
    carried = jnp.einsum("bsnc,tnc->sbtc", entries, lead_pow, precision=highest)
    response = (within + carried).reshape(seq_count, length, channels)
    gated_out = (queries * response).astype(jnp.bfloat16)
    gated_rows = gated_out.reshape(seq_count * length, channels)
    mixed = lax.psum_scatter(
        lax.dot_general(
            out_weight, gated_rows, (((0,), (1,)), ((), ())), preferred_element_type=jnp.float32
        ),
        "tp",
        scatter_dimension=0,
        tiled=True,
    ).T
    return mixed.astype(jnp.bfloat16).reshape(seq_count, length, channels)


def solution(mesh):
    in_specs = (
        P(None, None, "ctx", "tp"),
        P(None, None, "tp"),
        P(None, "tp"),
        P(None, "tp"),
        P(None, None, "tp"),
        P("tp", None),
    )
    out_specs = P(None, "ctx", "tp")
    return jax.shard_map(
        per_device, mesh=mesh, in_specs=in_specs, out_specs=out_specs, check_vma=False
    )
```

profile of v0, /device:TPU:0, one launch (start us, length us, event | category | flops | bytes accessed | tf_op | source)
XLA Modules:
  0.0 374.0 jit_solution(5490809223708077465)
XLA Ops:
  6.5 0.0 copy-start.6
  6.5 0.0 reduce-scatter.2.cloned.1.call-start
  6.5 0.8 slice.57
  7.3 4.9 %collective-permute-start = (bf16[3,1,6,512]{3,2,1,0:T(8,128)(2,1)S(1)}, bf16[3,1,6,512]{3,2,1,0:T(8,128)(2,1)S(1)}, u32[]{:S(2)}, u32[]{:S(2)}) collective-permute-start(bf16[3,1,6,512]{3,2,1,0:T(8,128)(2,1)S(1)} %slice.57), channel_id=1, source_target_pairs={{0,16},{1,17},{2,18},{3,19},{4,20},{5,21},{6,22},{7,23},{8,24},{9,... | collective-permute-start | bytes 55304 | tf_op jit(solution)/shard_map/ppermute | solution.py:10
  12.2 0.6 broadcast_subtract_fusion
  12.8 0.5 convert_multiply_fusion
  13.3 1.2 fusion.40
  14.5 0.8 multiply_exponential_fusion
  15.3 0.0 copy-start.2
  15.3 0.1 copy.23
  15.4 0.0 copy-start.3
  15.5 0.9 copy.44
  16.4 6.0 %multiply_reduce_fusion = f32[512,128]{1,0:T(8,128)S(1)} fusion(f32[512,16]{1,0:T(8,128)S(1)} %copy.44, f32[16,512]{0,1:T(8,128)S(1)} %copy.23, f32[128]{0:T(128)S(1)} %iota_convert_fusion), kind=kLoop, calls=%fused_computation.9 | loop fusion | flops 3080192 | bytes 328192
  22.4 0.5 broadcast_add_fusion
  22.9 0.0 copy-done.2
  22.9 0.0 copy-done.6
  22.9 0.8 copy.26
  23.7 0.0 copy-done.3
  23.8 0.1 copy.36
  23.9 64.4 %gather_fusion = f32[16384,512]{1,0:T(8,128)} fusion(f32[128,512]{1,0:T(8,128)S(1)} %bitcast.82, s32[16384]{0:T(1024)S(1)} %bitcast_clamp_fusion), kind=kCustom, calls=%fused_computation | custom fusion | bytes 67174400 | tf_op jit(solution)/shard_map/gather | solution.py:53
  88.3 0.0 copy-start
  88.3 35.7 %copy.24 = f32[128,128,512]{1,0,2:T(8,128)} copy(f32[128,128,512]{2,1,0:T(8,128)} %bitcast.83) | data formatting | bytes 67108864 | tf_op jit(solution)/shard_map/gather | solution.py:53
  123.9 4.6 %all-gather = f32[32,512]{1,0:T(8,128)S(1)} all-gather(f32[16,512]{1,0:T(8,128)S(1)} %get-tuple-element.106), channel_id=2, replica_groups=mesh['ctx'=2,'tp'=16] {'ctx'}, dimensions={0}, use_global_device_ids=true | all-gather | bytes 98304 | tf_op jit(solution)/shard_map/all_gather | solution.py:15
  128.5 0.0 collective-permute-done
  128.5 0.0 copy-done
  128.5 0.4 maximum_convert_fusion
  128.9 2.0 fusion.11
  130.8 1.0 slice_multiply_fusion.7
  131.9 1.5 copy.25
  133.4 8.9 %fusion.25 = f32[3,1,16,512]{2,0,3,1:T(4,128)} fusion(f32[3,128,512]{1,0,2:T(4,128)S(1)} %copy.25, f32[128]{0:T(128)} %broadcast_subtract_fusion, f32[16,512]{0,1:T(8,128)} %copy-done.3), kind=kOutput, calls=%fused_computation.36 | convolution fusion | flops 38797312 | bytes 918016 | tf_op jit(solution)/shard_map/sbjc,jnc->sbnc/dot_general | solution.py:58
  142.3 2.1 copy.28
  144.4 4.2 %while.3 = (s32[]{:T(128)}, f32[1,16,512]{2,1,0:T(8,128)S(1)}, f32[3,1,16,512]{3,2,1,0:T(8,128)}, f32[16,512]{1,0:T(8,128)S(1)}, f32[3,1,16,512]{3,2,1,0:T(8,128)}, /*index=5*/s32[]{:T(128)}, s32[]{:T(128)}) while((s32[]{:T(128)}, f32[1,16,512]{2,1,0:T(8,128)S(1)}, f32[3,1,16,512]{3,2,1,0:T(8,128)}, f32[16,512]{1,0:T(8,128)S(1)}, ...), condition=%wide.region_1.2_spmd.clone, body=%wide.region_0.1_spmd.clone.sunk | while | flops 32771 | bytes 197212 | solution.py:64
  144.4 0.6 bitcast_dynamic-update-slice_fusion.2
  145.0 0.8 bitcast_add_fusion.2
  145.8 0.6 bitcast_dynamic-update-slice_fusion.2
  146.4 0.8 bitcast_add_fusion.2
  147.2 0.6 bitcast_dynamic-update-slice_fusion.2
  147.8 0.8 bitcast_add_fusion.2
  148.6 4.8 %all-gather.1 = f32[2,16,512]{2,1,0:T(8,128)S(1)} all-gather(f32[1,16,512]{2,1,0:T(8,128)S(1)} %get-tuple-element.55), channel_id=3, replica_groups=mesh['ctx'=2,'tp'=16] {'ctx'}, dimensions={0}, use_global_device_ids=true | all-gather | bytes 98304 | tf_op jit(solution)/shard_map/all_gather | solution.py:15
  153.4 0.8 fusion.38
  154.1 1.0 add_bitcast_fusion
  155.1 1.3 copy.29
  156.5 0.0 copy-start.1
  156.5 0.0 copy-start.4
  156.5 0.0 copy-start.5
  156.5 0.0 copy-start.7
  156.5 55.8 %fusion.22 = f32[1,3,128,512]{2,1,3,0:T(4,128)S(1)} fusion(f32[3,128,512]{1,0,2:T(4,128)S(1)} %copy.25, f32[128,128,512]{1,0,2:T(8,128)} %copy.24, pred[128,128]{1,0:T(8,128)(4,1)S(1)} %subtract_compare_fusion), kind=kOutput, calls=%fused_computation.35 | convolution fusion | flops 310378496 | bytes 35143680 | tf_op jit(solution)/shard_map/tjc,sbjc->sbtc/dot_general | solution.py:56
  212.3 0.0 copy-done.1
  212.3 0.0 copy-done.4
  212.3 0.0 copy-done.5
  212.3 0.0 copy-done.7
  212.3 6.4 %fusion.31 = f32[1,3,128,512]{2,1,3,0:T(4,128)} fusion(f32[1,3,128,512]{2,1,3,0:T(4,128)S(1)} %fusion.22, f32[3,16,512]{1,0,2:T(4,128)S(1)} %copy-done.1, f32[16,512]{0,1:T(8,128)S(1)} %copy-done.5, f32[128]{0:T(128)S(1)} %copy-done.7, f32[16,512]{0,1:T(8,128)S(1)} %copy-done.4), kind=kOutput, calls=%fused_computation.38 | convolution fusion | flops 40042496 | bytes 1737216 | tf_op jit(solution)/shard_map/bsnc,tnc->sbtc/dot_general | solution.py:84
  218.8 1.5 copy.30
  220.3 0.2 fusion.35
  220.5 9.7 %convolution_bitcast_fusion = f32[8192,384]{0,1:T(8,128)} fusion(bf16[384,512]{1,0:T(8,128)(2,1)S(1)} %fusion.35, bf16[512,8192]{1,0:T(8,128)(2,1)} %param.13), kind=kOutput, calls=%fused_computation.8 | convolution fusion | flops 3221225472 | bytes 21364736 | tf_op jit(solution)/shard_map/dot_general | solution.py:89
  230.2 0.0 reduce-scatter.2.cloned.1.call-update
  230.2 135.1 %reduce-scatter.2.cloned.1.call-done = f32[512,384]{0,1:T(8,128)} async-done(((f32[8192,384]{0,1:T(8,128)}), f32[512,384]{0,1:T(8,128)}) %reduce-scatter.2.cloned.1.call-update) | async-done | bytes 786448 | tf_op jit(solution)/shard_map/reduce_scatter | solution.py:88
  365.3 1.9 convert_bitcast_fusion
  (9 shorter events, 0.1 us)
Async XLA Ops:
  6.5 16.4 %copy-start.6 = (f32[16,512]{1,0:T(8,128)S(1)}, f32[16,512]{1,0:T(8,128)}, u32[]{:S(2)}) copy-start(f32[16,512]{1,0:T(8,128)} %param.11) | copy-start | bytes 98308
  6.5 358.7 %reduce-scatter.2.cloned.1.call-start = ((), (), s32[]{:S(2)}) async-start(), calls=%async_computation.1 | async-start | bytes 13369344 | tf_op jit(solution)/shard_map/reduce_scatter | solution.py:88
  7.3 121.2 %collective-permute-start = (bf16[3,1,6,512]{3,2,1,0:T(8,128)(2,1)S(1)}, bf16[3,1,6,512]{3,2,1,0:T(8,128)(2,1)S(1)}, u32[]{:S(2)}, u32[]{:S(2)}) collective-permute-start(bf16[3,1,6,512]{3,2,1,0:T(8,128)(2,1)S(1)} %slice.57), channel_id=1, source_target_pairs={{0,16},{1,17},{2,18},{3,19},{4,20},{5,21},{6,22},{7,23},{8,24},{9,... | collective-permute-start | bytes 55304 | tf_op jit(solution)/shard_map/ppermute | solution.py:10
  15.3 7.6 %copy-start.2 = (f32[16,512]{1,0:T(8,128)}, f32[16,512]{1,0:T(8,128)S(1)}, u32[]{:S(2)}) copy-start(f32[16,512]{1,0:T(8,128)S(1)} %get-tuple-element.108) | copy-start | bytes 98308
  15.4 8.3 %copy-start.3 = (f32[16,512]{0,1:T(8,128)}, f32[16,512]{0,1:T(8,128)S(1)}, u32[]{:S(2)}) copy-start(f32[16,512]{0,1:T(8,128)S(1)} %copy.23) | copy-start | bytes 98308
  88.3 40.2 %copy-start = (bf16[3,1,384,512]{3,2,1,0:T(8,128)(2,1)S(1)}, bf16[3,1,384,512]{3,2,1,0:T(8,128)(2,1)}, u32[]{:S(2)}) copy-start(bf16[3,1,384,512]{3,2,1,0:T(8,128)(2,1)} %param.8) | copy-start | bytes 3538948
  156.5 55.8 %copy-start.1 = (f32[3,16,512]{1,0,2:T(4,128)S(1)}, f32[3,16,512]{1,0,2:T(4,128)}, u32[]{:S(2)}) copy-start(f32[3,16,512]{1,0,2:T(4,128)} %copy.29) | copy-start | bytes 294916
  156.5 55.8 %copy-start.4 = (f32[16,512]{0,1:T(8,128)S(1)}, f32[16,512]{0,1:T(8,128)}, u32[]{:S(2)}) copy-start(f32[16,512]{0,1:T(8,128)} %copy-done.3) | copy-start | bytes 98308
  156.5 55.8 %copy-start.5 = (f32[16,512]{0,1:T(8,128)S(1)}, f32[16,512]{0,1:T(8,128)}, u32[]{:S(2)}) copy-start(f32[16,512]{0,1:T(8,128)} %copy.26) | copy-start | bytes 98308
  156.5 55.8 %copy-start.7 = (f32[128]{0:T(128)S(1)}, f32[128]{0:T(128)}, u32[]{:S(2)}) copy-start(f32[128]{0:T(128)} %broadcast_add_fusion) | copy-start | bytes 1540
Sparse Core Ops, SparseCore 0:
  230.3 134.8 reduce-scatter.1
where the time goes:
time: 376 us; the launch traced here: 374 us
  waiting for transfers between devices  135 us (36%)
  local copies, waits for them, and re-layouts  110 us (29%)
  matrix products  80.9 us (22%)
  other arithmetic  19.8 us (5%)
  between operations  13.6 us (4%)
  blocking collectives  9.35 us (2%)
  starting transfers between devices  4.87 us (1%)
    reduce_scatter x1, waiting for transfers between devices, per_device(): lax.psum_scatter(lax.dot_general(out_weight, gated_rows, (((0,), (1,)), (...  135 us
    gather x2, local copies, waits for them, and re-layouts, per_device(): kernel[jnp.maximum(offset, 0)]  100 us
    dot_general x1, matrix products, per_device(): within = jnp.einsum('tjc,sbjc->sbtc', toeplitz, blocked, precision=highest)  55.8 us
    dot_general x1, matrix products, per_device(): lax.dot_general(out_weight, gated_rows, (((0,), (1,)), ((), ())), preferr...  9.74 us
    all_gather x2, blocking collectives, prefix(): pieces = jax.tree.map(lambda part: lax.all_gather(part, axis), value)  9.35 us
    dot_general x1, matrix products, per_device(): jnp.einsum('sbjc,jnc->sbnc', blocked, tail_pow, precision=highest)  8.89 us
  transfers between devices with their start and end apart: 2, of which 1 were waited for; matrix products, arithmetic and copies ran while one was open for 30% of the time, Pallas kernels for 0%

commit v1 on v0

v1 whole, which is shorter than its diff:
```python
import functools

import jax
import jax.numpy as jnp
from jax import lax
from jax.experimental import pallas as pl
from jax.experimental.pallas import tpu as pltpu
from jax.sharding import PartitionSpec as P

F32 = jnp.float32
BF16 = jnp.bfloat16
LANES = 128
SEGS = 8
PAD = 8


def power(base, exponent):
    result, square = None, base
    while exponent:
        if exponent & 1:
            result = square if result is None else result * square
        exponent >>= 1
        if exponent:
            square = square * square
    return result


def tree_sum(terms):
    while len(terms) > 1:
        paired = [a + b for a, b in zip(terms[::2], terms[1::2])]
        terms = paired + terms[len(paired) * 2 :]
    return terms[0]


def driven_kernel(where_ref, streams_ref, taps_ref, decay_ref, init_ref, weight_ref, driven_ref, inner_ref, message_ref, sent_ref, wide_ref, sems):
    first = where_ref[0] == 0
    core = where_ref[1]
    poles = decay_ref.shape[0]
    tap_count = taps_ref.shape[1]
    length, channels = streams_ref.shape[2:]
    tiles = channels // LANES
    seg_len = length // SEGS
    width = sent_ref.shape[2]
    copies = []
    for part in range(sent_ref.shape[0]):
        column = pl.multiple_of((2 * part + 1 - core) * width, LANES)
        copy = pltpu.make_async_copy(weight_ref.at[:, pl.ds(column, width)], sent_ref.at[part], sems.at[part])
        copy.start()
        copies.append(copy)
    sublane = lax.broadcasted_iota(jnp.int32, (SEGS, LANES), 0)
    early = jnp.logical_and(sublane == 0, jnp.logical_not(first))
    for tile in range(tiles):
        lanes = slice(tile * LANES, (tile + 1) * LANES)
        for s in range(2):
            wide_ref[s, 0:PAD, :] = jnp.zeros((PAD, LANES), F32)
            wide_ref[s, PAD : PAD + length, :] = streams_ref[1 + s, 0, :, lanes].astype(F32)
        taps = [[jnp.broadcast_to(taps_ref[1 + s, i : i + 1, lanes], (SEGS, LANES)) for i in range(tap_count)] for s in range(2)]

        def row(s, j):
            return wide_ref[s, pl.ds(PAD + j, SEGS, stride=seg_len), :]

        def block(base, windows, masked):
            windows = list(windows)
            for step in range(8):
                made = []
                for s in range(2):
                    seen = list(windows[s]) + [row(s, base + step)]
                    made.append(tree_sum([taps[s][i] * seen[-1 - i] for i in range(tap_count)]))
                    windows[s] = tuple(seen[1:])
                product = made[0] * made[1]
                if masked and step < tap_count - 1:
                    product = jnp.where(early, 0.0, product)
                driven_ref[tile, base + step] = product
            return tuple(windows)

        windows = tuple(tuple(row(s, j - (tap_count - 1)) for j in range(tap_count - 1)) for s in range(2))
        windows = block(0, windows, True)
        lax.fori_loop(1, seg_len // 8, lambda b, w: block(b * 8, w, False), windows)

        decays = [jnp.broadcast_to(decay_ref[n : n + 1, lanes], (SEGS, LANES)) for n in range(poles)]

        def scan(b, states):
            states = list(states)
            for step in range(8):
                value = driven_ref[tile, b * 8 + step]
                states = [d * s + value for d, s in zip(decays, states)]
            return tuple(states)

        zero = jnp.zeros((SEGS, LANES), F32)
        ends = lax.fori_loop(0, seg_len // 8, scan, (zero,) * poles)
        for n in range(poles):
            total, factor = ends[n], power(decays[n], seg_len)
            for reach in (1, 2, 4):
                moved = jnp.where(sublane >= reach, pltpu.roll(total, reach, 0), 0.0)
                total = total + factor * moved
                factor = factor * factor
            inner_ref[tile, n] = total
            message_ref[n : n + 1, lanes] = total[SEGS - 1 : SEGS, :]
    carried = power(decay_ref[...], length) * init_ref[0]
    message_ref[0:poles, :] = message_ref[0:poles, :] + jnp.where(first, carried, 0.0)
    for s in range(3):
        message_ref[poles + s * PAD : poles + (s + 1) * PAD, :] = streams_ref[s, 0, length - 16 :, :].astype(F32)[16 - PAD :]
    for copy in copies:
        copy.wait()


def gated_kernel(where_ref, message_ref, streams_ref, taps_ref, decay_ref, residues_ref, init_ref, driven_in_ref, inner_ref, gated_ref, driven_ref, wide_ref, query_ref, head_ref, start_ref, out_ref):
    first = where_ref[0] == 0
    poles = decay_ref.shape[0]
    tap_count = taps_ref.shape[1]
    lag = tap_count - 1
    length, channels = streams_ref.shape[2:]
    tiles = channels // LANES
    seg_len = length // SEGS
    sublane = lax.broadcasted_iota(jnp.int32, (SEGS, LANES), 0)

    head = []
    for s in range(2):
        head_ref[0:PAD, :] = message_ref[poles + (1 + s) * PAD : poles + (2 + s) * PAD, :]
        head_ref[PAD : PAD + 16, :] = streams_ref[1 + s, 0, 0:16, :].astype(F32)
        head.append(tree_sum([taps_ref[1 + s, i : i + 1, :] * head_ref[PAD - i : 2 * PAD - i, :] for i in range(tap_count)]))
    head = head[0] * head[1]
    decay = decay_ref[...]
    state = jnp.where(first, init_ref[0], message_ref[0:poles, :])
    start_ref[0:poles, :] = state
    counted = jnp.where(first, 0.0, head)
    for j in range(lag):
        state = decay * state + counted[j : j + 1, :]
    start_ref[poles:, :] = state * power(decay, seg_len - lag)

    for tile in range(tiles):
        lanes = slice(tile * LANES, (tile + 1) * LANES)
        driven_ref[...] = driven_in_ref[tile]
        for j in range(lag):
            driven_ref[j, 0:1, :] = head[j : j + 1, lanes]
        wide_ref[0:PAD, :] = message_ref[poles : poles + PAD, lanes]
        wide_ref[PAD : PAD + length, :] = streams_ref[0, 0, :, lanes].astype(F32)
        taps = [jnp.broadcast_to(taps_ref[0, i : i + 1, lanes], (SEGS, LANES)) for i in range(tap_count)]

        def row(j):
            return wide_ref[pl.ds(PAD + j, SEGS, stride=seg_len), :]

        def fir(b, window):
            window = list(window)
            for step in range(8):
                window.append(row(b * 8 + step))
                query_ref[b * 8 + step] = tree_sum([taps[i] * window[-1 - i] for i in range(tap_count)])
                window = window[1:]
            return tuple(window)

        lax.fori_loop(0, seg_len // 8, fir, tuple(row(j - lag) for j in range(lag)))

        decays = [jnp.broadcast_to(decay_ref[n : n + 1, lanes], (SEGS, LANES)) for n in range(poles)]
        weights = [jnp.broadcast_to(residues_ref[n : n + 1, lanes], (SEGS, LANES)) for n in range(poles)]
        states = []
        for n in range(poles):
            factor = power(decays[n], seg_len)
            spread = jnp.broadcast_to(start_ref[poles + n : poles + n + 1, lanes], (SEGS, LANES))
            before = sublane - 1
            for bit in (1, 2, 4):
                spread = jnp.where(jnp.bitwise_and(before, bit) != 0, spread * factor, spread)
                factor = factor * factor
            entry = pltpu.roll(inner_ref[tile, n], 1, 0) + spread
            own = jnp.broadcast_to(start_ref[n : n + 1, lanes], (SEGS, LANES))
            states.append(jnp.where(sublane == 0, own, entry))

        def scan(b, states):
            states = list(states)
            for step in range(8):
                value = driven_ref[b * 8 + step]
                states = [d * s + value for d, s in zip(decays, states)]
                response = tree_sum([r * s for r, s in zip(weights, states)])
                out_ref[pl.ds(b * 8 + step, SEGS, stride=seg_len), :] = response * query_ref[b * 8 + step]
            return tuple(states)

        lax.fori_loop(0, seg_len // 8, scan, tuple(states))
        gated_ref[:, lanes] = out_ref[...].astype(BF16)


def project_kernel(where_ref, own_ref, other_ref, wos_ref, wok_ref, wts_ref, wtk_ref, send_ref, keep_ref):
    cut = wos_ref.shape[1]
    mine = jnp.concatenate([wos_ref[...], wok_ref[...]], axis=1)
    theirs = jnp.concatenate([wts_ref[0], wtk_ref[0]], axis=1)
    total = jnp.dot(own_ref[...], mine, preferred_element_type=F32) + jnp.dot(other_ref[...], theirs, preferred_element_type=F32)
    send_ref[0] = total[:, :cut].astype(BF16)
    keep_ref[0] = total[:, cut:]


def project(where, own, other, weight, swapped, order, part, cut):
    length, channels = own.shape
    halves, _, width = swapped.shape
    rest = halves // 2
    cuts = width // cut

    def relative(index, high):
        value = high << (order[0] - 1)
        count = len(order) - 1
        for place, bit in enumerate(order[1:]):
            value = value | (((index >> (count - 1 - place)) & 1) << (bit - 1))
        return value

    def column(high):
        def at(index, where_ref):
            block = relative(index, high) ^ where_ref[2]
            return (0, (2 * block + where_ref[1]) * cuts + part)

        return at

    def swapped_at(high):
        return lambda index, where_ref: (relative(index, high) ^ where_ref[2], 0, part)

    whole = pl.BlockSpec((length, channels), lambda index, where_ref: (0, 0))
    flops = 2 * length * 2 * channels * halves * cut
    moved = 2 * channels * halves * cut * 2 + 6 * rest * length * cut
    return pl.pallas_call(
        project_kernel,
        out_shape=(jax.ShapeDtypeStruct((rest, length, cut), BF16), jax.ShapeDtypeStruct((rest, length, cut), F32)),
        grid_spec=pltpu.PrefetchScalarGridSpec(
            num_scalar_prefetch=1,
            grid=(rest,),
            in_specs=[
                whole,
                whole,
                pl.BlockSpec((channels, cut), column(1)),
                pl.BlockSpec((channels, cut), column(0)),
                pl.BlockSpec((1, channels, cut), swapped_at(1)),
                pl.BlockSpec((1, channels, cut), swapped_at(0)),
            ],
            out_specs=(
                pl.BlockSpec((1, length, cut), lambda index, where_ref: (index, 0, 0)),
                pl.BlockSpec((1, length, cut), lambda index, where_ref: (index, 0, 0)),
            ),
        ),
        compiler_params=pltpu.CompilerParams(vmem_limit_bytes=24 * 1024 * 1024),
        cost_estimate=pl.CostEstimate(flops=flops, bytes_accessed=moved, transcendentals=0),
        name="project",
    )(where, own, other, weight, weight, swapped, swapped)


def across(x, bit):
    count = lax.axis_size("tp")
    return lax.ppermute(x, "tp", [(i, i ^ (1 << bit)) for i in range(count)])


def after(x, axis):
    count = lax.axis_size(axis)
    return lax.ppermute(x, axis, [(i, i + 1) for i in range(count - 1)])


def later_rounds(message, inner_end, streams, taps, decay, init_state):
    first = lax.axis_index("ctx") == 0
    poles = decay.shape[0]
    tap_count = taps.shape[1]
    lag = tap_count - 1
    length = streams.shape[2]
    rims = message[poles:].reshape(3, PAD, -1)
    joined = jnp.concatenate([rims, streams[:, 0, :PAD].astype(F32)], axis=1)
    featured = sum(taps[:, i][:, None, :] * joined[:, PAD - i : 2 * PAD - i, :] for i in range(tap_count))
    head = jnp.where(first, 0.0, featured[1] * featured[2])
    local = jnp.where(first, 0.0, inner_end)

    def one(_, incoming):
        state = jnp.where(first, init_state[0], incoming)
        for j in range(lag):
            state = decay * state + head[j][None]
        ended = jnp.where(first, inner_end, local + power(decay, length - lag) * state)
        return after(ended, "ctx")

    state = lax.fori_loop(0, lax.axis_size("ctx") - 2, one, message[:poles])
    return jnp.concatenate([state, message[poles:]], axis=0)


def per_device(streams, taps, decay, residues, init_state, out_weight):
    length, channels = streams.shape[2:]
    poles = decay.shape[0]
    tiles = channels // LANES
    seg_len = length // SEGS
    peers = lax.axis_size("tp")
    width = out_weight.shape[1] // peers
    me = lax.axis_index("tp")
    where = jnp.stack([lax.axis_index("ctx"), me & 1, me >> 1]).astype(jnp.int32)
    smem = pl.BlockSpec(memory_space=pltpu.SMEM)
    vmem = pl.BlockSpec(memory_space=pltpu.VMEM)
    hbm = pl.BlockSpec(memory_space=pl.ANY)
    rows = poles + 3 * PAD
    driven, inner, message, sent = pl.pallas_call(
        driven_kernel,
        out_shape=(
            jax.ShapeDtypeStruct((tiles, seg_len, SEGS, LANES), F32),
            jax.ShapeDtypeStruct((tiles, poles, SEGS, LANES), F32),
            jax.ShapeDtypeStruct((rows, channels), F32),
            jax.ShapeDtypeStruct((peers // 2, channels, width), BF16),
        ),
        in_specs=[smem, vmem, vmem, vmem, vmem, hbm],
        out_specs=(vmem, vmem, vmem, hbm),
        scratch_shapes=[pltpu.VMEM((2, PAD + length, LANES), F32), pltpu.SemaphoreType.DMA((peers // 2,))],
        compiler_params=pltpu.CompilerParams(vmem_limit_bytes=24 * 1024 * 1024),
        cost_estimate=pl.CostEstimate(flops=10_000_000, bytes_accessed=12_000_000, transcendentals=0),
        name="driven",
    )(where, streams, taps, decay, init_state, out_weight)
    passed = after(message, "ctx")
    swapped = across(sent, 0)
    if lax.axis_size("ctx") > 2:
        passed = later_rounds(passed, message[:poles], streams, taps, decay, init_state)
    gated = pl.pallas_call(
        gated_kernel,
        out_shape=jax.ShapeDtypeStruct((length, channels), BF16),
        in_specs=[smem] + [vmem] * 8,
        out_specs=vmem,
        scratch_shapes=[
            pltpu.VMEM((seg_len, SEGS, LANES), F32),
            pltpu.VMEM((PAD + length, LANES), F32),
            pltpu.VMEM((seg_len, SEGS, LANES), F32),
            pltpu.VMEM((PAD + 16, channels), F32),
            pltpu.VMEM((2 * poles, channels), F32),
            pltpu.VMEM((length, LANES), F32),
        ],
        compiler_params=pltpu.CompilerParams(vmem_limit_bytes=24 * 1024 * 1024),
        cost_estimate=pl.CostEstimate(flops=10_000_000, bytes_accessed=3_000_000, transcendentals=0),
        name="gated",
    )(where, passed, streams, taps, decay, residues, init_state, driven, inner)
    other = across(gated, 0)

    bits = tuple(range(1, peers.bit_length() - 1))
    cut = LANES
    finished = []
    for part in range(width // cut):
        order = bits
        send, keep = project(where, gated, other, out_weight, swapped, order, part, cut)
        for place, bit in enumerate(order):
            received = across(send, bit).astype(F32)
            total = keep + received
            half = total.shape[0] // 2
            if place + 1 < len(order):
                send, keep = total[half:].astype(BF16), total[:half]
            else:
                finished.append(total[0].astype(BF16))
    return jnp.concatenate(finished, axis=-1)[None]


def solution(mesh):
    in_specs = (
        P(None, None, "ctx", "tp"),
        P(None, None, "tp"),
        P(None, "tp"),
        P(None, "tp"),
        P(None, None, "tp"),
        P("tp", None),
    )
    out_specs = P(None, "ctx", "tp")
    return jax.shard_map(
        per_device, mesh=mesh, in_specs=in_specs, out_specs=out_specs, check_vma=False
    )
```

time: 376 us -> 85.5 us (0.23)
  local copies, waits for them, and re-layouts: 110 us -> 7.14 us
  waiting for transfers between devices: 135 us -> 34.6 us
  matrix products: 80.9 us -> 0 us
  starting transfers between devices: 4.87 us -> 23.9 us
  other arithmetic: 19.8 us -> 1.37 us
  Pallas kernels: 0 us -> 17.9 us
  between operations: 13.6 us -> 0.2 us
  blocking collectives: 9.35 us -> 0 us
    reduce_scatter x1 -> x0, waiting for transfers between devices: 135 us -> none  [per_device(): lax.psum_scatter(lax.dot_general(out_weight, gated_rows, (((0,), (1,)), (...]
    gather x2 -> x0, local copies, waits for them, and re-layouts: 100 us -> none  [per_device(): kernel[jnp.maximum(offset, 0)]]
    dot_general x4 -> x0, matrix products: 80.9 us -> none  [the longest x1 55.8 us: per_device(): within = jnp.einsum('tjc,sbjc->sbtc', toeplitz, blocked, precision=highest)]
    ppermute x1 -> x15, waiting for transfers between devices: 0.01 us -> 34.6 us  [the longest x14 32.3 us: across(): return lax.ppermute(x, 'tp', [(i, i ^ 1 << bit) for i in range(count)])]
    ppermute x1 -> x15, starting transfers between devices: 4.87 us -> 23.9 us  [the longest x14 19.5 us: across(): return lax.ppermute(x, 'tp', [(i, i ^ 1 << bit) for i in range(count)])]
    pallas_call x0 -> x6, Pallas kernels: none -> 17.9 us  [the longest x4 11.2 us: project(): pl.pallas_call(project_kernel, out_shape=(jax.ShapeDtypeStruct((rest, len...]
    all_gather x2 -> x0, blocking collectives: 9.35 us -> none  [prefix(): pieces = jax.tree.map(lambda part: lax.all_gather(part, axis), value)]
    unnamed x2 -> x0, other arithmetic: 5.97 us -> none
  transfers between devices with their start and end apart: 2 -> 15, of which waited for: 1 -> 9; matrix products, arithmetic and copies ran while one was open for 30% -> 1% of each run, Pallas kernels for 0% -> 14%
where the time goes in v1:
time: 85.5 us; the launch traced here: 85.2 us
  waiting for transfers between devices  34.6 us (40%)
  starting transfers between devices  23.9 us (28%)
  Pallas kernels  17.9 us (21%)
  local copies, waits for them, and re-layouts  7.14 us (8%)
  other arithmetic  1.37 us (2%)
    ppermute x14, waiting for transfers between devices, across(): return lax.ppermute(x, 'tp', [(i, i ^ 1 << bit) for i in range(count)])  32.3 us
    ppermute x14, starting transfers between devices, across(): return lax.ppermute(x, 'tp', [(i, i ^ 1 << bit) for i in range(count)])  19.5 us
    pallas_call x4, Pallas kernels, project(): pl.pallas_call(project_kernel, out_shape=(jax.ShapeDtypeStruct((rest, len...  11.2 us
    unnamed x14, local copies, waits for them, and re-layouts  6.97 us
    ppermute x1, starting transfers between devices, after(): return lax.ppermute(x, axis, [(i, i + 1) for i in range(count - 1)])  4.44 us
    pallas_call x1, Pallas kernels, per_device(): pl.pallas_call(driven_kernel, out_shape=(jax.ShapeDtypeStruct((tiles, seg...  3.43 us
    pallas_call x1, Pallas kernels, per_device(): pl.pallas_call(gated_kernel, out_shape=jax.ShapeDtypeStruct((length, chan...  3.3 us
    ppermute x1, waiting for transfers between devices, after(): return lax.ppermute(x, axis, [(i, i + 1) for i in range(count - 1)])  2.33 us
  transfers between devices with their start and end apart: 15, of which 9 were waited for; matrix products, arithmetic and copies ran while one was open for 1% of the time, Pallas kernels for 14%

profile of v1, /device:TPU:0, one launch (start us, length us, event | category | flops | bytes accessed | tf_op | source)
XLA Modules:
  0.0 85.2 jit_solution(18211800312025876012)
XLA Ops:
  0.0 0.1 pad_add_fusion.where_ref
  0.1 0.0 copy-start
  0.1 3.4 %copy-done = bf16[512,8192]{1,0:T(8,128)(2,1)S(1)} copy-done((bf16[512,8192]{1,0:T(8,128)(2,1)S(1)}, bf16[512,8192]{1,0:T(8,128)(2,1)}, u32[]{:S(2)}) %copy-start) | copy-done | bytes 8388632
  3.5 0.0 copy-start.2
  3.5 1.3 %copy-done.2 = bf16[3,1,384,512]{3,2,1,0:T(8,128)(2,1)S(1)} copy-done((bf16[3,1,384,512]{3,2,1,0:T(8,128)(2,1)S(1)}, bf16[3,1,384,512]{3,2,1,0:T(8,128)(2,1)}, u32[]{:S(2)}) %copy-start.2) | copy-done | bytes 1179672
  4.7 0.0 copy-start.3
  4.7 0.8 copy-done.3
  5.5 0.0 copy-start.4
  5.5 0.8 copy-done.4
  6.3 0.0 copy-start.5
  6.3 0.8 copy-done.5
  7.0 0.0 copy-start.6
  7.0 0.0 copy-start.1
  7.1 3.4 %driven.1 = (f32[4,48,8,128]{3,2,1,0:T(8,128)S(1)}, f32[4,16,8,128]{3,2,1,0:T(8,128)S(1)}, f32[40,512]{1,0:T(8,128)S(1)}, bf16[8,512,512]{2,1,0:T(8,128)(2,1)S(1)}) custom-call(s32[3]{0:T(128)S(1)} %pad_add_fusion.where_ref, bf16[3,1,384,512]{3,2,1,0:T(8,128)(2,1)S(1)} %copy-done.2, f32[3,7,512]{2,1,0:T(8,128)S(1)} %copy-done.3, f32[16,512]{1,0:T(8,128)S(1)} %copy-done.4, ...), custom_call_target="tpu_custom_call" | custom-call | flops 10000000 | bytes 12000000 | tf_op jit(solution)/shard_map/driven/pallas_call | solution.py:286
  10.5 0.5 collective-permute-start.2
  11.0 4.4 %collective-permute-start = (f32[40,512]{1,0:T(8,128)S(1)}, f32[40,512]{1,0:T(8,128)S(1)}, u32[]{:S(2)}, u32[]{:S(2)}) collective-permute-start(f32[40,512]{1,0:T(8,128)S(1)} %get-tuple-element.17), channel_id=1, source_target_pairs={{0,16},{1,17},{2,18},{3,19},{4,20},{5,21},{6,22},{7,23},{8,24},{9,... | collective-permute-start | bytes 245768 | tf_op jit(solution)/shard_map/ppermute | solution.py:247
  15.5 2.3 %collective-permute-done.message_ref = f32[40,512]{1,0:T(8,128)S(1)} collective-permute-done((f32[40,512]{1,0:T(8,128)S(1)}, f32[40,512]{1,0:T(8,128)S(1)}, u32[]{:S(2)}, u32[]{:S(2)}) %collective-permute-start) | collective-permute-done | bytes 81952 | tf_op jit(solution)/shard_map/ppermute | solution.py:247
  17.8 0.0 copy-done.6
  17.8 3.3 %gated.1.own_ref = bf16[384,512]{1,0:T(8,128)(2,1)S(1)} custom-call(s32[3]{0:T(128)S(1)} %pad_add_fusion.where_ref, f32[40,512]{1,0:T(8,128)S(1)} %collective-permute-done.message_ref, bf16[3,1,384,512]{3,2,1,0:T(8,128)(2,1)S(1)} %copy-done.2, f32[3,7,512]{2,1,0:T(8,128)S(1)} %copy-done.3, f32[16,512]{1,0:T(8,128)S(1)} %copy-done.4, ...), custom_call_target="tpu_custom_call" | custom-call | flops 10000000 | bytes 3000000 | tf_op jit(solution)/shard_map/gated/pallas_call | solution.py:305
  21.1 0.1 collective-permute-start.1
  21.2 1.7 %collective-permute-done.1.other_ref = bf16[384,512]{1,0:T(8,128)(2,1)S(1)} collective-permute-done((bf16[384,512]{1,0:T(8,128)(2,1)S(1)}, bf16[384,512]{1,0:T(8,128)(2,1)S(1)}, u32[]{:S(2)}, u32[]{:S(2)}) %collective-permute-start.1) | collective-permute-done | bytes 393248 | tf_op jit(solution)/shard_map/ppermute | solution.py:242
  22.9 0.0 collective-permute-done.2.wts_ref.wtk_ref
  22.9 0.0 copy-done.1
  22.9 2.8 %project.7 = (bf16[4,384,128]{2,1,0:T(8,128)(2,1)S(1)}, f32[4,384,128]{2,1,0:T(8,128)S(1)}) custom-call(s32[3]{0:T(128)S(1)} %pad_add_fusion.where_ref, bf16[384,512]{1,0:T(8,128)(2,1)S(1)} %gated.1.own_ref, bf16[384,512]{1,0:T(8,128)(2,1)S(1)} %collective-permute-done.1.other_ref, bf16[512,8192]{1,0:T(8,128)(2,1)S(1)} %copy-done.1, ...), custom_call_target="tpu_custom_call" | custom-call | flops 805306368 | bytes 3276800 | tf_op jit(solution)/shard_map/project/pallas_call | solution.py:215
  25.7 1.6 %collective-permute-start.12 = (bf16[4,384,128]{2,1,0:T(8,128)(2,1)S(1)}, bf16[4,384,128]{2,1,0:T(8,128)(2,1)S(1)}, u32[]{:S(2)}, u32[]{:S(2)}) collective-permute-start(bf16[4,384,128]{2,1,0:T(8,128)(2,1)S(1)} %get-tuple-element.28), channel_id=1, source_target_pairs={{0,2},{1,3},{2,0},{3,1},{4,6},{5,7},{6,4},{7,5},{8,10},{9,11},{10,... | collective-permute-start | bytes 1179656 | tf_op jit(solution)/shard_map/ppermute | solution.py:242
  27.3 2.8 %project.6 = (bf16[4,384,128]{2,1,0:T(8,128)(2,1)S(1)}, f32[4,384,128]{2,1,0:T(8,128)S(1)}) custom-call(s32[3]{0:T(128)S(1)} %pad_add_fusion.where_ref, bf16[384,512]{1,0:T(8,128)(2,1)S(1)} %gated.1.own_ref, bf16[384,512]{1,0:T(8,128)(2,1)S(1)} %collective-permute-done.1.other_ref, bf16[512,8192]{1,0:T(8,128)(2,1)S(1)} %copy-done.1, ...), custom_call_target="tpu_custom_call" | custom-call | flops 805306368 | bytes 3276800 | tf_op jit(solution)/shard_map/project/pallas_call | solution.py:215
  30.1 0.6 collective-permute-start.9
  30.7 2.8 %project.5 = (bf16[4,384,128]{2,1,0:T(8,128)(2,1)S(1)}, f32[4,384,128]{2,1,0:T(8,128)S(1)}) custom-call(s32[3]{0:T(128)S(1)} %pad_add_fusion.where_ref, bf16[384,512]{1,0:T(8,128)(2,1)S(1)} %gated.1.own_ref, bf16[384,512]{1,0:T(8,128)(2,1)S(1)} %collective-permute-done.1.other_ref, bf16[512,8192]{1,0:T(8,128)(2,1)S(1)} %copy-done.1, ...), custom_call_target="tpu_custom_call" | custom-call | flops 805306368 | bytes 3276800 | tf_op jit(solution)/shard_map/project/pallas_call | solution.py:215
  33.5 1.6 %collective-permute-start.6 = (bf16[4,384,128]{2,1,0:T(8,128)(2,1)S(1)}, bf16[4,384,128]{2,1,0:T(8,128)(2,1)S(1)}, u32[]{:S(2)}, u32[]{:S(2)}) collective-permute-start(bf16[4,384,128]{2,1,0:T(8,128)(2,1)S(1)} %get-tuple-element.24), channel_id=1, source_target_pairs={{0,2},{1,3},{2,0},{3,1},{4,6},{5,7},{6,4},{7,5},{8,10},{9,11},{10,... | collective-permute-start | bytes 1179656 | tf_op jit(solution)/shard_map/ppermute | solution.py:242
  35.0 2.8 %project.4 = (bf16[4,384,128]{2,1,0:T(8,128)(2,1)S(1)}, f32[4,384,128]{2,1,0:T(8,128)S(1)}) custom-call(s32[3]{0:T(128)S(1)} %pad_add_fusion.where_ref, bf16[384,512]{1,0:T(8,128)(2,1)S(1)} %gated.1.own_ref, bf16[384,512]{1,0:T(8,128)(2,1)S(1)} %collective-permute-done.1.other_ref, bf16[512,8192]{1,0:T(8,128)(2,1)S(1)} %copy-done.1, ...), custom_call_target="tpu_custom_call" | custom-call | flops 805306368 | bytes 3276800 | tf_op jit(solution)/shard_map/project/pallas_call | solution.py:215
  37.9 0.6 collective-permute-start.3
  38.5 0.0 collective-permute-done.12
  38.5 0.1 convert_add_fusion
  38.6 1.6 %collective-permute-start.13 = (bf16[2,384,128]{2,1,0:T(8,128)(2,1)S(1)}, bf16[2,384,128]{2,1,0:T(8,128)(2,1)S(1)}, u32[]{:S(2)}, u32[]{:S(2)}) collective-permute-start(bf16[2,384,128]{2,1,0:T(8,128)(2,1)S(1)} %slice.120), channel_id=1, source_target_pairs={{0,4},{1,5},{2,6},{3,7},{4,0},{5,1},{6,2},{7,3},{8,12},{9,13},{10,... | collective-permute-start | bytes 589832 | tf_op jit(solution)/shard_map/ppermute | solution.py:242
  40.2 5.9 %collective-permute-done.9 = bf16[4,384,128]{2,1,0:T(8,128)(2,1)S(1)} collective-permute-done((bf16[4,384,128]{2,1,0:T(8,128)(2,1)S(1)}, bf16[4,384,128]{2,1,0:T(8,128)(2,1)S(1)}, u32[]{:S(2)}, u32[]{:S(2)}) %collective-permute-start.9) | collective-permute-done | bytes 393248 | tf_op jit(solution)/shard_map/ppermute | solution.py:242
  46.1 0.1 convert_add_fusion.1
  46.3 1.6 %collective-permute-start.10 = (bf16[2,384,128]{2,1,0:T(8,128)(2,1)S(1)}, bf16[2,384,128]{2,1,0:T(8,128)(2,1)S(1)}, u32[]{:S(2)}, u32[]{:S(2)}) collective-permute-start(bf16[2,384,128]{2,1,0:T(8,128)(2,1)S(1)} %slice.121), channel_id=1, source_target_pairs={{0,4},{1,5},{2,6},{3,7},{4,0},{5,1},{6,2},{7,3},{8,12},{9,13},{10,... | collective-permute-start | bytes 589832 | tf_op jit(solution)/shard_map/ppermute | solution.py:242
  47.9 6.7 %collective-permute-done.6 = bf16[4,384,128]{2,1,0:T(8,128)(2,1)S(1)} collective-permute-done((bf16[4,384,128]{2,1,0:T(8,128)(2,1)S(1)}, bf16[4,384,128]{2,1,0:T(8,128)(2,1)S(1)}, u32[]{:S(2)}, u32[]{:S(2)}) %collective-permute-start.6) | collective-permute-done | bytes 393248 | tf_op jit(solution)/shard_map/ppermute | solution.py:242
  54.6 0.1 convert_add_fusion.2
  54.7 1.6 %collective-permute-start.7 = (bf16[2,384,128]{2,1,0:T(8,128)(2,1)S(1)}, bf16[2,384,128]{2,1,0:T(8,128)(2,1)S(1)}, u32[]{:S(2)}, u32[]{:S(2)}) collective-permute-start(bf16[2,384,128]{2,1,0:T(8,128)(2,1)S(1)} %slice.122), channel_id=1, source_target_pairs={{0,4},{1,5},{2,6},{3,7},{4,0},{5,1},{6,2},{7,3},{8,12},{9,13},{10,... | collective-permute-start | bytes 589832 | tf_op jit(solution)/shard_map/ppermute | solution.py:242
  56.3 5.9 %collective-permute-done.3 = bf16[4,384,128]{2,1,0:T(8,128)(2,1)S(1)} collective-permute-done((bf16[4,384,128]{2,1,0:T(8,128)(2,1)S(1)}, bf16[4,384,128]{2,1,0:T(8,128)(2,1)S(1)}, u32[]{:S(2)}, u32[]{:S(2)}) %collective-permute-start.3) | collective-permute-done | bytes 393248 | tf_op jit(solution)/shard_map/ppermute | solution.py:242
  62.2 0.1 convert_add_fusion.3
  62.3 1.6 %collective-permute-start.4 = (bf16[2,384,128]{2,1,0:T(8,128)(2,1)S(1)}, bf16[2,384,128]{2,1,0:T(8,128)(2,1)S(1)}, u32[]{:S(2)}, u32[]{:S(2)}) collective-permute-start(bf16[2,384,128]{2,1,0:T(8,128)(2,1)S(1)} %slice.123), channel_id=1, source_target_pairs={{0,4},{1,5},{2,6},{3,7},{4,0},{5,1},{6,2},{7,3},{8,12},{9,13},{10,... | collective-permute-start | bytes 589832 | tf_op jit(solution)/shard_map/ppermute | solution.py:242
  64.0 0.0 collective-permute-done.13
  64.0 2.7 %collective-permute-start.14 = (bf16[1,384,128]{2,1,0:T(8,128)(2,1)S(1)}, bf16[1,384,128]{2,1,0:T(8,128)(2,1)S(1)}, u32[]{:S(2)}, u32[]{:S(2)}) collective-permute-start(bf16[1,384,128]{2,1,0:T(8,128)(2,1)S(1)} %slice.124), channel_id=1, source_target_pairs={{0,8},{1,9},{2,10},{3,11},{4,12},{5,13},{6,14},{7,15},{8,0},{9,1},... | collective-permute-start | bytes 294920 | tf_op jit(solution)/shard_map/ppermute | solution.py:242
  66.7 0.0 collective-permute-done.10
  66.7 0.4 collective-permute-start.11
  67.1 0.0 collective-permute-done.7
  67.2 2.7 %collective-permute-start.8 = (bf16[1,384,128]{2,1,0:T(8,128)(2,1)S(1)}, bf16[1,384,128]{2,1,0:T(8,128)(2,1)S(1)}, u32[]{:S(2)}, u32[]{:S(2)}) collective-permute-start(bf16[1,384,128]{2,1,0:T(8,128)(2,1)S(1)} %slice.126), channel_id=1, source_target_pairs={{0,8},{1,9},{2,10},{3,11},{4,12},{5,13},{6,14},{7,15},{8,0},{9,1},... | collective-permute-start | bytes 294920 | tf_op jit(solution)/shard_map/ppermute | solution.py:242
  69.8 0.9 %collective-permute-done.4 = bf16[2,384,128]{2,1,0:T(8,128)(2,1)S(1)} collective-permute-done((bf16[2,384,128]{2,1,0:T(8,128)(2,1)S(1)}, bf16[2,384,128]{2,1,0:T(8,128)(2,1)S(1)}, u32[]{:S(2)}, u32[]{:S(2)}) %collective-permute-start.4) | collective-permute-done | bytes 196640 | tf_op jit(solution)/shard_map/ppermute | solution.py:242
  70.9 2.3 %collective-permute-start.5 = (bf16[1,384,128]{2,1,0:T(8,128)(2,1)S(1)}, bf16[1,384,128]{2,1,0:T(8,128)(2,1)S(1)}, u32[]{:S(2)}, u32[]{:S(2)}) collective-permute-start(bf16[1,384,128]{2,1,0:T(8,128)(2,1)S(1)} %slice.127), channel_id=1, source_target_pairs={{0,8},{1,9},{2,10},{3,11},{4,12},{5,13},{6,14},{7,15},{8,0},{9,1},... | collective-permute-start | bytes 294920 | tf_op jit(solution)/shard_map/ppermute | solution.py:242
  73.1 0.0 collective-permute-done.14
  73.2 7.7 %collective-permute-done.11 = bf16[1,384,128]{2,1,0:T(8,128)(2,1)S(1)} collective-permute-done((bf16[1,384,128]{2,1,0:T(8,128)(2,1)S(1)}, bf16[1,384,128]{2,1,0:T(8,128)(2,1)S(1)}, u32[]{:S(2)}, u32[]{:S(2)}) %collective-permute-start.11) | collective-permute-done | bytes 98336 | tf_op jit(solution)/shard_map/ppermute | solution.py:242
  80.9 2.1 %collective-permute-done.8 = bf16[1,384,128]{2,1,0:T(8,128)(2,1)S(1)} collective-permute-done((bf16[1,384,128]{2,1,0:T(8,128)(2,1)S(1)}, bf16[1,384,128]{2,1,0:T(8,128)(2,1)S(1)}, u32[]{:S(2)}, u32[]{:S(2)}) %collective-permute-start.8) | collective-permute-done | bytes 98336 | tf_op jit(solution)/shard_map/ppermute | solution.py:242
  83.0 1.3 %collective-permute-done.5 = bf16[1,384,128]{2,1,0:T(8,128)(2,1)S(1)} collective-permute-done((bf16[1,384,128]{2,1,0:T(8,128)(2,1)S(1)}, bf16[1,384,128]{2,1,0:T(8,128)(2,1)S(1)}, u32[]{:S(2)}, u32[]{:S(2)}) %collective-permute-start.5) | collective-permute-done | bytes 98336 | tf_op jit(solution)/shard_map/ppermute | solution.py:242
  84.4 0.8 maximum_bitcast_fusion
  (16 shorter events, 0.4 us)
Async XLA Ops:
  0.1 3.4 %copy-start = (bf16[512,8192]{1,0:T(8,128)(2,1)S(1)}, bf16[512,8192]{1,0:T(8,128)(2,1)}, u32[]{:S(2)}) copy-start(bf16[512,8192]{1,0:T(8,128)(2,1)} %wok_ref.7) | copy-start | bytes 25165828
  3.5 1.3 %copy-start.2 = (bf16[3,1,384,512]{3,2,1,0:T(8,128)(2,1)S(1)}, bf16[3,1,384,512]{3,2,1,0:T(8,128)(2,1)}, u32[]{:S(2)}) copy-start(bf16[3,1,384,512]{3,2,1,0:T(8,128)(2,1)} %streams_ref.3) | copy-start | bytes 3538948
  4.7 0.8 copy-start.3
  5.5 0.8 copy-start.4
  6.3 0.8 copy-start.5
  7.0 10.7 %copy-start.6 = (f32[16,512]{1,0:T(8,128)S(1)}, f32[16,512]{1,0:T(8,128)}, u32[]{:S(2)}) copy-start(f32[16,512]{1,0:T(8,128)} %residues_ref.1) | copy-start | bytes 98308
  7.0 15.8 %copy-start.1 = (bf16[512,8192]{1,0:T(8,128)(2,1)S(1)}, bf16[512,8192]{1,0:T(8,128)(2,1)}, u32[]{:S(2)}) copy-start(bf16[512,8192]{1,0:T(8,128)(2,1)} %wok_ref.7) | copy-start | bytes 25165828
  10.5 12.4 %collective-permute-start.2 = (bf16[8,512,512]{2,1,0:T(8,128)(2,1)S(1)}, bf16[8,512,512]{2,1,0:T(8,128)(2,1)S(1)}, u32[]{:S(2)}, u32[]{:S(2)}) collective-permute-start(bf16[8,512,512]{2,1,0:T(8,128)(2,1)S(1)} %get-tuple-element.20), channel_id=1, source_target_pairs={{0,1},{1,0},{2,3},{3,2},{4,5},{5,4},{6,7},{7,6},{8,9},{9,8},{10,11... | collective-permute-start | bytes 12582920 | tf_op jit(solution)/shard_map/ppermute | solution.py:242
  11.0 6.8 %collective-permute-start = (f32[40,512]{1,0:T(8,128)S(1)}, f32[40,512]{1,0:T(8,128)S(1)}, u32[]{:S(2)}, u32[]{:S(2)}) collective-permute-start(f32[40,512]{1,0:T(8,128)S(1)} %get-tuple-element.17), channel_id=1, source_target_pairs={{0,16},{1,17},{2,18},{3,19},{4,20},{5,21},{6,22},{7,23},{8,24},{9,... | collective-permute-start | bytes 245768 | tf_op jit(solution)/shard_map/ppermute | solution.py:247
  21.1 1.8 %collective-permute-start.1 = (bf16[384,512]{1,0:T(8,128)(2,1)S(1)}, bf16[384,512]{1,0:T(8,128)(2,1)S(1)}, u32[]{:S(2)}, u32[]{:S(2)}) collective-permute-start(bf16[384,512]{1,0:T(8,128)(2,1)S(1)} %gated.1.own_ref), channel_id=1, source_target_pairs={{0,1},{1,0},{2,3},{3,2},{4,5},{5,4},{6,7},{7,6},{8,9},{9,8},{10,11... | collective-permute-start | bytes 1179656 | tf_op jit(solution)/shard_map/ppermute | solution.py:242
  25.7 12.8 %collective-permute-start.12 = (bf16[4,384,128]{2,1,0:T(8,128)(2,1)S(1)}, bf16[4,384,128]{2,1,0:T(8,128)(2,1)S(1)}, u32[]{:S(2)}, u32[]{:S(2)}) collective-permute-start(bf16[4,384,128]{2,1,0:T(8,128)(2,1)S(1)} %get-tuple-element.28), channel_id=1, source_target_pairs={{0,2},{1,3},{2,0},{3,1},{4,6},{5,7},{6,4},{7,5},{8,10},{9,11},{10,... | collective-permute-start | bytes 1179656 | tf_op jit(solution)/shard_map/ppermute | solution.py:242
  30.1 16.1 %collective-permute-start.9 = (bf16[4,384,128]{2,1,0:T(8,128)(2,1)S(1)}, bf16[4,384,128]{2,1,0:T(8,128)(2,1)S(1)}, u32[]{:S(2)}, u32[]{:S(2)}) collective-permute-start(bf16[4,384,128]{2,1,0:T(8,128)(2,1)S(1)} %get-tuple-element.26), channel_id=1, source_target_pairs={{0,2},{1,3},{2,0},{3,1},{4,6},{5,7},{6,4},{7,5},{8,10},{9,11},{10,... | collective-permute-start | bytes 1179656 | tf_op jit(solution)/shard_map/ppermute | solution.py:242
  33.5 21.1 %collective-permute-start.6 = (bf16[4,384,128]{2,1,0:T(8,128)(2,1)S(1)}, bf16[4,384,128]{2,1,0:T(8,128)(2,1)S(1)}, u32[]{:S(2)}, u32[]{:S(2)}) collective-permute-start(bf16[4,384,128]{2,1,0:T(8,128)(2,1)S(1)} %get-tuple-element.24), channel_id=1, source_target_pairs={{0,2},{1,3},{2,0},{3,1},{4,6},{5,7},{6,4},{7,5},{8,10},{9,11},{10,... | collective-permute-start | bytes 1179656 | tf_op jit(solution)/shard_map/ppermute | solution.py:242
  37.9 24.3 %collective-permute-start.3 = (bf16[4,384,128]{2,1,0:T(8,128)(2,1)S(1)}, bf16[4,384,128]{2,1,0:T(8,128)(2,1)S(1)}, u32[]{:S(2)}, u32[]{:S(2)}) collective-permute-start(bf16[4,384,128]{2,1,0:T(8,128)(2,1)S(1)} %get-tuple-element.22), channel_id=1, source_target_pairs={{0,2},{1,3},{2,0},{3,1},{4,6},{5,7},{6,4},{7,5},{8,10},{9,11},{10,... | collective-permute-start | bytes 1179656 | tf_op jit(solution)/shard_map/ppermute | solution.py:242
  38.6 25.4 %collective-permute-start.13 = (bf16[2,384,128]{2,1,0:T(8,128)(2,1)S(1)}, bf16[2,384,128]{2,1,0:T(8,128)(2,1)S(1)}, u32[]{:S(2)}, u32[]{:S(2)}) collective-permute-start(bf16[2,384,128]{2,1,0:T(8,128)(2,1)S(1)} %slice.120), channel_id=1, source_target_pairs={{0,4},{1,5},{2,6},{3,7},{4,0},{5,1},{6,2},{7,3},{8,12},{9,13},{10,... | collective-permute-start | bytes 589832 | tf_op jit(solution)/shard_map/ppermute | solution.py:242
  46.3 20.4 %collective-permute-start.10 = (bf16[2,384,128]{2,1,0:T(8,128)(2,1)S(1)}, bf16[2,384,128]{2,1,0:T(8,128)(2,1)S(1)}, u32[]{:S(2)}, u32[]{:S(2)}) collective-permute-start(bf16[2,384,128]{2,1,0:T(8,128)(2,1)S(1)} %slice.121), channel_id=1, source_target_pairs={{0,4},{1,5},{2,6},{3,7},{4,0},{5,1},{6,2},{7,3},{8,12},{9,13},{10,... | collective-permute-start | bytes 589832 | tf_op jit(solution)/shard_map/ppermute | solution.py:242
  54.7 12.5 %collective-permute-start.7 = (bf16[2,384,128]{2,1,0:T(8,128)(2,1)S(1)}, bf16[2,384,128]{2,1,0:T(8,128)(2,1)S(1)}, u32[]{:S(2)}, u32[]{:S(2)}) collective-permute-start(bf16[2,384,128]{2,1,0:T(8,128)(2,1)S(1)} %slice.122), channel_id=1, source_target_pairs={{0,4},{1,5},{2,6},{3,7},{4,0},{5,1},{6,2},{7,3},{8,12},{9,13},{10,... | collective-permute-start | bytes 589832 | tf_op jit(solution)/shard_map/ppermute | solution.py:242
  62.3 8.5 %collective-permute-start.4 = (bf16[2,384,128]{2,1,0:T(8,128)(2,1)S(1)}, bf16[2,384,128]{2,1,0:T(8,128)(2,1)S(1)}, u32[]{:S(2)}, u32[]{:S(2)}) collective-permute-start(bf16[2,384,128]{2,1,0:T(8,128)(2,1)S(1)} %slice.123), channel_id=1, source_target_pairs={{0,4},{1,5},{2,6},{3,7},{4,0},{5,1},{6,2},{7,3},{8,12},{9,13},{10,... | collective-permute-start | bytes 589832 | tf_op jit(solution)/shard_map/ppermute | solution.py:242
  64.0 9.1 %collective-permute-start.14 = (bf16[1,384,128]{2,1,0:T(8,128)(2,1)S(1)}, bf16[1,384,128]{2,1,0:T(8,128)(2,1)S(1)}, u32[]{:S(2)}, u32[]{:S(2)}) collective-permute-start(bf16[1,384,128]{2,1,0:T(8,128)(2,1)S(1)} %slice.124), channel_id=1, source_target_pairs={{0,8},{1,9},{2,10},{3,11},{4,12},{5,13},{6,14},{7,15},{8,0},{9,1},... | collective-permute-start | bytes 294920 | tf_op jit(solution)/shard_map/ppermute | solution.py:242
  66.7 14.1 %collective-permute-start.11 = (bf16[1,384,128]{2,1,0:T(8,128)(2,1)S(1)}, bf16[1,384,128]{2,1,0:T(8,128)(2,1)S(1)}, u32[]{:S(2)}, u32[]{:S(2)}) collective-permute-start(bf16[1,384,128]{2,1,0:T(8,128)(2,1)S(1)} %slice.125), channel_id=1, source_target_pairs={{0,8},{1,9},{2,10},{3,11},{4,12},{5,13},{6,14},{7,15},{8,0},{9,1},... | collective-permute-start | bytes 294920 | tf_op jit(solution)/shard_map/ppermute | solution.py:242
  67.2 15.8 %collective-permute-start.8 = (bf16[1,384,128]{2,1,0:T(8,128)(2,1)S(1)}, bf16[1,384,128]{2,1,0:T(8,128)(2,1)S(1)}, u32[]{:S(2)}, u32[]{:S(2)}) collective-permute-start(bf16[1,384,128]{2,1,0:T(8,128)(2,1)S(1)} %slice.126), channel_id=1, source_target_pairs={{0,8},{1,9},{2,10},{3,11},{4,12},{5,13},{6,14},{7,15},{8,0},{9,1},... | collective-permute-start | bytes 294920 | tf_op jit(solution)/shard_map/ppermute | solution.py:242
  70.9 13.5 %collective-permute-start.5 = (bf16[1,384,128]{2,1,0:T(8,128)(2,1)S(1)}, bf16[1,384,128]{2,1,0:T(8,128)(2,1)S(1)}, u32[]{:S(2)}, u32[]{:S(2)}) collective-permute-start(bf16[1,384,128]{2,1,0:T(8,128)(2,1)S(1)} %slice.127), channel_id=1, source_target_pairs={{0,8},{1,9},{2,10},{3,11},{4,12},{5,13},{6,14},{7,15},{8,0},{9,1},... | collective-permute-start | bytes 294920 | tf_op jit(solution)/shard_map/ppermute | solution.py:242

commit v2 on v1

v2 whole, which is shorter than its diff:
```python
import dataclasses
import functools

import jax
import jax.numpy as jnp
from jax import lax
from jax.experimental import pallas as pl
from jax.experimental.pallas import tpu as pltpu
from jax.sharding import PartitionSpec as P

F32 = jnp.float32
BF16 = jnp.bfloat16
LANES = 128
SEGS = 8
PAD = 8
EDGE = 2 * PAD


def power(base, exponent):
    result, square = None, base
    while exponent:
        if exponent & 1:
            result = square if result is None else result * square
        exponent >>= 1
        if exponent:
            square = square * square
    return result


def segments(length):
    seg_len = (length + PAD) // SEGS
    return seg_len, next(n for n in (7, 8, 6, 5, 4, 3, 2, 1) if seg_len % n == 0)


def tree_sum(terms):
    while len(terms) > 1:
        paired = [a + b for a, b in zip(terms[::2], terms[1::2])]
        terms = paired + terms[len(paired) * 2 :]
    return terms[0]


def weight_columns(weight_hbm, ref, side, sems):
    width = ref.shape[2]
    copies = []
    for part in range(ref.shape[0]):
        column = pl.multiple_of((2 * part + side) * width, LANES)
        copies.append(pltpu.make_async_copy(weight_hbm.at[:, pl.ds(column, width)], ref.at[part], sems.at[part]))
    return copies


def driven_kernel(where_ref, streams_hbm, taps_hbm, decay_hbm, init_hbm, weight_hbm, driven_ref, inner_ref, message_ref, sent_ref, wide_ref, streams_ref, rim_ref, taps_ref, decay_ref, init_ref, weight_sems, sems):
    first = where_ref[0] == 0
    core = where_ref[1]
    poles = decay_ref.shape[0]
    tap_count = taps_ref.shape[1]
    length, channels = streams_hbm.shape[2:]
    tiles = channels // LANES
    seg_len, turn = segments(length)
    heads = -(-(PAD + tap_count) // turn)
    small = [
        pltpu.make_async_copy(taps_hbm, taps_ref, sems.at[0]),
        pltpu.make_async_copy(decay_hbm, decay_ref, sems.at[1]),
        pltpu.make_async_copy(init_hbm, init_ref, sems.at[2]),
        pltpu.make_async_copy(streams_hbm.at[:, 0, length - 16 :], rim_ref, sems.at[3]),
    ]
    loads = []
    for tile in range(tiles):
        lanes = pl.ds(tile * LANES, LANES)
        loads.append(pltpu.make_async_copy(streams_hbm.at[1:3, 0, :, lanes], streams_ref.at[tile], sems.at[4 + tile]))
    loads[0].start()
    for copy in small + loads[1:]:
        copy.start()
    copies = weight_columns(weight_hbm, sent_ref, 1 - core, weight_sems)
    for copy in copies:
        copy.start()
    for copy in small:
        copy.wait()
    sublane = lax.broadcasted_iota(jnp.int32, (SEGS, LANES), 0)
    early = jnp.logical_and(sublane == 0, jnp.logical_not(first))
    for tile in range(tiles):
        lanes = slice(tile * LANES, (tile + 1) * LANES)
        loads[tile].wait()
        for s in range(2):
            wide_ref[s, 0:EDGE, :] = jnp.zeros((EDGE, LANES), F32)
            wide_ref[s, EDGE : EDGE + length, :] = streams_ref[tile, s].astype(F32)
        taps = [[jnp.broadcast_to(taps_ref[1 + s, i : i + 1, lanes], (SEGS, LANES)) for i in range(tap_count)] for s in range(2)]

        def row(s, j):
            return wide_ref[s, pl.ds(PAD + j, SEGS, stride=seg_len), :]

        def block(base, windows, masked):
            windows = list(windows)
            for step in range(turn):
                made = []
                for s in range(2):
                    seen = list(windows[s]) + [row(s, base + step)]
                    made.append(tree_sum([taps[s][i] * seen[-1 - i] for i in range(tap_count)]))
                    windows[s] = tuple(seen[1:])
                product = made[0] * made[1]
                if masked and PAD <= base + step < PAD + tap_count - 1:
                    product = jnp.where(early, 0.0, product)
                driven_ref[tile, base + step] = product
            return tuple(windows)

        windows = tuple(tuple(row(s, j - (tap_count - 1)) for j in range(tap_count - 1)) for s in range(2))
        for b in range(heads):
            windows = block(b * turn, windows, True)
        lax.fori_loop(heads, seg_len // turn, lambda b, w: block(b * turn, w, False), windows)

        decays = [jnp.broadcast_to(decay_ref[n : n + 1, lanes], (SEGS, LANES)) for n in range(poles)]

        def scan(b, states):
            states = list(states)
            for step in range(turn):
                value = driven_ref[tile, b * turn + step]
                states = [d * s + value for d, s in zip(decays, states)]
            return tuple(states)

        zero = jnp.zeros((SEGS, LANES), F32)
        ends = lax.fori_loop(0, seg_len // turn, scan, (zero,) * poles)
        for n in range(poles):
            total, factor = ends[n], power(decays[n], seg_len)
            for reach in (1, 2, 4):
                moved = jnp.where(sublane >= reach, pltpu.roll(total, reach, 0), 0.0)
                total = total + factor * moved
                factor = factor * factor
            inner_ref[tile, n] = total
            message_ref[n : n + 1, lanes] = total[SEGS - 1 : SEGS, :]
    carried = power(decay_ref[...], length) * init_ref[0]
    message_ref[0:poles, :] = message_ref[0:poles, :] + jnp.where(first, carried, 0.0)
    for s in range(3):
        message_ref[poles + s * PAD : poles + (s + 1) * PAD, :] = rim_ref[s].astype(F32)[16 - PAD :]
    for copy in copies:
        copy.wait()


def response_kernel(where_ref, query_in_ref, taps_ref, decay_ref, residues_ref, driven_ref, inner_ref, weight_hbm, response_ref, query_ref, mine_ref, wide_ref, weight_sems):
    poles = decay_ref.shape[0]
    tap_count = taps_ref.shape[1]
    lag = tap_count - 1
    length, channels = query_in_ref.shape[2:]
    tiles = channels // LANES
    seg_len, turn = segments(length)
    copies = weight_columns(weight_hbm, mine_ref, where_ref[1], weight_sems)
    for copy in copies:
        copy.start()
    sublane = lax.broadcasted_iota(jnp.int32, (SEGS, LANES), 0)
    for tile in range(tiles):
        lanes = slice(tile * LANES, (tile + 1) * LANES)
        wide_ref[0:EDGE, :] = jnp.zeros((EDGE, LANES), F32)
        wide_ref[EDGE : EDGE + length, :] = query_in_ref[0, 0, :, lanes].astype(F32)
        taps = [jnp.broadcast_to(taps_ref[0, i : i + 1, lanes], (SEGS, LANES)) for i in range(tap_count)]

        def row(j):
            return wide_ref[pl.ds(PAD + j, SEGS, stride=seg_len), :]

        def fir(b, window):
            window = list(window)
            for step in range(turn):
                window.append(row(b * turn + step))
                query_ref[tile, b * turn + step] = tree_sum([taps[i] * window[-1 - i] for i in range(tap_count)])
                window = window[1:]
            return tuple(window)

        lax.fori_loop(0, seg_len // turn, fir, tuple(row(j - lag) for j in range(lag)))

        decays = [jnp.broadcast_to(decay_ref[n : n + 1, lanes], (SEGS, LANES)) for n in range(poles)]
        weights = [jnp.broadcast_to(residues_ref[n : n + 1, lanes], (SEGS, LANES)) for n in range(poles)]
        states = [jnp.where(sublane == 0, 0.0, pltpu.roll(inner_ref[tile, n], 1, 0)) for n in range(poles)]

        def scan(b, states):
            states = list(states)
            for step in range(turn):
                value = driven_ref[tile, b * turn + step]
                states = [d * s + value for d, s in zip(decays, states)]
                response_ref[tile, b * turn + step] = tree_sum([r * s for r, s in zip(weights, states)])
            return tuple(states)

        lax.fori_loop(0, seg_len // turn, scan, tuple(states))
    for copy in copies:
        copy.wait()


def gated_kernel(where_ref, message_ref, head_in_ref, taps_ref, decay_ref, residues_ref, init_ref, response_ref, query_ref, gated_ref, head_ref, start_ref, out_ref):
    first = where_ref[0] == 0
    poles = decay_ref.shape[0]
    tap_count = taps_ref.shape[1]
    lag = tap_count - 1
    length, channels = gated_ref.shape
    tiles = channels // LANES
    seg_len, turn = segments(length)
    heads_count = -(-(PAD + tap_count) // turn)
    sublane = lax.broadcasted_iota(jnp.int32, (SEGS, LANES), 0)

    heads = []
    for s in range(3):
        head_ref[0:PAD, :] = message_ref[poles + s * PAD : poles + (s + 1) * PAD, :]
        head_ref[PAD : PAD + 16, :] = head_in_ref[s, 0, 0:16, :].astype(F32)
        heads.append(tree_sum([taps_ref[s, i : i + 1, :] * head_ref[PAD - i : 2 * PAD - i, :] for i in range(tap_count)]))
    head_query = heads[0]
    counted = jnp.where(first, 0.0, heads[1] * heads[2])
    decay = decay_ref[...]
    state = jnp.where(first, init_ref[0], message_ref[0:poles, :])
    start_ref[0:poles, :] = state * residues_ref[...]
    for j in range(lag):
        state = decay * state + counted[j : j + 1, :]
    start_ref[poles:, :] = state * residues_ref[...] * power(decay, seg_len - PAD - lag)

    for tile in range(tiles):
        lanes = slice(tile * LANES, (tile + 1) * LANES)
        decays = [jnp.broadcast_to(decay_ref[n : n + 1, lanes], (SEGS, LANES)) for n in range(poles)]
        states = []
        for n in range(poles):
            factor = power(decays[n], seg_len)
            spread = jnp.broadcast_to(start_ref[poles + n : poles + n + 1, lanes], (SEGS, LANES))
            before = sublane - 1
            for bit in (1, 2, 4):
                spread = jnp.where(jnp.bitwise_and(before, bit) != 0, spread * factor, spread)
                factor = factor * factor
            states.append(jnp.where(sublane == 0, 0.0, spread))

        def block(b, states, head):
            states = list(states)
            for step in range(turn):
                at = b * turn + step
                query = query_ref[tile, at]
                if head and at == PAD:
                    states = [jnp.where(sublane == 0, jnp.broadcast_to(start_ref[n : n + 1, lanes], (SEGS, LANES)), s) for n, s in enumerate(states)]
                states = [d * s for d, s in zip(decays, states)]
                if head and PAD <= at < PAD + lag:
                    j = at - PAD
                    value = jnp.where(sublane == 0, jnp.broadcast_to(counted[j : j + 1, lanes], (SEGS, LANES)), 0.0)
                    states = [s + value * jnp.broadcast_to(residues_ref[n : n + 1, lanes], (SEGS, LANES)) for n, s in enumerate(states)]
                    query = jnp.where(sublane == 0, jnp.broadcast_to(head_query[j : j + 1, lanes], (SEGS, LANES)), query)
                total = response_ref[tile, at] + tree_sum(states)
                out_ref[pl.ds(at, SEGS, stride=seg_len), :] = total * query
            return tuple(states)

        for b in range(heads_count):
            states = block(b, states, True)
        lax.fori_loop(heads_count, seg_len // turn, lambda b, states: block(b, states, False), states)
        gated_ref[:, lanes] = out_ref[PAD:, :].astype(BF16)


def relative(index, high, order):
    value = high << (order[0] - 1)
    count = len(order) - 1
    for place, bit in enumerate(order[1:]):
        value = value | (((index >> (count - 1 - place)) & 1) << (bit - 1))
    return value


def project_kernel(part, where_ref, own_ref, other_ref, mine_ref, theirs_ref, order_ref, send_ref, keep_ref):
    row, rows, column, columns = part.box
    take = slice(column, column + columns)
    wide = jnp.concatenate([own_ref[row : row + rows, :], other_ref[row : row + rows, :]], axis=1)

    def step(index, carry):
        sides = []
        for high in (1, 0):
            block = relative(index, high, part.order) ^ where_ref[2]
            sides.append(jnp.concatenate([mine_ref[block, :, take], theirs_ref[block, :, take]], axis=0))
        total = jnp.dot(wide, jnp.concatenate(sides, axis=1), preferred_element_type=F32)
        send_ref[index] = total[:, :columns].astype(BF16)
        keep_ref[index] = total[:, columns:]
        return carry

    lax.fori_loop(0, send_ref.shape[0], step, 0)


def merge_kernel(keep_ref, received_ref, order_ref, send_ref, kept_ref):
    half = kept_ref.shape[0]
    send_ref[...] = (keep_ref[half:] + received_ref[half:].astype(F32)).astype(BF16)
    kept_ref[...] = keep_ref[:half] + received_ref[:half].astype(F32)


def finish_kernel(keep_ref, received_ref, order_ref, out_ref):
    out_ref[...] = (keep_ref[0] + received_ref[0].astype(F32)).astype(BF16)


def gather_kernel(boxes, *refs):
    count = len(boxes) - 1
    pieces, (keep_ref, received_ref, order_ref, out_ref, last_ref, sems) = refs[:count], refs[count:]
    copies = []
    for at, (piece, (row, rows, column, columns)) in enumerate(zip(list(pieces) + [last_ref], boxes)):
        if at == count:
            last_ref[...] = (keep_ref[0] + received_ref[0].astype(F32)).astype(BF16)
        place = out_ref.at[0, pl.ds(row, rows), pl.ds(column, columns)]
        copies.append(pltpu.make_async_copy(piece, place, sems.at[at]))
        copies[-1].start()
    for copy in copies:
        copy.wait()


SMEM = pl.BlockSpec(memory_space=pltpu.SMEM)
VMEM = pl.BlockSpec(memory_space=pltpu.VMEM)
HBM = pl.BlockSpec(memory_space=pltpu.HBM)
ANYWHERE = pl.BlockSpec(memory_space=pl.ANY)
LIMIT = 24 * 1024 * 1024
QUICK = pl.CostEstimate(flops=1, bytes_accessed=1, transcendentals=0)


def in_hbm(x):
    return pltpu.with_memory_space_constraint(x, pltpu.MemorySpace.HBM)


@dataclasses.dataclass(frozen=True)
class Part:
    box: tuple
    order: tuple


def project(part, where, own, other, mine, theirs, ordered):
    channels = own.shape[1]
    halves = mine.shape[0]
    rest = halves // 2
    _, rows, _, columns = part.box
    return pl.pallas_call(
        functools.partial(project_kernel, part),
        out_shape=(jax.ShapeDtypeStruct((rest, rows, columns), BF16), jax.ShapeDtypeStruct((rest, rows, columns), F32)),
        in_specs=[SMEM, VMEM, VMEM, VMEM, VMEM, ANYWHERE],
        out_specs=(VMEM, VMEM),
        compiler_params=pltpu.CompilerParams(vmem_limit_bytes=LIMIT),
        cost_estimate=QUICK,
        name="project",
    )(where, own, other, mine, theirs, ordered)


def merge(keep, received, ordered):
    half = keep.shape[0] // 2
    shape = (half,) + keep.shape[1:]
    return pl.pallas_call(
        merge_kernel,
        out_shape=(jax.ShapeDtypeStruct(shape, BF16), jax.ShapeDtypeStruct(shape, F32)),
        in_specs=[VMEM, VMEM, ANYWHERE],
        out_specs=(VMEM, VMEM),
        compiler_params=pltpu.CompilerParams(vmem_limit_bytes=LIMIT),
        cost_estimate=QUICK,
        name="merge",
    )(keep, received, ordered)


def finish(keep, received, ordered):
    return pl.pallas_call(
        finish_kernel,
        out_shape=jax.ShapeDtypeStruct(keep.shape[1:], BF16),
        in_specs=[VMEM, VMEM, ANYWHERE],
        out_specs=VMEM,
        compiler_params=pltpu.CompilerParams(vmem_limit_bytes=LIMIT),
        cost_estimate=QUICK,
        name="finish",
    )(keep, received, ordered)


def gather(pieces, boxes, keep, received, ordered, length, width):
    return pl.pallas_call(
        functools.partial(gather_kernel, boxes),
        out_shape=jax.ShapeDtypeStruct((1, length, width), BF16),
        in_specs=[VMEM] * len(pieces) + [VMEM, VMEM, ANYWHERE],
        out_specs=HBM,
        scratch_shapes=[pltpu.VMEM(keep.shape[1:], BF16), pltpu.SemaphoreType.DMA((len(boxes),))],
        compiler_params=pltpu.CompilerParams(vmem_limit_bytes=LIMIT),
        cost_estimate=QUICK,
        name="gather",
    )(*pieces, keep, received, ordered)


def plan(peers, length, width):
    bits = tuple(range(1, peers.bit_length() - 1))
    far = bits[-2:] + bits[:-2]
    count = width // LANES
    if count == 4 and len(bits) == 3 and length % 48 == 0:
        third = length // 3
        boxes = [(0, length, 0, LANES), (0, length, LANES, LANES), (0, 2 * third, 2 * LANES, LANES), (2 * third, third, 2 * LANES, LANES), (0, length, 3 * LANES, LANES)]
        parts = [Part(box, bits) for box in boxes[:4]] + [Part(boxes[4], far)]
        steps = [(0, -1), (4, -1), (1, -1), (2, -1), (0, 0), (3, -1), (4, 0), (1, 0), (0, 1), (4, 1), (2, 0), (1, 1), (3, 0), (2, 1), (3, 1), (0, 2), (1, 2), (2, 2), (4, 2), (3, 2)]
    else:
        parts = [Part((0, length, LANES * at, LANES), far if at == 1 else bits) for at in range(count)]
        steps = [(at, wave - at - 1) for wave in range(count + len(bits)) for at in range(count) if -1 <= wave - at - 1 < len(bits)]
    return parts, steps


def across(x, bit):
    count = lax.axis_size("tp")
    return lax.ppermute(x, "tp", [(i, i ^ (1 << bit)) for i in range(count)])


def after(x, axis):
    count = lax.axis_size(axis)
    return lax.ppermute(x, axis, [(i, i + 1) for i in range(count - 1)])


def later_rounds(message, inner_end, streams, taps, decay, init_state):
    first = lax.axis_index("ctx") == 0
    poles = decay.shape[0]
    tap_count = taps.shape[1]
    lag = tap_count - 1
    length = streams.shape[2]
    rims = message[poles:].reshape(3, PAD, -1)
    joined = jnp.concatenate([rims, streams[:, 0, :PAD].astype(F32)], axis=1)
    featured = sum(taps[:, i][:, None, :] * joined[:, PAD - i : 2 * PAD - i, :] for i in range(tap_count))
    head = jnp.where(first, 0.0, featured[1] * featured[2])
    local = jnp.where(first, 0.0, inner_end)

    def one(_, incoming):
        state = jnp.where(first, init_state[0], incoming)
        for j in range(lag):
            state = decay * state + head[j][None]
        ended = jnp.where(first, inner_end, local + power(decay, length - lag) * state)
        return after(ended, "ctx")

    state = lax.fori_loop(0, lax.axis_size("ctx") - 2, one, message[:poles])
    return jnp.concatenate([state, message[poles:]], axis=0)


def per_device(streams, taps, decay, residues, init_state, out_weight):
    length, channels = streams.shape[2:]
    poles = decay.shape[0]
    tiles = channels // LANES
    seg_len, turn = segments(length)
    peers = lax.axis_size("tp")
    width = out_weight.shape[1] // peers
    me = lax.axis_index("tp")
    where = jnp.stack([lax.axis_index("ctx"), me & 1, me >> 1]).astype(jnp.int32)
    rows = poles + 3 * PAD
    streams_hbm, weight_hbm = in_hbm(streams), in_hbm(out_weight)
    split = (tiles, seg_len, SEGS, LANES)
    driven, inner, message, sent = pl.pallas_call(
        driven_kernel,
        out_shape=(
            jax.ShapeDtypeStruct(split, F32),
            jax.ShapeDtypeStruct((tiles, poles, SEGS, LANES), F32),
            jax.ShapeDtypeStruct((rows, channels), F32),
            jax.ShapeDtypeStruct((peers // 2, channels, width), BF16),
        ),
        in_specs=[SMEM, HBM, HBM, HBM, HBM, HBM],
        out_specs=(VMEM, VMEM, VMEM, VMEM),
        scratch_shapes=[
            pltpu.VMEM((2, EDGE + length, LANES), F32),
            pltpu.VMEM((tiles, 2, length, LANES), BF16),
            pltpu.VMEM((3, 16, channels), BF16),
            pltpu.VMEM(taps.shape, F32),
            pltpu.VMEM(decay.shape, F32),
            pltpu.VMEM(init_state.shape, F32),
            pltpu.SemaphoreType.DMA((peers // 2,)),
            pltpu.SemaphoreType.DMA((4 + tiles,)),
        ],
        compiler_params=pltpu.CompilerParams(vmem_limit_bytes=LIMIT),
        cost_estimate=QUICK,
        name="driven",
    )(where, streams_hbm, in_hbm(taps), in_hbm(decay), in_hbm(init_state), weight_hbm)
    passed = after(message, "ctx")
    swapped = across(sent, 0)
    response, query, mine = pl.pallas_call(
        response_kernel,
        out_shape=(
            jax.ShapeDtypeStruct(split, F32),
            jax.ShapeDtypeStruct(split, F32),
            jax.ShapeDtypeStruct((peers // 2, channels, width), BF16),
        ),
        in_specs=[SMEM] + [VMEM] * 6 + [HBM],
        out_specs=(VMEM, VMEM, VMEM),
        scratch_shapes=[pltpu.VMEM((EDGE + length, LANES), F32), pltpu.SemaphoreType.DMA((peers // 2,))],
        compiler_params=pltpu.CompilerParams(vmem_limit_bytes=LIMIT),
        cost_estimate=QUICK,
        name="response",
    )(where, streams, taps, decay, residues, driven, inner, weight_hbm)
    if lax.axis_size("ctx") > 2:
        passed = later_rounds(passed, message[:poles], streams, taps, decay, init_state)
    gated = pl.pallas_call(
        gated_kernel,
        out_shape=jax.ShapeDtypeStruct((length, channels), BF16),
        in_specs=[SMEM] + [VMEM] * 8,
        out_specs=VMEM,
        scratch_shapes=[
            pltpu.VMEM((PAD + 16, channels), F32),
            pltpu.VMEM((2 * poles, channels), F32),
            pltpu.VMEM((PAD + length, LANES), F32),
        ],
        compiler_params=pltpu.CompilerParams(vmem_limit_bytes=LIMIT),
        cost_estimate=QUICK,
        name="gated",
    )(where, passed, streams, taps, decay, residues, init_state, response, query)
    other = across(gated, 0)

    parts, steps = plan(peers, length, width)
    flying, kept, finished, ordered = {}, {}, {}, gated
    for at, stage in steps:
        part = parts[at]
        if stage < 0:
            send, kept[at] = project(part, where, gated, other, mine, swapped, ordered)
            ordered = send
        elif stage + 1 < len(part.order):
            send, kept[at] = merge(kept[at], flying[at], ordered)
            ordered = send
        elif len(finished) + 1 < len(parts):
            ordered = finished[at] = finish(kept[at], flying[at], ordered)
            continue
        else:
            boxes = [parts[done].box for done in finished] + [part.box]
            return gather(list(finished.values()), boxes, kept[at], flying[at], ordered, length, width)
        flying[at] = across(send, part.order[stage + 1])


def solution(mesh):
    in_specs = (
        P(None, None, "ctx", "tp"),
        P(None, None, "tp"),
        P(None, "tp"),
        P(None, "tp"),
        P(None, None, "tp"),
        P("tp", None),
    )
    out_specs = P(None, "ctx", "tp")
    return jax.shard_map(
        per_device, mesh=mesh, in_specs=in_specs, out_specs=out_specs, check_vma=False
    )
```

time: 85.5 us -> 61.8 us (0.72)
  waiting for transfers between devices: 34.6 us -> 11.9 us
  local copies, waits for them, and re-layouts: 7.14 us -> 0.02 us
  starting transfers between devices: 23.9 us -> 29.2 us
  Pallas kernels: 17.9 us -> 20.2 us
  other arithmetic: 1.37 us -> 0.08 us
    ppermute x14 -> x17, waiting for transfers between devices: 32.3 us -> 11.9 us  [across(): return lax.ppermute(x, 'tp', [(i, i ^ 1 << bit) for i in range(count)])]
    unnamed x14 -> x10, local copies, waits for them, and re-layouts: 6.97 us -> 0.02 us
    ppermute x14 -> x17, starting transfers between devices: 19.5 us -> 24.7 us  [across(): return lax.ppermute(x, 'tp', [(i, i ^ 1 << bit) for i in range(count)])]
    pallas_call x5 -> x22, Pallas kernels: 14.7 us -> 18.3 us  [the longest x5 9.7 us: project(): pl.pallas_call(functools.partial(project_kernel, part), out_shape=(jax.Sh...]
    ppermute x1, waiting for transfers between devices: 2.33 us -> 0.01 us  [after(): return lax.ppermute(x, axis, [(i, i + 1) for i in range(count - 1)])]
    pallas_call x1, Pallas kernels: 3.3 us -> 1.98 us  [per_device(): pl.pallas_call(gated_kernel, out_shape=jax.ShapeDtypeStruct((length, chan...]
  transfers between devices with their start and end apart: 15 -> 18, of which waited for: 9 -> 9; matrix products, arithmetic and copies ran while one was open for 1% -> 0% of each run, Pallas kernels for 14% -> 21%
where the time goes in v2:
time: 61.8 us; the launch traced here: 61.6 us
  starting transfers between devices  29.2 us (47%)
  Pallas kernels  20.2 us (33%)
  waiting for transfers between devices  11.9 us (19%)
    ppermute x17, starting transfers between devices, across(): return lax.ppermute(x, 'tp', [(i, i ^ 1 << bit) for i in range(count)])  24.7 us
    ppermute x17, waiting for transfers between devices, across(): return lax.ppermute(x, 'tp', [(i, i ^ 1 << bit) for i in range(count)])  11.9 us
    pallas_call x5, Pallas kernels, project(): pl.pallas_call(functools.partial(project_kernel, part), out_shape=(jax.Sh...  9.7 us
    ppermute x1, starting transfers between devices, after(): return lax.ppermute(x, axis, [(i, i + 1) for i in range(count - 1)])  4.44 us
    pallas_call x1, Pallas kernels, per_device(): pl.pallas_call(driven_kernel, out_shape=(jax.ShapeDtypeStruct(split, F32)...  4.38 us
    pallas_call x1, Pallas kernels, per_device(): pl.pallas_call(response_kernel, out_shape=(jax.ShapeDtypeStruct(split, F3...  2.89 us
    pallas_call x1, Pallas kernels, per_device(): pl.pallas_call(gated_kernel, out_shape=jax.ShapeDtypeStruct((length, chan...  1.98 us
  transfers between devices with their start and end apart: 18, of which 9 were waited for; matrix products, arithmetic and copies ran while one was open for 0% of the time, Pallas kernels for 21%

profile of v2, /device:TPU:0, one launch (start us, length us, event | category | flops | bytes accessed | tf_op | source)
XLA Modules:
  0.0 61.6 jit_solution(11652699505611810631)
XLA Ops:
  0.0 0.1 pad_add_fusion.where_ref
  0.1 0.0 copy-start
  0.1 0.0 copy-start.1
  0.1 0.0 copy-start.2
  0.1 0.0 copy-start.4
  0.1 4.4 %driven.1 = (f32[4,49,8,128]{3,2,1,0:T(8,128)S(1)}, f32[4,16,8,128]{3,2,1,0:T(8,128)S(1)}, f32[40,512]{1,0:T(8,128)S(1)}, bf16[8,512,512]{2,1,0:T(8,128)(2,1)S(1)}) custom-call(s32[3]{0:T(128)S(1)} %pad_add_fusion.where_ref, bf16[3,1,384,512]{3,2,1,0:T(8,128)(2,1)} %head_in_ref.1, f32[3,7,512]{2,1,0:T(8,128)} %taps_ref.3, f32[16,512]{1,0:T(8,128)} %decay_ref.3, ...), custom_call_target="tpu_custom_call" | custom-call | flops 1 | bytes 1 | tf_op jit(solution)/shard_map/driven/pallas_call | solution.py:428
  4.5 0.5 collective-permute-start.2
  5.0 4.4 %collective-permute-start = (f32[40,512]{1,0:T(8,128)S(1)}, f32[40,512]{1,0:T(8,128)S(1)}, u32[]{:S(2)}, u32[]{:S(2)}) collective-permute-start(f32[40,512]{1,0:T(8,128)S(1)} %get-tuple-element.42), channel_id=1, source_target_pairs={{0,16},{1,17},{2,18},{3,19},{4,20},{5,21},{6,22},{7,23},{8,24},{9,... | collective-permute-start | bytes 245768 | tf_op jit(solution)/shard_map/ppermute | solution.py:390
  9.4 0.0 copy-done
  9.4 0.0 copy-done.1
  9.5 0.0 copy-done.2
  9.5 0.0 copy-done.4
  9.5 0.0 copy-start.3
  9.5 2.9 %response.1 = (f32[4,49,8,128]{3,2,1,0:T(8,128)S(1)}, f32[4,49,8,128]{3,2,1,0:T(8,128)S(1)}, bf16[8,512,512]{2,1,0:T(8,128)(2,1)S(1)}) custom-call(s32[3]{0:T(128)S(1)} %pad_add_fusion.where_ref, bf16[3,1,384,512]{3,2,1,0:T(8,128)(2,1)S(1)} %copy-done, f32[3,7,512]{2,1,0:T(8,128)S(1)} %copy-done.1, f32[16,512]{1,0:T(8,128)S(1)} %copy-done.2, ...), custom_call_target="tpu_custom_call" | custom-call | flops 1 | bytes 1 | tf_op jit(solution)/shard_map/response/pallas_call | solution.py:454
  12.4 0.0 collective-permute-done.message_ref
  12.4 0.0 copy-done.3
  12.4 2.0 %gated.1.own_ref.order_ref = bf16[384,512]{1,0:T(8,128)(2,1)S(1)} custom-call(s32[3]{0:T(128)S(1)} %pad_add_fusion.where_ref, f32[40,512]{1,0:T(8,128)S(1)} %collective-permute-done.message_ref, bf16[3,1,384,512]{3,2,1,0:T(8,128)(2,1)S(1)} %copy-done, f32[3,7,512]{2,1,0:T(8,128)S(1)} %copy-done.1, f32[16,512]{1,0:T(8,128)S(1)} %copy-done.2, ...), custom_call_target="tpu_custom_call" | custom-call | flops 1 | bytes 1 | tf_op jit(solution)/shard_map/gated/pallas_call | solution.py:470
  14.4 0.3 collective-permute-start.1
  14.7 1.5 %collective-permute-done.1.other_ref = bf16[384,512]{1,0:T(8,128)(2,1)S(1)} collective-permute-done((bf16[384,512]{1,0:T(8,128)(2,1)S(1)}, bf16[384,512]{1,0:T(8,128)(2,1)S(1)}, u32[]{:S(2)}, u32[]{:S(2)}) %collective-permute-start.1) | collective-permute-done | bytes 393248 | tf_op jit(solution)/shard_map/ppermute | solution.py:385
  16.2 0.0 collective-permute-done.2.theirs_ref
  16.2 2.1 %project.5 = (bf16[4,384,128]{2,1,0:T(8,128)(2,1)S(1)}, f32[4,384,128]{2,1,0:T(8,128)S(1)}) custom-call(s32[3]{0:T(128)S(1)} %pad_add_fusion.where_ref, bf16[384,512]{1,0:T(8,128)(2,1)S(1)} %gated.1.own_ref.order_ref, bf16[384,512]{1,0:T(8,128)(2,1)S(1)} %collective-permute-done.1.other_ref, bf16[8,512,512]{2,1,0:T(8,128)(2,1)S(1)} %get-tuple-element.47.mine_ref, ...), custom_call_target="tpu_custom_call" | custom-call | flops 1 | bytes 1 | tf_op jit(solution)/shard_map/project/pallas_call | solution.py:318
  18.3 1.6 %collective-permute-start.3 = (bf16[4,384,128]{2,1,0:T(8,128)(2,1)S(1)}, bf16[4,384,128]{2,1,0:T(8,128)(2,1)S(1)}, u32[]{:S(2)}, u32[]{:S(2)}) collective-permute-start(bf16[4,384,128]{2,1,0:T(8,128)(2,1)S(1)} %get-tuple-element.50.order_ref), channel_id=1, source_target_pairs={{0,2},{1,3},{2,0},{3,1},{4,6},{5,7},{6,4},{7,5},{8,10},{9,11},{10,... | collective-permute-start | bytes 1179656 | tf_op jit(solution)/shard_map/ppermute | solution.py:385
  19.9 2.1 %project.6 = (bf16[4,384,128]{2,1,0:T(8,128)(2,1)S(1)}, f32[4,384,128]{2,1,0:T(8,128)S(1)}) custom-call(s32[3]{0:T(128)S(1)} %pad_add_fusion.where_ref, bf16[384,512]{1,0:T(8,128)(2,1)S(1)} %gated.1.own_ref.order_ref, bf16[384,512]{1,0:T(8,128)(2,1)S(1)} %collective-permute-done.1.other_ref, bf16[8,512,512]{2,1,0:T(8,128)(2,1)S(1)} %get-tuple-element.47.mine_ref, ...), custom_call_target="tpu_custom_call" | custom-call | flops 1 | bytes 1 | tf_op jit(solution)/shard_map/project/pallas_call | solution.py:318
  22.0 1.6 %collective-permute-start.6 = (bf16[4,384,128]{2,1,0:T(8,128)(2,1)S(1)}, bf16[4,384,128]{2,1,0:T(8,128)(2,1)S(1)}, u32[]{:S(2)}, u32[]{:S(2)}) collective-permute-start(bf16[4,384,128]{2,1,0:T(8,128)(2,1)S(1)} %get-tuple-element.51.order_ref), channel_id=1, source_target_pairs={{0,4},{1,5},{2,6},{3,7},{4,0},{5,1},{6,2},{7,3},{8,12},{9,13},{10,... | collective-permute-start | bytes 1179656 | tf_op jit(solution)/shard_map/ppermute | solution.py:385
  23.6 2.1 %project.7 = (bf16[4,384,128]{2,1,0:T(8,128)(2,1)S(1)}, f32[4,384,128]{2,1,0:T(8,128)S(1)}) custom-call(s32[3]{0:T(128)S(1)} %pad_add_fusion.where_ref, bf16[384,512]{1,0:T(8,128)(2,1)S(1)} %gated.1.own_ref.order_ref, bf16[384,512]{1,0:T(8,128)(2,1)S(1)} %collective-permute-done.1.other_ref, bf16[8,512,512]{2,1,0:T(8,128)(2,1)S(1)} %get-tuple-element.47.mine_ref, ...), custom_call_target="tpu_custom_call" | custom-call | flops 1 | bytes 1 | tf_op jit(solution)/shard_map/project/pallas_call | solution.py:318
  25.7 0.6 collective-permute-start.5
  26.3 1.8 %project.8 = (bf16[4,256,128]{2,1,0:T(8,128)(2,1)S(1)}, f32[4,256,128]{2,1,0:T(8,128)S(1)}) custom-call(s32[3]{0:T(128)S(1)} %pad_add_fusion.where_ref, bf16[384,512]{1,0:T(8,128)(2,1)S(1)} %gated.1.own_ref.order_ref, bf16[384,512]{1,0:T(8,128)(2,1)S(1)} %collective-permute-done.1.other_ref, bf16[8,512,512]{2,1,0:T(8,128)(2,1)S(1)} %get-tuple-element.47.mine_ref, ...), custom_call_target="tpu_custom_call" | custom-call | flops 1 | bytes 1 | tf_op jit(solution)/shard_map/project/pallas_call | solution.py:318
  28.2 1.6 %collective-permute-start.10 = (bf16[4,256,128]{2,1,0:T(8,128)(2,1)S(1)}, bf16[4,256,128]{2,1,0:T(8,128)(2,1)S(1)}, u32[]{:S(2)}, u32[]{:S(2)}) collective-permute-start(bf16[4,256,128]{2,1,0:T(8,128)(2,1)S(1)} %get-tuple-element.53.order_ref), channel_id=1, source_target_pairs={{0,2},{1,3},{2,0},{3,1},{4,6},{5,7},{6,4},{7,5},{8,10},{9,11},{10,... | collective-permute-start | bytes 786440 | tf_op jit(solution)/shard_map/ppermute | solution.py:385
  29.7 0.6 collective-permute-done.3.received_ref
  30.3 0.1 merge.10
  30.4 1.6 %collective-permute-start.4 = (bf16[2,384,128]{2,1,0:T(8,128)(2,1)S(1)}, bf16[2,384,128]{2,1,0:T(8,128)(2,1)S(1)}, u32[]{:S(2)}, u32[]{:S(2)}) collective-permute-start(bf16[2,384,128]{2,1,0:T(8,128)(2,1)S(1)} %get-tuple-element.55.order_ref), channel_id=1, source_target_pairs={{0,4},{1,5},{2,6},{3,7},{4,0},{5,1},{6,2},{7,3},{8,12},{9,13},{10,... | collective-permute-start | bytes 589832 | tf_op jit(solution)/shard_map/ppermute | solution.py:385
  32.0 1.5 %project.9 = (bf16[4,128,128]{2,1,0:T(8,128)(2,1)S(1)}, f32[4,128,128]{2,1,0:T(8,128)S(1)}) custom-call(s32[3]{0:T(128)S(1)} %pad_add_fusion.where_ref, bf16[384,512]{1,0:T(8,128)(2,1)S(1)} %gated.1.own_ref.order_ref, bf16[384,512]{1,0:T(8,128)(2,1)S(1)} %collective-permute-done.1.other_ref, bf16[8,512,512]{2,1,0:T(8,128)(2,1)S(1)} %get-tuple-element.47.mine_ref, ...), custom_call_target="tpu_custom_call" | custom-call | flops 1 | bytes 1 | tf_op jit(solution)/shard_map/project/pallas_call | solution.py:318
  33.6 0.4 collective-permute-done.6.received_ref
  34.0 0.1 merge.11
  34.1 2.7 %collective-permute-start.11 = (bf16[2,384,128]{2,1,0:T(8,128)(2,1)S(1)}, bf16[2,384,128]{2,1,0:T(8,128)(2,1)S(1)}, u32[]{:S(2)}, u32[]{:S(2)}) collective-permute-start(bf16[2,384,128]{2,1,0:T(8,128)(2,1)S(1)} %get-tuple-element.59.order_ref), channel_id=1, source_target_pairs={{0,8},{1,9},{2,10},{3,11},{4,12},{5,13},{6,14},{7,15},{8,0},{9,1},... | collective-permute-start | bytes 589832 | tf_op jit(solution)/shard_map/ppermute | solution.py:385
  36.8 2.0 %collective-permute-done.5.received_ref = bf16[4,384,128]{2,1,0:T(8,128)(2,1)S(1)} collective-permute-done((bf16[4,384,128]{2,1,0:T(8,128)(2,1)S(1)}, bf16[4,384,128]{2,1,0:T(8,128)(2,1)S(1)}, u32[]{:S(2)}, u32[]{:S(2)}) %collective-permute-start.5) | collective-permute-done | bytes 393248 | tf_op jit(solution)/shard_map/ppermute | solution.py:385
  38.7 0.1 merge.12
  38.8 1.6 %collective-permute-start.9 = (bf16[2,384,128]{2,1,0:T(8,128)(2,1)S(1)}, bf16[2,384,128]{2,1,0:T(8,128)(2,1)S(1)}, u32[]{:S(2)}, u32[]{:S(2)}) collective-permute-start(bf16[2,384,128]{2,1,0:T(8,128)(2,1)S(1)} %get-tuple-element.60.order_ref), channel_id=1, source_target_pairs={{0,4},{1,5},{2,6},{3,7},{4,0},{5,1},{6,2},{7,3},{8,12},{9,13},{10,... | collective-permute-start | bytes 589832 | tf_op jit(solution)/shard_map/ppermute | solution.py:385
  40.5 1.5 %collective-permute-start.8 = (bf16[4,128,128]{2,1,0:T(8,128)(2,1)S(1)}, bf16[4,128,128]{2,1,0:T(8,128)(2,1)S(1)}, u32[]{:S(2)}, u32[]{:S(2)}) collective-permute-start(bf16[4,128,128]{2,1,0:T(8,128)(2,1)S(1)} %get-tuple-element.58.order_ref), channel_id=1, source_target_pairs={{0,2},{1,3},{2,0},{3,1},{4,6},{5,7},{6,4},{7,5},{8,10},{9,11},{10,... | collective-permute-start | bytes 393224 | tf_op jit(solution)/shard_map/ppermute | solution.py:385
  42.0 0.0 collective-permute-done.4.received_ref
  42.0 2.8 %collective-permute-done.11.received_ref = bf16[2,384,128]{2,1,0:T(8,128)(2,1)S(1)} collective-permute-done((bf16[2,384,128]{2,1,0:T(8,128)(2,1)S(1)}, bf16[2,384,128]{2,1,0:T(8,128)(2,1)S(1)}, u32[]{:S(2)}, u32[]{:S(2)}) %collective-permute-start.11) | collective-permute-done | bytes 196640 | tf_op jit(solution)/shard_map/ppermute | solution.py:385
  44.9 0.0 collective-permute-done.10.received_ref
  44.9 0.1 merge.15
  44.9 1.1 %collective-permute-start.13 = (bf16[2,256,128]{2,1,0:T(8,128)(2,1)S(1)}, bf16[2,256,128]{2,1,0:T(8,128)(2,1)S(1)}, u32[]{:S(2)}, u32[]{:S(2)}) collective-permute-start(bf16[2,256,128]{2,1,0:T(8,128)(2,1)S(1)} %get-tuple-element.68.order_ref), channel_id=1, source_target_pairs={{0,4},{1,5},{2,6},{3,7},{4,0},{5,1},{6,2},{7,3},{8,12},{9,13},{10,... | collective-permute-start | bytes 393224 | tf_op jit(solution)/shard_map/ppermute | solution.py:385
  46.1 2.6 %collective-permute-start.7 = (bf16[1,384,128]{2,1,0:T(8,128)(2,1)S(1)}, bf16[1,384,128]{2,1,0:T(8,128)(2,1)S(1)}, u32[]{:S(2)}, u32[]{:S(2)}) collective-permute-start(bf16[1,384,128]{2,1,0:T(8,128)(2,1)S(1)} %get-tuple-element.62.order_ref), channel_id=1, source_target_pairs={{0,8},{1,9},{2,10},{3,11},{4,12},{5,13},{6,14},{7,15},{8,0},{9,1},... | collective-permute-start | bytes 294920 | tf_op jit(solution)/shard_map/ppermute | solution.py:385
  48.6 0.0 collective-permute-done.9.received_ref
  48.7 2.5 %collective-permute-start.14 = (bf16[1,384,128]{2,1,0:T(8,128)(2,1)S(1)}, bf16[1,384,128]{2,1,0:T(8,128)(2,1)S(1)}, u32[]{:S(2)}, u32[]{:S(2)}) collective-permute-start(bf16[1,384,128]{2,1,0:T(8,128)(2,1)S(1)} %get-tuple-element.69.order_ref), channel_id=1, source_target_pairs={{0,8},{1,9},{2,10},{3,11},{4,12},{5,13},{6,14},{7,15},{8,0},{9,1},... | collective-permute-start | bytes 294920 | tf_op jit(solution)/shard_map/ppermute | solution.py:385
  51.1 0.0 collective-permute-done.8.received_ref
  51.2 2.5 %collective-permute-start.12 = (bf16[2,128,128]{2,1,0:T(8,128)(2,1)S(1)}, bf16[2,128,128]{2,1,0:T(8,128)(2,1)S(1)}, u32[]{:S(2)}, u32[]{:S(2)}) collective-permute-start(bf16[2,128,128]{2,1,0:T(8,128)(2,1)S(1)} %get-tuple-element.71.order_ref), channel_id=1, source_target_pairs={{0,4},{1,5},{2,6},{3,7},{4,0},{5,1},{6,2},{7,3},{8,12},{9,13},{10,... | collective-permute-start | bytes 196616 | tf_op jit(solution)/shard_map/ppermute | solution.py:385
  53.7 0.6 %collective-permute-start.16 = (bf16[1,384,128]{2,1,0:T(8,128)(2,1)S(1)}, bf16[1,384,128]{2,1,0:T(8,128)(2,1)S(1)}, u32[]{:S(2)}, u32[]{:S(2)}) collective-permute-start(bf16[1,384,128]{2,1,0:T(8,128)(2,1)S(1)} %get-tuple-element.67.order_ref), channel_id=1, source_target_pairs={{0,2},{1,3},{2,0},{3,1},{4,6},{5,7},{6,4},{7,5},{8,10},{9,11},{10,... | collective-permute-start | bytes 294920 | tf_op jit(solution)/shard_map/ppermute | solution.py:385
  54.4 0.0 collective-permute-done.13.received_ref
  54.4 0.1 collective-permute-start.15
  54.5 1.5 %collective-permute-done.12.received_ref = bf16[2,128,128]{2,1,0:T(8,128)(2,1)S(1)} collective-permute-done((bf16[2,128,128]{2,1,0:T(8,128)(2,1)S(1)}, bf16[2,128,128]{2,1,0:T(8,128)(2,1)S(1)}, u32[]{:S(2)}, u32[]{:S(2)}) %collective-permute-start.12) | collective-permute-done | bytes 65568 | tf_op jit(solution)/shard_map/ppermute | solution.py:385
  56.0 1.7 %collective-permute-start.17 = (bf16[1,128,128]{2,1,0:T(8,128)(2,1)S(1)}, bf16[1,128,128]{2,1,0:T(8,128)(2,1)S(1)}, u32[]{:S(2)}, u32[]{:S(2)}) collective-permute-start(bf16[1,128,128]{2,1,0:T(8,128)(2,1)S(1)} %get-tuple-element.74.order_ref), channel_id=1, source_target_pairs={{0,8},{1,9},{2,10},{3,11},{4,12},{5,13},{6,14},{7,15},{8,0},{9,1},... | collective-permute-start | bytes 98312 | tf_op jit(solution)/shard_map/ppermute | solution.py:385
  57.7 0.0 collective-permute-done.7.received_ref
  57.7 1.6 %collective-permute-done.14.received_ref = bf16[1,384,128]{2,1,0:T(8,128)(2,1)S(1)} collective-permute-done((bf16[1,384,128]{2,1,0:T(8,128)(2,1)S(1)}, bf16[1,384,128]{2,1,0:T(8,128)(2,1)S(1)}, u32[]{:S(2)}, u32[]{:S(2)}) %collective-permute-start.14) | collective-permute-done | bytes 98336 | tf_op jit(solution)/shard_map/ppermute | solution.py:385
  59.4 0.8 %collective-permute-done.15.received_ref = bf16[1,256,128]{2,1,0:T(8,128)(2,1)S(1)} collective-permute-done((bf16[1,256,128]{2,1,0:T(8,128)(2,1)S(1)}, bf16[1,256,128]{2,1,0:T(8,128)(2,1)S(1)}, u32[]{:S(2)}, u32[]{:S(2)}) %collective-permute-start.15) | collective-permute-done | bytes 65568 | tf_op jit(solution)/shard_map/ppermute | solution.py:385
  60.2 0.0 collective-permute-done.16.received_ref
  60.2 0.6 %collective-permute-done.17.refs_5_ = bf16[1,128,128]{2,1,0:T(8,128)(2,1)S(1)} collective-permute-done((bf16[1,128,128]{2,1,0:T(8,128)(2,1)S(1)}, bf16[1,128,128]{2,1,0:T(8,128)(2,1)S(1)}, u32[]{:S(2)}, u32[]{:S(2)}) %collective-permute-start.17) | collective-permute-done | bytes 32800 | tf_op jit(solution)/shard_map/ppermute | solution.py:385
  60.9 0.8 %gather.1 = bf16[1,384,512]{2,1,0:T(8,128)(2,1)} custom-call(bf16[384,128]{1,0:T(8,128)(2,1)S(1)} %finish.4.order_ref.refs_0_, bf16[384,128]{1,0:T(8,128)(2,1)S(1)} %finish.5.order_ref.refs_1_, bf16[256,128]{1,0:T(8,128)(2,1)S(1)} %finish.6.order_ref.refs_2_, bf16[384,128]{1,0:T(8,128)(2,1)S(1)} %finish.7.refs_3_.refs_6_, ...), custom_call_target="tpu_custom_call" | custom-call | flops 1 | bytes 1 | tf_op jit(solution)/shard_map/gather/pallas_call | solution.py:356
  (10 shorter events, 0.2 us)
Async XLA Ops:
  0.1 9.4 %copy-start = (bf16[3,1,384,512]{3,2,1,0:T(8,128)(2,1)S(1)}, bf16[3,1,384,512]{3,2,1,0:T(8,128)(2,1)}, u32[]{:S(2)}) copy-start(bf16[3,1,384,512]{3,2,1,0:T(8,128)(2,1)} %head_in_ref.1) | copy-start | bytes 3538948
  0.1 9.4 %copy-start.1 = (f32[3,7,512]{2,1,0:T(8,128)S(1)}, f32[3,7,512]{2,1,0:T(8,128)}, u32[]{:S(2)}) copy-start(f32[3,7,512]{2,1,0:T(8,128)} %taps_ref.3) | copy-start | bytes 129028
  0.1 9.4 %copy-start.2 = (f32[16,512]{1,0:T(8,128)S(1)}, f32[16,512]{1,0:T(8,128)}, u32[]{:S(2)}) copy-start(f32[16,512]{1,0:T(8,128)} %decay_ref.3) | copy-start | bytes 98308
  0.1 9.4 %copy-start.4 = (f32[16,512]{1,0:T(8,128)S(1)}, f32[16,512]{1,0:T(8,128)}, u32[]{:S(2)}) copy-start(f32[16,512]{1,0:T(8,128)} %residues_ref.3) | copy-start | bytes 98308
  4.5 11.7 %collective-permute-start.2 = (bf16[8,512,512]{2,1,0:T(8,128)(2,1)S(1)}, bf16[8,512,512]{2,1,0:T(8,128)(2,1)S(1)}, u32[]{:S(2)}, u32[]{:S(2)}) collective-permute-start(bf16[8,512,512]{2,1,0:T(8,128)(2,1)S(1)} %get-tuple-element.48), channel_id=1, source_target_pairs={{0,1},{1,0},{2,3},{3,2},{4,5},{5,4},{6,7},{7,6},{8,9},{9,8},{10,11... | collective-permute-start | bytes 12582920 | tf_op jit(solution)/shard_map/ppermute | solution.py:385
  5.0 7.4 %collective-permute-start = (f32[40,512]{1,0:T(8,128)S(1)}, f32[40,512]{1,0:T(8,128)S(1)}, u32[]{:S(2)}, u32[]{:S(2)}) collective-permute-start(f32[40,512]{1,0:T(8,128)S(1)} %get-tuple-element.42), channel_id=1, source_target_pairs={{0,16},{1,17},{2,18},{3,19},{4,20},{5,21},{6,22},{7,23},{8,24},{9,... | collective-permute-start | bytes 245768 | tf_op jit(solution)/shard_map/ppermute | solution.py:390
  9.5 2.9 %copy-start.3 = (f32[1,16,512]{2,1,0:T(8,128)S(1)}, f32[1,16,512]{2,1,0:T(8,128)}, u32[]{:S(2)}) copy-start(f32[1,16,512]{2,1,0:T(8,128)} %init_ref.1) | copy-start | bytes 98308
  14.4 1.8 %collective-permute-start.1 = (bf16[384,512]{1,0:T(8,128)(2,1)S(1)}, bf16[384,512]{1,0:T(8,128)(2,1)S(1)}, u32[]{:S(2)}, u32[]{:S(2)}) collective-permute-start(bf16[384,512]{1,0:T(8,128)(2,1)S(1)} %gated.1.own_ref.order_ref), channel_id=1, source_target_pairs={{0,1},{1,0},{2,3},{3,2},{4,5},{5,4},{6,7},{7,6},{8,9},{9,8},{10,11... | collective-permute-start | bytes 1179656 | tf_op jit(solution)/shard_map/ppermute | solution.py:385
  18.3 12.0 %collective-permute-start.3 = (bf16[4,384,128]{2,1,0:T(8,128)(2,1)S(1)}, bf16[4,384,128]{2,1,0:T(8,128)(2,1)S(1)}, u32[]{:S(2)}, u32[]{:S(2)}) collective-permute-start(bf16[4,384,128]{2,1,0:T(8,128)(2,1)S(1)} %get-tuple-element.50.order_ref), channel_id=1, source_target_pairs={{0,2},{1,3},{2,0},{3,1},{4,6},{5,7},{6,4},{7,5},{8,10},{9,11},{10,... | collective-permute-start | bytes 1179656 | tf_op jit(solution)/shard_map/ppermute | solution.py:385
  22.0 12.1 %collective-permute-start.6 = (bf16[4,384,128]{2,1,0:T(8,128)(2,1)S(1)}, bf16[4,384,128]{2,1,0:T(8,128)(2,1)S(1)}, u32[]{:S(2)}, u32[]{:S(2)}) collective-permute-start(bf16[4,384,128]{2,1,0:T(8,128)(2,1)S(1)} %get-tuple-element.51.order_ref), channel_id=1, source_target_pairs={{0,4},{1,5},{2,6},{3,7},{4,0},{5,1},{6,2},{7,3},{8,12},{9,13},{10,... | collective-permute-start | bytes 1179656 | tf_op jit(solution)/shard_map/ppermute | solution.py:385
  25.7 13.0 %collective-permute-start.5 = (bf16[4,384,128]{2,1,0:T(8,128)(2,1)S(1)}, bf16[4,384,128]{2,1,0:T(8,128)(2,1)S(1)}, u32[]{:S(2)}, u32[]{:S(2)}) collective-permute-start(bf16[4,384,128]{2,1,0:T(8,128)(2,1)S(1)} %get-tuple-element.52.order_ref), channel_id=1, source_target_pairs={{0,2},{1,3},{2,0},{3,1},{4,6},{5,7},{6,4},{7,5},{8,10},{9,11},{10,... | collective-permute-start | bytes 1179656 | tf_op jit(solution)/shard_map/ppermute | solution.py:385
  28.2 16.7 %collective-permute-start.10 = (bf16[4,256,128]{2,1,0:T(8,128)(2,1)S(1)}, bf16[4,256,128]{2,1,0:T(8,128)(2,1)S(1)}, u32[]{:S(2)}, u32[]{:S(2)}) collective-permute-start(bf16[4,256,128]{2,1,0:T(8,128)(2,1)S(1)} %get-tuple-element.53.order_ref), channel_id=1, source_target_pairs={{0,2},{1,3},{2,0},{3,1},{4,6},{5,7},{6,4},{7,5},{8,10},{9,11},{10,... | collective-permute-start | bytes 786440 | tf_op jit(solution)/shard_map/ppermute | solution.py:385
  30.4 11.5 %collective-permute-start.4 = (bf16[2,384,128]{2,1,0:T(8,128)(2,1)S(1)}, bf16[2,384,128]{2,1,0:T(8,128)(2,1)S(1)}, u32[]{:S(2)}, u32[]{:S(2)}) collective-permute-start(bf16[2,384,128]{2,1,0:T(8,128)(2,1)S(1)} %get-tuple-element.55.order_ref), channel_id=1, source_target_pairs={{0,4},{1,5},{2,6},{3,7},{4,0},{5,1},{6,2},{7,3},{8,12},{9,13},{10,... | collective-permute-start | bytes 589832 | tf_op jit(solution)/shard_map/ppermute | solution.py:385
  34.1 10.7 %collective-permute-start.11 = (bf16[2,384,128]{2,1,0:T(8,128)(2,1)S(1)}, bf16[2,384,128]{2,1,0:T(8,128)(2,1)S(1)}, u32[]{:S(2)}, u32[]{:S(2)}) collective-permute-start(bf16[2,384,128]{2,1,0:T(8,128)(2,1)S(1)} %get-tuple-element.59.order_ref), channel_id=1, source_target_pairs={{0,8},{1,9},{2,10},{3,11},{4,12},{5,13},{6,14},{7,15},{8,0},{9,1},... | collective-permute-start | bytes 589832 | tf_op jit(solution)/shard_map/ppermute | solution.py:385
  38.8 9.8 %collective-permute-start.9 = (bf16[2,384,128]{2,1,0:T(8,128)(2,1)S(1)}, bf16[2,384,128]{2,1,0:T(8,128)(2,1)S(1)}, u32[]{:S(2)}, u32[]{:S(2)}) collective-permute-start(bf16[2,384,128]{2,1,0:T(8,128)(2,1)S(1)} %get-tuple-element.60.order_ref), channel_id=1, source_target_pairs={{0,4},{1,5},{2,6},{3,7},{4,0},{5,1},{6,2},{7,3},{8,12},{9,13},{10,... | collective-permute-start | bytes 589832 | tf_op jit(solution)/shard_map/ppermute | solution.py:385
  40.5 10.7 %collective-permute-start.8 = (bf16[4,128,128]{2,1,0:T(8,128)(2,1)S(1)}, bf16[4,128,128]{2,1,0:T(8,128)(2,1)S(1)}, u32[]{:S(2)}, u32[]{:S(2)}) collective-permute-start(bf16[4,128,128]{2,1,0:T(8,128)(2,1)S(1)} %get-tuple-element.58.order_ref), channel_id=1, source_target_pairs={{0,2},{1,3},{2,0},{3,1},{4,6},{5,7},{6,4},{7,5},{8,10},{9,11},{10,... | collective-permute-start | bytes 393224 | tf_op jit(solution)/shard_map/ppermute | solution.py:385
  44.9 9.4 %collective-permute-start.13 = (bf16[2,256,128]{2,1,0:T(8,128)(2,1)S(1)}, bf16[2,256,128]{2,1,0:T(8,128)(2,1)S(1)}, u32[]{:S(2)}, u32[]{:S(2)}) collective-permute-start(bf16[2,256,128]{2,1,0:T(8,128)(2,1)S(1)} %get-tuple-element.68.order_ref), channel_id=1, source_target_pairs={{0,4},{1,5},{2,6},{3,7},{4,0},{5,1},{6,2},{7,3},{8,12},{9,13},{10,... | collective-permute-start | bytes 393224 | tf_op jit(solution)/shard_map/ppermute | solution.py:385
  46.1 11.6 %collective-permute-start.7 = (bf16[1,384,128]{2,1,0:T(8,128)(2,1)S(1)}, bf16[1,384,128]{2,1,0:T(8,128)(2,1)S(1)}, u32[]{:S(2)}, u32[]{:S(2)}) collective-permute-start(bf16[1,384,128]{2,1,0:T(8,128)(2,1)S(1)} %get-tuple-element.62.order_ref), channel_id=1, source_target_pairs={{0,8},{1,9},{2,10},{3,11},{4,12},{5,13},{6,14},{7,15},{8,0},{9,1},... | collective-permute-start | bytes 294920 | tf_op jit(solution)/shard_map/ppermute | solution.py:385
  48.7 10.7 %collective-permute-start.14 = (bf16[1,384,128]{2,1,0:T(8,128)(2,1)S(1)}, bf16[1,384,128]{2,1,0:T(8,128)(2,1)S(1)}, u32[]{:S(2)}, u32[]{:S(2)}) collective-permute-start(bf16[1,384,128]{2,1,0:T(8,128)(2,1)S(1)} %get-tuple-element.69.order_ref), channel_id=1, source_target_pairs={{0,8},{1,9},{2,10},{3,11},{4,12},{5,13},{6,14},{7,15},{8,0},{9,1},... | collective-permute-start | bytes 294920 | tf_op jit(solution)/shard_map/ppermute | solution.py:385
  51.2 4.8 %collective-permute-start.12 = (bf16[2,128,128]{2,1,0:T(8,128)(2,1)S(1)}, bf16[2,128,128]{2,1,0:T(8,128)(2,1)S(1)}, u32[]{:S(2)}, u32[]{:S(2)}) collective-permute-start(bf16[2,128,128]{2,1,0:T(8,128)(2,1)S(1)} %get-tuple-element.71.order_ref), channel_id=1, source_target_pairs={{0,4},{1,5},{2,6},{3,7},{4,0},{5,1},{6,2},{7,3},{8,12},{9,13},{10,... | collective-permute-start | bytes 196616 | tf_op jit(solution)/shard_map/ppermute | solution.py:385
  53.7 6.5 %collective-permute-start.16 = (bf16[1,384,128]{2,1,0:T(8,128)(2,1)S(1)}, bf16[1,384,128]{2,1,0:T(8,128)(2,1)S(1)}, u32[]{:S(2)}, u32[]{:S(2)}) collective-permute-start(bf16[1,384,128]{2,1,0:T(8,128)(2,1)S(1)} %get-tuple-element.67.order_ref), channel_id=1, source_target_pairs={{0,2},{1,3},{2,0},{3,1},{4,6},{5,7},{6,4},{7,5},{8,10},{9,11},{10,... | collective-permute-start | bytes 294920 | tf_op jit(solution)/shard_map/ppermute | solution.py:385
  54.4 5.8 %collective-permute-start.15 = (bf16[1,256,128]{2,1,0:T(8,128)(2,1)S(1)}, bf16[1,256,128]{2,1,0:T(8,128)(2,1)S(1)}, u32[]{:S(2)}, u32[]{:S(2)}) collective-permute-start(bf16[1,256,128]{2,1,0:T(8,128)(2,1)S(1)} %get-tuple-element.73.order_ref), channel_id=1, source_target_pairs={{0,8},{1,9},{2,10},{3,11},{4,12},{5,13},{6,14},{7,15},{8,0},{9,1},... | collective-permute-start | bytes 196616 | tf_op jit(solution)/shard_map/ppermute | solution.py:385
  56.0 4.9 %collective-permute-start.17 = (bf16[1,128,128]{2,1,0:T(8,128)(2,1)S(1)}, bf16[1,128,128]{2,1,0:T(8,128)(2,1)S(1)}, u32[]{:S(2)}, u32[]{:S(2)}) collective-permute-start(bf16[1,128,128]{2,1,0:T(8,128)(2,1)S(1)} %get-tuple-element.74.order_ref), channel_id=1, source_target_pairs={{0,8},{1,9},{2,10},{3,11},{4,12},{5,13},{6,14},{7,15},{8,0},{9,1},... | collective-permute-start | bytes 98312 | tf_op jit(solution)/shard_map/ppermute | solution.py:385

commit v3 on v2

--- a/solution.py
+++ b/solution.py
@@ -40,11 +40,13 @@
 
 
 def weight_columns(weight_hbm, ref, side, sems):
-    width = ref.shape[2]
+    parts, _, width = ref.shape
     copies = []
-    for part in range(ref.shape[0]):
+    for part in range(parts):
         column = pl.multiple_of((2 * part + side) * width, LANES)
         copies.append(pltpu.make_async_copy(weight_hbm.at[:, pl.ds(column, width)], ref.at[part], sems.at[part]))
+    for copy in copies:
+        copy.start()
     return copies
 
 
@@ -56,7 +58,6 @@
     length, channels = streams_hbm.shape[2:]
     tiles = channels // LANES
     seg_len, turn = segments(length)
-    heads = -(-(PAD + tap_count) // turn)
     small = [
         pltpu.make_async_copy(taps_hbm, taps_ref, sems.at[0]),
         pltpu.make_async_copy(decay_hbm, decay_ref, sems.at[1]),
@@ -71,12 +72,9 @@
     for copy in small + loads[1:]:
         copy.start()
     copies = weight_columns(weight_hbm, sent_ref, 1 - core, weight_sems)
-    for copy in copies:
-        copy.start()
     for copy in small:
         copy.wait()
     sublane = lax.broadcasted_iota(jnp.int32, (SEGS, LANES), 0)
-    early = jnp.logical_and(sublane == 0, jnp.logical_not(first))
     for tile in range(tiles):
         lanes = slice(tile * LANES, (tile + 1) * LANES)
         loads[tile].wait()
@@ -88,7 +86,7 @@
         def row(s, j):
             return wide_ref[s, pl.ds(PAD + j, SEGS, stride=seg_len), :]
 
-        def block(base, windows, masked):
+        def block(base, windows):
             windows = list(windows)
             for step in range(turn):
                 made = []
@@ -96,16 +94,13 @@
                     seen = list(windows[s]) + [row(s, base + step)]
                     made.append(tree_sum([taps[s][i] * seen[-1 - i] for i in range(tap_count)]))
                     windows[s] = tuple(seen[1:])
-                product = made[0] * made[1]
-                if masked and PAD <= base + step < PAD + tap_count - 1:
-                    product = jnp.where(early, 0.0, product)
-                driven_ref[tile, base + step] = product
+                driven_ref[tile, base + step] = made[0] * made[1]
             return tuple(windows)
 
         windows = tuple(tuple(row(s, j - (tap_count - 1)) for j in range(tap_count - 1)) for s in range(2))
-        for b in range(heads):
-            windows = block(b * turn, windows, True)
-        lax.fori_loop(heads, seg_len // turn, lambda b, w: block(b * turn, w, False), windows)
+        lax.fori_loop(0, seg_len // turn, lambda b, w: block(b * turn, w), windows)
+        for j in range(tap_count - 1):
+            driven_ref[tile, PAD + j, 0:1, :] = jnp.where(first, driven_ref[tile, PAD + j, 0:1, :], 0.0)
 
         decays = [jnp.broadcast_to(decay_ref[n : n + 1, lanes], (SEGS, LANES)) for n in range(poles)]
 
@@ -142,8 +137,6 @@
     tiles = channels // LANES
     seg_len, turn = segments(length)
     copies = weight_columns(weight_hbm, mine_ref, where_ref[1], weight_sems)
-    for copy in copies:
-        copy.start()
     sublane = lax.broadcasted_iota(jnp.int32, (SEGS, LANES), 0)
     for tile in range(tiles):
         lanes = slice(tile * LANES, (tile + 1) * LANES)
@@ -181,7 +174,7 @@
         copy.wait()
 
 
-def gated_kernel(where_ref, message_ref, head_in_ref, taps_ref, decay_ref, residues_ref, init_ref, response_ref, query_ref, gated_ref, head_ref, start_ref, out_ref):
+def gated_kernel(where_ref, message_ref, head_in_ref, taps_ref, decay_ref, residues_ref, init_ref, response_ref, query_ref, gated_ref, head_ref, start_ref, out_ref, early_ref):
     first = where_ref[0] == 0
     poles = decay_ref.shape[0]
     tap_count = taps_ref.shape[1]
@@ -189,22 +182,23 @@
     length, channels = gated_ref.shape
     tiles = channels // LANES
     seg_len, turn = segments(length)
-    heads_count = -(-(PAD + tap_count) // turn)
     sublane = lax.broadcasted_iota(jnp.int32, (SEGS, LANES), 0)
 
     heads = []
     for s in range(3):
-        head_ref[0:PAD, :] = message_ref[poles + s * PAD : poles + (s + 1) * PAD, :]
+        head_ref[0:PAD, :] = jnp.where(first, 0.0, message_ref[poles + s * PAD : poles + (s + 1) * PAD, :])
         head_ref[PAD : PAD + 16, :] = head_in_ref[s, 0, 0:16, :].astype(F32)
         heads.append(tree_sum([taps_ref[s, i : i + 1, :] * head_ref[PAD - i : 2 * PAD - i, :] for i in range(tap_count)]))
     head_query = heads[0]
     counted = jnp.where(first, 0.0, heads[1] * heads[2])
-    decay = decay_ref[...]
+    decay, residues = decay_ref[...], residues_ref[...]
     state = jnp.where(first, init_ref[0], message_ref[0:poles, :])
-    start_ref[0:poles, :] = state * residues_ref[...]
     for j in range(lag):
         state = decay * state + counted[j : j + 1, :]
-    start_ref[poles:, :] = state * residues_ref[...] * power(decay, seg_len - PAD - lag)
+        early_ref[j : j + 1, :] = jnp.sum(residues * state, axis=0, keepdims=True)
+    state = state * residues
+    start_ref[0:poles, :] = state / power(decay, PAD + lag)
+    start_ref[poles:, :] = state * power(decay, seg_len - PAD - lag)
 
     for tile in range(tiles):
         lanes = slice(tile * LANES, (tile + 1) * LANES)
@@ -217,28 +211,22 @@
             for bit in (1, 2, 4):
                 spread = jnp.where(jnp.bitwise_and(before, bit) != 0, spread * factor, spread)
                 factor = factor * factor
-            states.append(jnp.where(sublane == 0, 0.0, spread))
-
-        def block(b, states, head):
+            own = jnp.broadcast_to(start_ref[n : n + 1, lanes], (SEGS, LANES))
+            states.append(jnp.where(sublane == 0, own, spread))
+
+        def block(b, states):
             states = list(states)
             for step in range(turn):
                 at = b * turn + step
-                query = query_ref[tile, at]
-                if head and at == PAD:
-                    states = [jnp.where(sublane == 0, jnp.broadcast_to(start_ref[n : n + 1, lanes], (SEGS, LANES)), s) for n, s in enumerate(states)]
                 states = [d * s for d, s in zip(decays, states)]
-                if head and PAD <= at < PAD + lag:
-                    j = at - PAD
-                    value = jnp.where(sublane == 0, jnp.broadcast_to(counted[j : j + 1, lanes], (SEGS, LANES)), 0.0)
-                    states = [s + value * jnp.broadcast_to(residues_ref[n : n + 1, lanes], (SEGS, LANES)) for n, s in enumerate(states)]
-                    query = jnp.where(sublane == 0, jnp.broadcast_to(head_query[j : j + 1, lanes], (SEGS, LANES)), query)
                 total = response_ref[tile, at] + tree_sum(states)
-                out_ref[pl.ds(at, SEGS, stride=seg_len), :] = total * query
+                out_ref[pl.ds(at, SEGS, stride=seg_len), :] = total * query_ref[tile, at]
             return tuple(states)
 
-        for b in range(heads_count):
-            states = block(b, states, True)
-        lax.fori_loop(heads_count, seg_len // turn, lambda b, states: block(b, states, False), states)
+        lax.fori_loop(0, seg_len // turn, block, tuple(states))
+        for j in range(lag):
+            total = response_ref[tile, PAD + j, 0:1, :] + early_ref[j : j + 1, lanes]
+            out_ref[PAD + j : PAD + j + 1, :] = total * head_query[j : j + 1, lanes]
         gated_ref[:, lanes] = out_ref[PAD:, :].astype(BF16)
 
 
@@ -250,22 +238,46 @@
     return value
 
 
+def sides(part, where_ref, weight_ref, index):
+    _, _, column, columns = part.box
+    blocks = [relative(index, high, part.order) ^ where_ref[2] for high in (1, 0)]
+    return jnp.concatenate([weight_ref[block, :, column : column + columns] for block in blocks], axis=1)
+
+
 def project_kernel(part, where_ref, own_ref, other_ref, mine_ref, theirs_ref, order_ref, send_ref, keep_ref):
-    row, rows, column, columns = part.box
-    take = slice(column, column + columns)
+    row, rows, _, columns = part.box
     wide = jnp.concatenate([own_ref[row : row + rows, :], other_ref[row : row + rows, :]], axis=1)
 
-    def step(index, carry):
-        sides = []
-        for high in (1, 0):
-            block = relative(index, high, part.order) ^ where_ref[2]
-            sides.append(jnp.concatenate([mine_ref[block, :, take], theirs_ref[block, :, take]], axis=0))
-        total = jnp.dot(wide, jnp.concatenate(sides, axis=1), preferred_element_type=F32)
+    def step(index):
+        both = jnp.concatenate([sides(part, where_ref, ref, index) for ref in (mine_ref, theirs_ref)], axis=0)
+        total = jnp.dot(wide, both, preferred_element_type=F32)
         send_ref[index] = total[:, :columns].astype(BF16)
         keep_ref[index] = total[:, columns:]
-        return carry
-
-    lax.fori_loop(0, send_ref.shape[0], step, 0)
+
+    for index in range(send_ref.shape[0]):
+        step(index)
+
+
+def project_own_kernel(part, where_ref, own_ref, mine_ref, out_ref):
+    row, rows, _, _ = part.box
+
+    def step(index):
+        out_ref[index] = jnp.dot(own_ref[row : row + rows, :], sides(part, where_ref, mine_ref, index), preferred_element_type=F32)
+
+    for index in range(out_ref.shape[0]):
+        step(index)
+
+
+def project_other_kernel(part, where_ref, sum_ref, other_ref, theirs_ref, send_ref, keep_ref):
+    row, rows, _, columns = part.box
+
+    def step(index):
+        total = sum_ref[index] + jnp.dot(other_ref[row : row + rows, :], sides(part, where_ref, theirs_ref, index), preferred_element_type=F32)
+        send_ref[index] = total[:, :columns].astype(BF16)
+        keep_ref[index] = total[:, columns:]
+
+    for index in range(send_ref.shape[0]):
+        step(index)
 
 
 def merge_kernel(keep_ref, received_ref, order_ref, send_ref, kept_ref):
@@ -326,6 +338,33 @@
     )(where, own, other, mine, theirs, ordered)
 
 
+def project_own(part, where, own, mine):
+    _, rows, _, columns = part.box
+    return pl.pallas_call(
+        functools.partial(project_own_kernel, part),
+        out_shape=jax.ShapeDtypeStruct((mine.shape[0] // 2, rows, 2 * columns), F32),
+        in_specs=[SMEM, VMEM, VMEM],
+        out_specs=VMEM,
+        compiler_params=pltpu.CompilerParams(vmem_limit_bytes=LIMIT),
+        cost_estimate=QUICK,
+        name="project_own",
+    )(where, own, mine)
+
+
+def project_other(part, where, total, other, theirs):
+    _, rows, _, columns = part.box
+    shape = (total.shape[0], rows, columns)
+    return pl.pallas_call(
+        functools.partial(project_other_kernel, part),
+        out_shape=(jax.ShapeDtypeStruct(shape, BF16), jax.ShapeDtypeStruct(shape, F32)),
+        in_specs=[SMEM, VMEM, VMEM, VMEM],
+        out_specs=(VMEM, VMEM),
+        compiler_params=pltpu.CompilerParams(vmem_limit_bytes=LIMIT),
+        cost_estimate=QUICK,
+        name="project_other",
+    )(where, total, other, theirs)
+
+
 def merge(keep, received, ordered):
     half = keep.shape[0] // 2
     shape = (half,) + keep.shape[1:]
@@ -371,7 +410,7 @@
     count = width // LANES
     if count == 4 and len(bits) == 3 and length % 48 == 0:
         third = length // 3
-        boxes = [(0, length, 0, LANES), (0, length, LANES, LANES), (0, 2 * third, 2 * LANES, LANES), (2 * third, third, 2 * LANES, LANES), (0, length, 3 * LANES, LANES)]
+        boxes = [(0, length, 0, LANES), (0, length, 2 * LANES, LANES), (0, 2 * third, 3 * LANES, LANES), (2 * third, third, 3 * LANES, LANES), (0, length, LANES, LANES)]
         parts = [Part(box, bits) for box in boxes[:4]] + [Part(boxes[4], far)]
         steps = [(0, -1), (4, -1), (1, -1), (2, -1), (0, 0), (3, -1), (4, 0), (1, 0), (0, 1), (4, 1), (2, 0), (1, 1), (3, 0), (2, 1), (3, 1), (0, 2), (1, 2), (2, 2), (4, 2), (3, 2)]
     else:
@@ -387,7 +426,7 @@
 
 def after(x, axis):
     count = lax.axis_size(axis)
-    return lax.ppermute(x, axis, [(i, i + 1) for i in range(count - 1)])
+    return lax.ppermute(x, axis, [(i, (i + 1) % count) for i in range(count)])
 
 
 def later_rounds(message, inner_end, streams, taps, decay, init_state):
@@ -425,13 +464,14 @@
     rows = poles + 3 * PAD
     streams_hbm, weight_hbm = in_hbm(streams), in_hbm(out_weight)
     split = (tiles, seg_len, SEGS, LANES)
+    columns = jax.ShapeDtypeStruct((peers // 2, channels, width), BF16)
     driven, inner, message, sent = pl.pallas_call(
         driven_kernel,
         out_shape=(
             jax.ShapeDtypeStruct(split, F32),
             jax.ShapeDtypeStruct((tiles, poles, SEGS, LANES), F32),
             jax.ShapeDtypeStruct((rows, channels), F32),
-            jax.ShapeDtypeStruct((peers // 2, channels, width), BF16),
+            columns,
         ),
         in_specs=[SMEM, HBM, HBM, HBM, HBM, HBM],
         out_specs=(VMEM, VMEM, VMEM, VMEM),
@@ -450,13 +490,13 @@
         name="driven",
     )(where, streams_hbm, in_hbm(taps), in_hbm(decay), in_hbm(init_state), weight_hbm)
     passed = after(message, "ctx")
-    swapped = across(sent, 0)
+    theirs = across(sent, 0)
     response, query, mine = pl.pallas_call(
         response_kernel,
         out_shape=(
             jax.ShapeDtypeStruct(split, F32),
             jax.ShapeDtypeStruct(split, F32),
-            jax.ShapeDtypeStruct((peers // 2, channels, width), BF16),
+            columns,
         ),
         in_specs=[SMEM] + [VMEM] * 6 + [HBM],
         out_specs=(VMEM, VMEM, VMEM),
@@ -476,6 +516,7 @@
             pltpu.VMEM((PAD + 16, channels), F32),
             pltpu.VMEM((2 * poles, channels), F32),
             pltpu.VMEM((PAD + length, LANES), F32),
+            pltpu.VMEM((PAD, channels), F32),
         ],
         compiler_params=pltpu.CompilerParams(vmem_limit_bytes=LIMIT),
         cost_estimate=QUICK,
@@ -485,10 +526,14 @@
 
     parts, steps = plan(peers, length, width)
     flying, kept, finished, ordered = {}, {}, {}, gated
+    started = project_own(parts[steps[0][0]], where, gated, mine)
     for at, stage in steps:
         part = parts[at]
         if stage < 0:
-            send, kept[at] = project(part, where, gated, other, mine, swapped, ordered)
+            if at == steps[0][0]:
+                send, kept[at] = project_other(part, where, started, other, theirs)
+            else:
+                send, kept[at] = project(part, where, gated, other, mine, theirs, ordered)
             ordered = send
         elif stage + 1 < len(part.order):
             send, kept[at] = merge(kept[at], flying[at], ordered)

time: 61.8 us -> 58.8 us (0.951)
  Pallas kernels: 20.2 us -> 18.1 us
  starting transfers between devices: 29.2 us -> 28.2 us
    pallas_call x5 -> x4, Pallas kernels: 9.7 us -> 5.34 us  [project(): pl.pallas_call(functools.partial(project_kernel, part), out_shape=(jax.Sh...]
    pallas_call x0 -> x2, Pallas kernels: none -> 2.25 us  [the longest x1 1.13 us: project_other(): pl.pallas_call(functools.partial(project_other_kernel, part), out_shape=(...]
    ppermute x1, starting transfers between devices: 4.44 us -> 2.59 us  [after(): return lax.ppermute(x, axis, [(i, (i + 1) % count) for i in range(count)])]
    ppermute x17, starting transfers between devices: 24.7 us -> 25.6 us  [across(): return lax.ppermute(x, 'tp', [(i, i ^ 1 << bit) for i in range(count)])]
  transfers between devices with their start and end apart: 18 -> 18, of which waited for: 9 -> 11; matrix products, arithmetic and copies ran while one was open for 0% -> 0% of each run, Pallas kernels for 21% -> 20%
where the time goes in v3:
time: 58.8 us; the launch traced here: 58.7 us
  starting transfers between devices  28.2 us (48%)
  Pallas kernels  18.1 us (31%)
  waiting for transfers between devices  12.1 us (21%)
    ppermute x17, starting transfers between devices, across(): return lax.ppermute(x, 'tp', [(i, i ^ 1 << bit) for i in range(count)])  25.6 us
    ppermute x17, waiting for transfers between devices, across(): return lax.ppermute(x, 'tp', [(i, i ^ 1 << bit) for i in range(count)])  11.9 us
    pallas_call x4, Pallas kernels, project(): pl.pallas_call(functools.partial(project_kernel, part), out_shape=(jax.Sh...  5.34 us
    pallas_call x1, Pallas kernels, per_device(): pl.pallas_call(driven_kernel, out_shape=(jax.ShapeDtypeStruct(split, F32)...  4.44 us
    pallas_call x1, Pallas kernels, per_device(): pl.pallas_call(response_kernel, out_shape=(jax.ShapeDtypeStruct(split, F3...  2.89 us
    ppermute x1, starting transfers between devices, after(): return lax.ppermute(x, axis, [(i, (i + 1) % count) for i in range(count)])  2.59 us
    pallas_call x1, Pallas kernels, per_device(): pl.pallas_call(gated_kernel, out_shape=jax.ShapeDtypeStruct((length, chan...  1.93 us
  transfers between devices with their start and end apart: 18, of which 11 were waited for; matrix products, arithmetic and copies ran while one was open for 0% of the time, Pallas kernels for 20%

profile of v3, /device:TPU:0, one launch (start us, length us, event | category | flops | bytes accessed | tf_op | source)
XLA Modules:
  0.0 58.7 jit_solution(9488093995247008791)
XLA Ops:
  0.0 0.1 pad_add_fusion.where_ref
  0.1 0.0 copy-start
  0.1 0.0 copy-start.1
  0.1 0.0 copy-start.2
  0.1 0.0 copy-start.4
  0.1 4.4 %driven.1 = (f32[4,49,8,128]{3,2,1,0:T(8,128)S(1)}, f32[4,16,8,128]{3,2,1,0:T(8,128)S(1)}, f32[40,512]{1,0:T(8,128)S(1)}, bf16[8,512,512]{2,1,0:T(8,128)(2,1)S(1)}) custom-call(s32[3]{0:T(128)S(1)} %pad_add_fusion.where_ref, bf16[3,1,384,512]{3,2,1,0:T(8,128)(2,1)} %head_in_ref.1, f32[3,7,512]{2,1,0:T(8,128)} %taps_ref.3, f32[16,512]{1,0:T(8,128)} %decay_ref.3, ...), custom_call_target="tpu_custom_call" | custom-call | flops 1 | bytes 1 | tf_op jit(solution)/shard_map/driven/pallas_call | solution.py:468
  4.5 0.5 collective-permute-start.2
  5.1 2.6 %collective-permute-start = (f32[40,512]{1,0:T(8,128)S(1)}, f32[40,512]{1,0:T(8,128)S(1)}, u32[]{:S(2)}, u32[]{:S(2)}) collective-permute-start(f32[40,512]{1,0:T(8,128)S(1)} %get-tuple-element.42), channel_id=1, source_target_pairs={{0,16},{16,0},{1,17},{17,1},{2,18},{18,2},{3,19},{19,3},{4,20},{20... | collective-permute-start | bytes 245768 | tf_op jit(solution)/shard_map/ppermute | solution.py:429
  7.7 0.0 copy-done
  7.7 0.0 copy-done.1
  7.7 0.0 copy-done.2
  7.7 0.0 copy-done.4
  7.7 0.0 copy-start.3
  7.7 2.9 %response.1 = (f32[4,49,8,128]{3,2,1,0:T(8,128)S(1)}, f32[4,49,8,128]{3,2,1,0:T(8,128)S(1)}, bf16[8,512,512]{2,1,0:T(8,128)(2,1)S(1)}) custom-call(s32[3]{0:T(128)S(1)} %pad_add_fusion.where_ref, bf16[3,1,384,512]{3,2,1,0:T(8,128)(2,1)S(1)} %copy-done, f32[3,7,512]{2,1,0:T(8,128)S(1)} %copy-done.1, f32[16,512]{1,0:T(8,128)S(1)} %copy-done.2, ...), custom_call_target="tpu_custom_call" | custom-call | flops 1 | bytes 1 | tf_op jit(solution)/shard_map/response/pallas_call | solution.py:494
  10.6 0.1 collective-permute-done.message_ref
  10.7 0.0 copy-done.3
  10.7 1.9 %gated.1.own_ref = bf16[384,512]{1,0:T(8,128)(2,1)S(1)} custom-call(s32[3]{0:T(128)S(1)} %pad_add_fusion.where_ref, f32[40,512]{1,0:T(8,128)S(1)} %collective-permute-done.message_ref, bf16[3,1,384,512]{3,2,1,0:T(8,128)(2,1)S(1)} %copy-done, f32[3,7,512]{2,1,0:T(8,128)S(1)} %copy-done.1, f32[16,512]{1,0:T(8,128)S(1)} %copy-done.2, f32[16,512]{1,0:T(8,128)S(1)} %copy-done.4, ...), custom_call_target="tpu_custom_call" | custom-call | flops 1 | bytes 1 | tf_op jit(solution)/shard_map/gated/pallas_call | solution.py:510
  12.6 0.1 collective-permute-start.1
  12.8 1.1 %project_own.1.sum_ref = f32[4,384,256]{2,1,0:T(8,128)S(1)} custom-call(s32[3]{0:T(128)S(1)} %pad_add_fusion.where_ref, bf16[384,512]{1,0:T(8,128)(2,1)S(1)} %gated.1.own_ref, bf16[8,512,512]{2,1,0:T(8,128)(2,1)S(1)} %get-tuple-element.47.mine_ref), custom_call_target="tpu_custom_call" | custom-call | flops 1 | bytes 1 | tf_op jit(solution)/shard_map/project_own/pallas_call | solution.py:343
  13.9 0.5 collective-permute-done.1.other_ref
  14.4 0.0 collective-permute-done.2.theirs_ref
  14.4 1.1 %project_other.1 = (bf16[4,384,128]{2,1,0:T(8,128)(2,1)S(1)}, f32[4,384,128]{2,1,0:T(8,128)S(1)}) custom-call(s32[3]{0:T(128)S(1)} %pad_add_fusion.where_ref, f32[4,384,256]{2,1,0:T(8,128)S(1)} %project_own.1.sum_ref, bf16[384,512]{1,0:T(8,128)(2,1)S(1)} %collective-permute-done.1.other_ref, bf16[8,512,512]{2,1,0:T(8,128)(2,1)S(1)} %collective-permute-done.2.theirs_ref), custom_call_target="tpu_custom_call" | custom-call | flops 1 | bytes 1 | tf_op jit(solution)/shard_map/project_other/pallas_call | solution.py:357
  15.6 1.8 %collective-permute-start.3 = (bf16[4,384,128]{2,1,0:T(8,128)(2,1)S(1)}, bf16[4,384,128]{2,1,0:T(8,128)(2,1)S(1)}, u32[]{:S(2)}, u32[]{:S(2)}) collective-permute-start(bf16[4,384,128]{2,1,0:T(8,128)(2,1)S(1)} %get-tuple-element.50.order_ref), channel_id=1, source_target_pairs={{0,2},{1,3},{2,0},{3,1},{4,6},{5,7},{6,4},{7,5},{8,10},{9,11},{10,... | collective-permute-start | bytes 1179656 | tf_op jit(solution)/shard_map/ppermute | solution.py:424
  17.4 1.5 %project.4 = (bf16[4,384,128]{2,1,0:T(8,128)(2,1)S(1)}, f32[4,384,128]{2,1,0:T(8,128)S(1)}) custom-call(s32[3]{0:T(128)S(1)} %pad_add_fusion.where_ref, bf16[384,512]{1,0:T(8,128)(2,1)S(1)} %gated.1.own_ref, bf16[384,512]{1,0:T(8,128)(2,1)S(1)} %collective-permute-done.1.other_ref, bf16[8,512,512]{2,1,0:T(8,128)(2,1)S(1)} %get-tuple-element.47.mine_ref, ...), custom_call_target="tpu_custom_call" | custom-call | flops 1 | bytes 1 | tf_op jit(solution)/shard_map/project/pallas_call | solution.py:330
  18.9 1.6 %collective-permute-start.6 = (bf16[4,384,128]{2,1,0:T(8,128)(2,1)S(1)}, bf16[4,384,128]{2,1,0:T(8,128)(2,1)S(1)}, u32[]{:S(2)}, u32[]{:S(2)}) collective-permute-start(bf16[4,384,128]{2,1,0:T(8,128)(2,1)S(1)} %get-tuple-element.51.order_ref), channel_id=1, source_target_pairs={{0,4},{1,5},{2,6},{3,7},{4,0},{5,1},{6,2},{7,3},{8,12},{9,13},{10,... | collective-permute-start | bytes 1179656 | tf_op jit(solution)/shard_map/ppermute | solution.py:424
  20.5 1.5 %project.5 = (bf16[4,384,128]{2,1,0:T(8,128)(2,1)S(1)}, f32[4,384,128]{2,1,0:T(8,128)S(1)}) custom-call(s32[3]{0:T(128)S(1)} %pad_add_fusion.where_ref, bf16[384,512]{1,0:T(8,128)(2,1)S(1)} %gated.1.own_ref, bf16[384,512]{1,0:T(8,128)(2,1)S(1)} %collective-permute-done.1.other_ref, bf16[8,512,512]{2,1,0:T(8,128)(2,1)S(1)} %get-tuple-element.47.mine_ref, ...), custom_call_target="tpu_custom_call" | custom-call | flops 1 | bytes 1 | tf_op jit(solution)/shard_map/project/pallas_call | solution.py:330
  22.1 0.6 %collective-permute-start.5 = (bf16[4,384,128]{2,1,0:T(8,128)(2,1)S(1)}, bf16[4,384,128]{2,1,0:T(8,128)(2,1)S(1)}, u32[]{:S(2)}, u32[]{:S(2)}) collective-permute-start(bf16[4,384,128]{2,1,0:T(8,128)(2,1)S(1)} %get-tuple-element.52.order_ref), channel_id=1, source_target_pairs={{0,2},{1,3},{2,0},{3,1},{4,6},{5,7},{6,4},{7,5},{8,10},{9,11},{10,... | collective-permute-start | bytes 1179656 | tf_op jit(solution)/shard_map/ppermute | solution.py:424
  22.7 1.3 %project.6 = (bf16[4,256,128]{2,1,0:T(8,128)(2,1)S(1)}, f32[4,256,128]{2,1,0:T(8,128)S(1)}) custom-call(s32[3]{0:T(128)S(1)} %pad_add_fusion.where_ref, bf16[384,512]{1,0:T(8,128)(2,1)S(1)} %gated.1.own_ref, bf16[384,512]{1,0:T(8,128)(2,1)S(1)} %collective-permute-done.1.other_ref, bf16[8,512,512]{2,1,0:T(8,128)(2,1)S(1)} %get-tuple-element.47.mine_ref, ...), custom_call_target="tpu_custom_call" | custom-call | flops 1 | bytes 1 | tf_op jit(solution)/shard_map/project/pallas_call | solution.py:330
  24.0 1.6 %collective-permute-start.10 = (bf16[4,256,128]{2,1,0:T(8,128)(2,1)S(1)}, bf16[4,256,128]{2,1,0:T(8,128)(2,1)S(1)}, u32[]{:S(2)}, u32[]{:S(2)}) collective-permute-start(bf16[4,256,128]{2,1,0:T(8,128)(2,1)S(1)} %get-tuple-element.53.order_ref), channel_id=1, source_target_pairs={{0,2},{1,3},{2,0},{3,1},{4,6},{5,7},{6,4},{7,5},{8,10},{9,11},{10,... | collective-permute-start | bytes 786440 | tf_op jit(solution)/shard_map/ppermute | solution.py:424
  25.5 2.1 %collective-permute-done.3.received_ref = bf16[4,384,128]{2,1,0:T(8,128)(2,1)S(1)} collective-permute-done((bf16[4,384,128]{2,1,0:T(8,128)(2,1)S(1)}, bf16[4,384,128]{2,1,0:T(8,128)(2,1)S(1)}, u32[]{:S(2)}, u32[]{:S(2)}) %collective-permute-start.3) | collective-permute-done | bytes 393248 | tf_op jit(solution)/shard_map/ppermute | solution.py:424
  27.6 0.1 merge.10
  27.7 1.9 %collective-permute-start.4 = (bf16[2,384,128]{2,1,0:T(8,128)(2,1)S(1)}, bf16[2,384,128]{2,1,0:T(8,128)(2,1)S(1)}, u32[]{:S(2)}, u32[]{:S(2)}) collective-permute-start(bf16[2,384,128]{2,1,0:T(8,128)(2,1)S(1)} %get-tuple-element.55.order_ref), channel_id=1, source_target_pairs={{0,4},{1,5},{2,6},{3,7},{4,0},{5,1},{6,2},{7,3},{8,12},{9,13},{10,... | collective-permute-start | bytes 589832 | tf_op jit(solution)/shard_map/ppermute | solution.py:424
  29.5 1.0 %project.7 = (bf16[4,128,128]{2,1,0:T(8,128)(2,1)S(1)}, f32[4,128,128]{2,1,0:T(8,128)S(1)}) custom-call(s32[3]{0:T(128)S(1)} %pad_add_fusion.where_ref, bf16[384,512]{1,0:T(8,128)(2,1)S(1)} %gated.1.own_ref, bf16[384,512]{1,0:T(8,128)(2,1)S(1)} %collective-permute-done.1.other_ref, bf16[8,512,512]{2,1,0:T(8,128)(2,1)S(1)} %get-tuple-element.47.mine_ref, ...), custom_call_target="tpu_custom_call" | custom-call | flops 1 | bytes 1 | tf_op jit(solution)/shard_map/project/pallas_call | solution.py:330
  30.6 0.2 collective-permute-done.6.received_ref
  30.7 0.1 merge.11
  30.8 2.5 %collective-permute-start.11 = (bf16[2,384,128]{2,1,0:T(8,128)(2,1)S(1)}, bf16[2,384,128]{2,1,0:T(8,128)(2,1)S(1)}, u32[]{:S(2)}, u32[]{:S(2)}) collective-permute-start(bf16[2,384,128]{2,1,0:T(8,128)(2,1)S(1)} %get-tuple-element.59.order_ref), channel_id=1, source_target_pairs={{0,8},{1,9},{2,10},{3,11},{4,12},{5,13},{6,14},{7,15},{8,0},{9,1},... | collective-permute-start | bytes 589832 | tf_op jit(solution)/shard_map/ppermute | solution.py:424
  33.3 2.7 %collective-permute-done.5.received_ref = bf16[4,384,128]{2,1,0:T(8,128)(2,1)S(1)} collective-permute-done((bf16[4,384,128]{2,1,0:T(8,128)(2,1)S(1)}, bf16[4,384,128]{2,1,0:T(8,128)(2,1)S(1)}, u32[]{:S(2)}, u32[]{:S(2)}) %collective-permute-start.5) | collective-permute-done | bytes 393248 | tf_op jit(solution)/shard_map/ppermute | solution.py:424
  36.0 0.1 merge.12
  36.1 1.9 %collective-permute-start.9 = (bf16[2,384,128]{2,1,0:T(8,128)(2,1)S(1)}, bf16[2,384,128]{2,1,0:T(8,128)(2,1)S(1)}, u32[]{:S(2)}, u32[]{:S(2)}) collective-permute-start(bf16[2,384,128]{2,1,0:T(8,128)(2,1)S(1)} %get-tuple-element.60.order_ref), channel_id=1, source_target_pairs={{0,4},{1,5},{2,6},{3,7},{4,0},{5,1},{6,2},{7,3},{8,12},{9,13},{10,... | collective-permute-start | bytes 589832 | tf_op jit(solution)/shard_map/ppermute | solution.py:424
  38.0 1.5 %collective-permute-start.8 = (bf16[4,128,128]{2,1,0:T(8,128)(2,1)S(1)}, bf16[4,128,128]{2,1,0:T(8,128)(2,1)S(1)}, u32[]{:S(2)}, u32[]{:S(2)}) collective-permute-start(bf16[4,128,128]{2,1,0:T(8,128)(2,1)S(1)} %get-tuple-element.58.order_ref), channel_id=1, source_target_pairs={{0,2},{1,3},{2,0},{3,1},{4,6},{5,7},{6,4},{7,5},{8,10},{9,11},{10,... | collective-permute-start | bytes 393224 | tf_op jit(solution)/shard_map/ppermute | solution.py:424
  39.5 0.0 collective-permute-done.4.received_ref
  39.5 1.7 %collective-permute-done.11.received_ref = bf16[2,384,128]{2,1,0:T(8,128)(2,1)S(1)} collective-permute-done((bf16[2,384,128]{2,1,0:T(8,128)(2,1)S(1)}, bf16[2,384,128]{2,1,0:T(8,128)(2,1)S(1)}, u32[]{:S(2)}, u32[]{:S(2)}) %collective-permute-start.11) | collective-permute-done | bytes 196640 | tf_op jit(solution)/shard_map/ppermute | solution.py:424
  41.3 0.4 collective-permute-done.10.received_ref
  41.6 0.1 merge.15
  41.7 1.9 %collective-permute-start.13 = (bf16[2,256,128]{2,1,0:T(8,128)(2,1)S(1)}, bf16[2,256,128]{2,1,0:T(8,128)(2,1)S(1)}, u32[]{:S(2)}, u32[]{:S(2)}) collective-permute-start(bf16[2,256,128]{2,1,0:T(8,128)(2,1)S(1)} %get-tuple-element.68.order_ref), channel_id=1, source_target_pairs={{0,4},{1,5},{2,6},{3,7},{4,0},{5,1},{6,2},{7,3},{8,12},{9,13},{10,... | collective-permute-start | bytes 393224 | tf_op jit(solution)/shard_map/ppermute | solution.py:424
  43.6 2.6 %collective-permute-start.7 = (bf16[1,384,128]{2,1,0:T(8,128)(2,1)S(1)}, bf16[1,384,128]{2,1,0:T(8,128)(2,1)S(1)}, u32[]{:S(2)}, u32[]{:S(2)}) collective-permute-start(bf16[1,384,128]{2,1,0:T(8,128)(2,1)S(1)} %get-tuple-element.62.order_ref), channel_id=1, source_target_pairs={{0,8},{1,9},{2,10},{3,11},{4,12},{5,13},{6,14},{7,15},{8,0},{9,1},... | collective-permute-start | bytes 294920 | tf_op jit(solution)/shard_map/ppermute | solution.py:424
  46.2 0.0 collective-permute-done.9.received_ref
  46.2 1.8 %collective-permute-start.14 = (bf16[1,384,128]{2,1,0:T(8,128)(2,1)S(1)}, bf16[1,384,128]{2,1,0:T(8,128)(2,1)S(1)}, u32[]{:S(2)}, u32[]{:S(2)}) collective-permute-start(bf16[1,384,128]{2,1,0:T(8,128)(2,1)S(1)} %get-tuple-element.69.order_ref), channel_id=1, source_target_pairs={{0,8},{1,9},{2,10},{3,11},{4,12},{5,13},{6,14},{7,15},{8,0},{9,1},... | collective-permute-start | bytes 294920 | tf_op jit(solution)/shard_map/ppermute | solution.py:424
  48.0 0.0 collective-permute-done.8.received_ref
  48.1 2.5 %collective-permute-start.12 = (bf16[2,128,128]{2,1,0:T(8,128)(2,1)S(1)}, bf16[2,128,128]{2,1,0:T(8,128)(2,1)S(1)}, u32[]{:S(2)}, u32[]{:S(2)}) collective-permute-start(bf16[2,128,128]{2,1,0:T(8,128)(2,1)S(1)} %get-tuple-element.71.order_ref), channel_id=1, source_target_pairs={{0,4},{1,5},{2,6},{3,7},{4,0},{5,1},{6,2},{7,3},{8,12},{9,13},{10,... | collective-permute-start | bytes 196616 | tf_op jit(solution)/shard_map/ppermute | solution.py:424
  50.6 0.6 %collective-permute-start.16 = (bf16[1,384,128]{2,1,0:T(8,128)(2,1)S(1)}, bf16[1,384,128]{2,1,0:T(8,128)(2,1)S(1)}, u32[]{:S(2)}, u32[]{:S(2)}) collective-permute-start(bf16[1,384,128]{2,1,0:T(8,128)(2,1)S(1)} %get-tuple-element.67.order_ref), channel_id=1, source_target_pairs={{0,2},{1,3},{2,0},{3,1},{4,6},{5,7},{6,4},{7,5},{8,10},{9,11},{10,... | collective-permute-start | bytes 294920 | tf_op jit(solution)/shard_map/ppermute | solution.py:424
  51.2 0.0 collective-permute-done.13.received_ref
  51.2 0.1 collective-permute-start.15
  51.4 1.5 %collective-permute-done.12.received_ref = bf16[2,128,128]{2,1,0:T(8,128)(2,1)S(1)} collective-permute-done((bf16[2,128,128]{2,1,0:T(8,128)(2,1)S(1)}, bf16[2,128,128]{2,1,0:T(8,128)(2,1)S(1)}, u32[]{:S(2)}, u32[]{:S(2)}) %collective-permute-start.12) | collective-permute-done | bytes 65568 | tf_op jit(solution)/shard_map/ppermute | solution.py:424
  52.9 2.0 %collective-permute-start.17 = (bf16[1,128,128]{2,1,0:T(8,128)(2,1)S(1)}, bf16[1,128,128]{2,1,0:T(8,128)(2,1)S(1)}, u32[]{:S(2)}, u32[]{:S(2)}) collective-permute-start(bf16[1,128,128]{2,1,0:T(8,128)(2,1)S(1)} %get-tuple-element.74.order_ref), channel_id=1, source_target_pairs={{0,8},{1,9},{2,10},{3,11},{4,12},{5,13},{6,14},{7,15},{8,0},{9,1},... | collective-permute-start | bytes 98312 | tf_op jit(solution)/shard_map/ppermute | solution.py:424
  54.9 0.0 collective-permute-done.7.received_ref
  54.9 1.9 %collective-permute-done.14.received_ref = bf16[1,384,128]{2,1,0:T(8,128)(2,1)S(1)} collective-permute-done((bf16[1,384,128]{2,1,0:T(8,128)(2,1)S(1)}, bf16[1,384,128]{2,1,0:T(8,128)(2,1)S(1)}, u32[]{:S(2)}, u32[]{:S(2)}) %collective-permute-start.14) | collective-permute-done | bytes 98336 | tf_op jit(solution)/shard_map/ppermute | solution.py:424
  56.9 0.7 %collective-permute-done.15.received_ref = bf16[1,256,128]{2,1,0:T(8,128)(2,1)S(1)} collective-permute-done((bf16[1,256,128]{2,1,0:T(8,128)(2,1)S(1)}, bf16[1,256,128]{2,1,0:T(8,128)(2,1)S(1)}, u32[]{:S(2)}, u32[]{:S(2)}) %collective-permute-start.15) | collective-permute-done | bytes 65568 | tf_op jit(solution)/shard_map/ppermute | solution.py:424
  57.6 0.0 collective-permute-done.16.received_ref
  57.6 0.3 collective-permute-done.17.refs_5_
  57.9 0.8 %gather.1 = bf16[1,384,512]{2,1,0:T(8,128)(2,1)} custom-call(bf16[384,128]{1,0:T(8,128)(2,1)S(1)} %finish.4.order_ref.refs_0_, bf16[384,128]{1,0:T(8,128)(2,1)S(1)} %finish.5.order_ref.refs_1_, bf16[256,128]{1,0:T(8,128)(2,1)S(1)} %finish.6.order_ref.refs_2_, bf16[384,128]{1,0:T(8,128)(2,1)S(1)} %finish.7.refs_3_.refs_6_, ...), custom_call_target="tpu_custom_call" | custom-call | flops 1 | bytes 1 | tf_op jit(solution)/shard_map/gather/pallas_call | solution.py:395
  (10 shorter events, 0.3 us)
Async XLA Ops:
  0.1 7.6 %copy-start = (bf16[3,1,384,512]{3,2,1,0:T(8,128)(2,1)S(1)}, bf16[3,1,384,512]{3,2,1,0:T(8,128)(2,1)}, u32[]{:S(2)}) copy-start(bf16[3,1,384,512]{3,2,1,0:T(8,128)(2,1)} %head_in_ref.1) | copy-start | bytes 3538948
  0.1 7.6 %copy-start.1 = (f32[3,7,512]{2,1,0:T(8,128)S(1)}, f32[3,7,512]{2,1,0:T(8,128)}, u32[]{:S(2)}) copy-start(f32[3,7,512]{2,1,0:T(8,128)} %taps_ref.3) | copy-start | bytes 129028
  0.1 7.6 %copy-start.2 = (f32[16,512]{1,0:T(8,128)S(1)}, f32[16,512]{1,0:T(8,128)}, u32[]{:S(2)}) copy-start(f32[16,512]{1,0:T(8,128)} %decay_ref.3) | copy-start | bytes 98308
  0.1 7.6 %copy-start.4 = (f32[16,512]{1,0:T(8,128)S(1)}, f32[16,512]{1,0:T(8,128)}, u32[]{:S(2)}) copy-start(f32[16,512]{1,0:T(8,128)} %residues_ref.3) | copy-start | bytes 98308
  4.5 9.9 %collective-permute-start.2 = (bf16[8,512,512]{2,1,0:T(8,128)(2,1)S(1)}, bf16[8,512,512]{2,1,0:T(8,128)(2,1)S(1)}, u32[]{:S(2)}, u32[]{:S(2)}) collective-permute-start(bf16[8,512,512]{2,1,0:T(8,128)(2,1)S(1)} %get-tuple-element.48), channel_id=1, source_target_pairs={{0,1},{1,0},{2,3},{3,2},{4,5},{5,4},{6,7},{7,6},{8,9},{9,8},{10,11... | collective-permute-start | bytes 12582920 | tf_op jit(solution)/shard_map/ppermute | solution.py:424
  5.1 5.6 %collective-permute-start = (f32[40,512]{1,0:T(8,128)S(1)}, f32[40,512]{1,0:T(8,128)S(1)}, u32[]{:S(2)}, u32[]{:S(2)}) collective-permute-start(f32[40,512]{1,0:T(8,128)S(1)} %get-tuple-element.42), channel_id=1, source_target_pairs={{0,16},{16,0},{1,17},{17,1},{2,18},{18,2},{3,19},{19,3},{4,20},{20... | collective-permute-start | bytes 245768 | tf_op jit(solution)/shard_map/ppermute | solution.py:429
  7.7 3.0 %copy-start.3 = (f32[1,16,512]{2,1,0:T(8,128)S(1)}, f32[1,16,512]{2,1,0:T(8,128)}, u32[]{:S(2)}) copy-start(f32[1,16,512]{2,1,0:T(8,128)} %init_ref.1) | copy-start | bytes 98308
  12.6 1.8 %collective-permute-start.1 = (bf16[384,512]{1,0:T(8,128)(2,1)S(1)}, bf16[384,512]{1,0:T(8,128)(2,1)S(1)}, u32[]{:S(2)}, u32[]{:S(2)}) collective-permute-start(bf16[384,512]{1,0:T(8,128)(2,1)S(1)} %gated.1.own_ref), channel_id=1, source_target_pairs={{0,1},{1,0},{2,3},{3,2},{4,5},{5,4},{6,7},{7,6},{8,9},{9,8},{10,11... | collective-permute-start | bytes 1179656 | tf_op jit(solution)/shard_map/ppermute | solution.py:424
  15.6 12.0 %collective-permute-start.3 = (bf16[4,384,128]{2,1,0:T(8,128)(2,1)S(1)}, bf16[4,384,128]{2,1,0:T(8,128)(2,1)S(1)}, u32[]{:S(2)}, u32[]{:S(2)}) collective-permute-start(bf16[4,384,128]{2,1,0:T(8,128)(2,1)S(1)} %get-tuple-element.50.order_ref), channel_id=1, source_target_pairs={{0,2},{1,3},{2,0},{3,1},{4,6},{5,7},{6,4},{7,5},{8,10},{9,11},{10,... | collective-permute-start | bytes 1179656 | tf_op jit(solution)/shard_map/ppermute | solution.py:424
  18.9 11.8 %collective-permute-start.6 = (bf16[4,384,128]{2,1,0:T(8,128)(2,1)S(1)}, bf16[4,384,128]{2,1,0:T(8,128)(2,1)S(1)}, u32[]{:S(2)}, u32[]{:S(2)}) collective-permute-start(bf16[4,384,128]{2,1,0:T(8,128)(2,1)S(1)} %get-tuple-element.51.order_ref), channel_id=1, source_target_pairs={{0,4},{1,5},{2,6},{3,7},{4,0},{5,1},{6,2},{7,3},{8,12},{9,13},{10,... | collective-permute-start | bytes 1179656 | tf_op jit(solution)/shard_map/ppermute | solution.py:424
  22.1 13.9 %collective-permute-start.5 = (bf16[4,384,128]{2,1,0:T(8,128)(2,1)S(1)}, bf16[4,384,128]{2,1,0:T(8,128)(2,1)S(1)}, u32[]{:S(2)}, u32[]{:S(2)}) collective-permute-start(bf16[4,384,128]{2,1,0:T(8,128)(2,1)S(1)} %get-tuple-element.52.order_ref), channel_id=1, source_target_pairs={{0,2},{1,3},{2,0},{3,1},{4,6},{5,7},{6,4},{7,5},{8,10},{9,11},{10,... | collective-permute-start | bytes 1179656 | tf_op jit(solution)/shard_map/ppermute | solution.py:424
  24.0 17.7 %collective-permute-start.10 = (bf16[4,256,128]{2,1,0:T(8,128)(2,1)S(1)}, bf16[4,256,128]{2,1,0:T(8,128)(2,1)S(1)}, u32[]{:S(2)}, u32[]{:S(2)}) collective-permute-start(bf16[4,256,128]{2,1,0:T(8,128)(2,1)S(1)} %get-tuple-element.53.order_ref), channel_id=1, source_target_pairs={{0,2},{1,3},{2,0},{3,1},{4,6},{5,7},{6,4},{7,5},{8,10},{9,11},{10,... | collective-permute-start | bytes 786440 | tf_op jit(solution)/shard_map/ppermute | solution.py:424
  27.7 11.8 %collective-permute-start.4 = (bf16[2,384,128]{2,1,0:T(8,128)(2,1)S(1)}, bf16[2,384,128]{2,1,0:T(8,128)(2,1)S(1)}, u32[]{:S(2)}, u32[]{:S(2)}) collective-permute-start(bf16[2,384,128]{2,1,0:T(8,128)(2,1)S(1)} %get-tuple-element.55.order_ref), channel_id=1, source_target_pairs={{0,4},{1,5},{2,6},{3,7},{4,0},{5,1},{6,2},{7,3},{8,12},{9,13},{10,... | collective-permute-start | bytes 589832 | tf_op jit(solution)/shard_map/ppermute | solution.py:424
  30.8 10.4 %collective-permute-start.11 = (bf16[2,384,128]{2,1,0:T(8,128)(2,1)S(1)}, bf16[2,384,128]{2,1,0:T(8,128)(2,1)S(1)}, u32[]{:S(2)}, u32[]{:S(2)}) collective-permute-start(bf16[2,384,128]{2,1,0:T(8,128)(2,1)S(1)} %get-tuple-element.59.order_ref), channel_id=1, source_target_pairs={{0,8},{1,9},{2,10},{3,11},{4,12},{5,13},{6,14},{7,15},{8,0},{9,1},... | collective-permute-start | bytes 589832 | tf_op jit(solution)/shard_map/ppermute | solution.py:424
  36.1 10.1 %collective-permute-start.9 = (bf16[2,384,128]{2,1,0:T(8,128)(2,1)S(1)}, bf16[2,384,128]{2,1,0:T(8,128)(2,1)S(1)}, u32[]{:S(2)}, u32[]{:S(2)}) collective-permute-start(bf16[2,384,128]{2,1,0:T(8,128)(2,1)S(1)} %get-tuple-element.60.order_ref), channel_id=1, source_target_pairs={{0,4},{1,5},{2,6},{3,7},{4,0},{5,1},{6,2},{7,3},{8,12},{9,13},{10,... | collective-permute-start | bytes 589832 | tf_op jit(solution)/shard_map/ppermute | solution.py:424
  38.0 10.1 %collective-permute-start.8 = (bf16[4,128,128]{2,1,0:T(8,128)(2,1)S(1)}, bf16[4,128,128]{2,1,0:T(8,128)(2,1)S(1)}, u32[]{:S(2)}, u32[]{:S(2)}) collective-permute-start(bf16[4,128,128]{2,1,0:T(8,128)(2,1)S(1)} %get-tuple-element.58.order_ref), channel_id=1, source_target_pairs={{0,2},{1,3},{2,0},{3,1},{4,6},{5,7},{6,4},{7,5},{8,10},{9,11},{10,... | collective-permute-start | bytes 393224 | tf_op jit(solution)/shard_map/ppermute | solution.py:424
  41.7 9.5 %collective-permute-start.13 = (bf16[2,256,128]{2,1,0:T(8,128)(2,1)S(1)}, bf16[2,256,128]{2,1,0:T(8,128)(2,1)S(1)}, u32[]{:S(2)}, u32[]{:S(2)}) collective-permute-start(bf16[2,256,128]{2,1,0:T(8,128)(2,1)S(1)} %get-tuple-element.68.order_ref), channel_id=1, source_target_pairs={{0,4},{1,5},{2,6},{3,7},{4,0},{5,1},{6,2},{7,3},{8,12},{9,13},{10,... | collective-permute-start | bytes 393224 | tf_op jit(solution)/shard_map/ppermute | solution.py:424
  43.6 11.3 %collective-permute-start.7 = (bf16[1,384,128]{2,1,0:T(8,128)(2,1)S(1)}, bf16[1,384,128]{2,1,0:T(8,128)(2,1)S(1)}, u32[]{:S(2)}, u32[]{:S(2)}) collective-permute-start(bf16[1,384,128]{2,1,0:T(8,128)(2,1)S(1)} %get-tuple-element.62.order_ref), channel_id=1, source_target_pairs={{0,8},{1,9},{2,10},{3,11},{4,12},{5,13},{6,14},{7,15},{8,0},{9,1},... | collective-permute-start | bytes 294920 | tf_op jit(solution)/shard_map/ppermute | solution.py:424
  46.2 10.6 %collective-permute-start.14 = (bf16[1,384,128]{2,1,0:T(8,128)(2,1)S(1)}, bf16[1,384,128]{2,1,0:T(8,128)(2,1)S(1)}, u32[]{:S(2)}, u32[]{:S(2)}) collective-permute-start(bf16[1,384,128]{2,1,0:T(8,128)(2,1)S(1)} %get-tuple-element.69.order_ref), channel_id=1, source_target_pairs={{0,8},{1,9},{2,10},{3,11},{4,12},{5,13},{6,14},{7,15},{8,0},{9,1},... | collective-permute-start | bytes 294920 | tf_op jit(solution)/shard_map/ppermute | solution.py:424
  48.1 4.8 %collective-permute-start.12 = (bf16[2,128,128]{2,1,0:T(8,128)(2,1)S(1)}, bf16[2,128,128]{2,1,0:T(8,128)(2,1)S(1)}, u32[]{:S(2)}, u32[]{:S(2)}) collective-permute-start(bf16[2,128,128]{2,1,0:T(8,128)(2,1)S(1)} %get-tuple-element.71.order_ref), channel_id=1, source_target_pairs={{0,4},{1,5},{2,6},{3,7},{4,0},{5,1},{6,2},{7,3},{8,12},{9,13},{10,... | collective-permute-start | bytes 196616 | tf_op jit(solution)/shard_map/ppermute | solution.py:424
  50.6 7.0 %collective-permute-start.16 = (bf16[1,384,128]{2,1,0:T(8,128)(2,1)S(1)}, bf16[1,384,128]{2,1,0:T(8,128)(2,1)S(1)}, u32[]{:S(2)}, u32[]{:S(2)}) collective-permute-start(bf16[1,384,128]{2,1,0:T(8,128)(2,1)S(1)} %get-tuple-element.67.order_ref), channel_id=1, source_target_pairs={{0,2},{1,3},{2,0},{3,1},{4,6},{5,7},{6,4},{7,5},{8,10},{9,11},{10,... | collective-permute-start | bytes 294920 | tf_op jit(solution)/shard_map/ppermute | solution.py:424
  51.2 6.3 %collective-permute-start.15 = (bf16[1,256,128]{2,1,0:T(8,128)(2,1)S(1)}, bf16[1,256,128]{2,1,0:T(8,128)(2,1)S(1)}, u32[]{:S(2)}, u32[]{:S(2)}) collective-permute-start(bf16[1,256,128]{2,1,0:T(8,128)(2,1)S(1)} %get-tuple-element.73.order_ref), channel_id=1, source_target_pairs={{0,8},{1,9},{2,10},{3,11},{4,12},{5,13},{6,14},{7,15},{8,0},{9,1},... | collective-permute-start | bytes 196616 | tf_op jit(solution)/shard_map/ppermute | solution.py:424
  52.9 5.0 %collective-permute-start.17 = (bf16[1,128,128]{2,1,0:T(8,128)(2,1)S(1)}, bf16[1,128,128]{2,1,0:T(8,128)(2,1)S(1)}, u32[]{:S(2)}, u32[]{:S(2)}) collective-permute-start(bf16[1,128,128]{2,1,0:T(8,128)(2,1)S(1)} %get-tuple-element.74.order_ref), channel_id=1, source_target_pairs={{0,8},{1,9},{2,10},{3,11},{4,12},{5,13},{6,14},{7,15},{8,0},{9,1},... | collective-permute-start | bytes 98312 | tf_op jit(solution)/shard_map/ppermute | solution.py:424

commit v4 on v3

--- a/solution.py
+++ b/solution.py
@@ -45,8 +45,6 @@
     for part in range(parts):
         column = pl.multiple_of((2 * part + side) * width, LANES)
         copies.append(pltpu.make_async_copy(weight_hbm.at[:, pl.ds(column, width)], ref.at[part], sems.at[part]))
-    for copy in copies:
-        copy.start()
     return copies
 
 
@@ -78,6 +76,9 @@
     for tile in range(tiles):
         lanes = slice(tile * LANES, (tile + 1) * LANES)
         loads[tile].wait()
+        if tile < 2:
+            for copy in copies[tile::2]:
+                copy.start()
         for s in range(2):
             wide_ref[s, 0:EDGE, :] = jnp.zeros((EDGE, LANES), F32)
             wide_ref[s, EDGE : EDGE + length, :] = streams_ref[tile, s].astype(F32)
@@ -137,6 +138,8 @@
     tiles = channels // LANES
     seg_len, turn = segments(length)
     copies = weight_columns(weight_hbm, mine_ref, where_ref[1], weight_sems)
+    for copy in copies:
+        copy.start()
     sublane = lax.broadcasted_iota(jnp.int32, (SEGS, LANES), 0)
     for tile in range(tiles):
         lanes = slice(tile * LANES, (tile + 1) * LANES)

time: 58.8 us -> 58.3 us (level)
  no operation moved by 1% of the time
where the time goes in v4:
time: 58.3 us; the launch traced here: 58.1 us
  starting transfers between devices  28.2 us (48%)
  Pallas kernels  17.6 us (30%)
  waiting for transfers between devices  12 us (21%)
    ppermute x17, starting transfers between devices, across(): return lax.ppermute(x, 'tp', [(i, i ^ 1 << bit) for i in range(count)])  25.6 us
    ppermute x17, waiting for transfers between devices, across(): return lax.ppermute(x, 'tp', [(i, i ^ 1 << bit) for i in range(count)])  11.9 us
    pallas_call x4, Pallas kernels, project(): pl.pallas_call(functools.partial(project_kernel, part), out_shape=(jax.Sh...  5.33 us
    pallas_call x1, Pallas kernels, per_device(): pl.pallas_call(driven_kernel, out_shape=(jax.ShapeDtypeStruct(split, F32)...  3.93 us
    pallas_call x1, Pallas kernels, per_device(): pl.pallas_call(response_kernel, out_shape=(jax.ShapeDtypeStruct(split, F3...  2.89 us
    ppermute x1, starting transfers between devices, after(): return lax.ppermute(x, axis, [(i, (i + 1) % count) for i in range(count)])  2.59 us
    pallas_call x1, Pallas kernels, per_device(): pl.pallas_call(gated_kernel, out_shape=jax.ShapeDtypeStruct((length, chan...  1.93 us
  transfers between devices with their start and end apart: 18, of which 11 were waited for; matrix products, arithmetic and copies ran while one was open for 0% of the time, Pallas kernels for 20%

profile of v4, /device:TPU:0, one launch (start us, length us, event | category | flops | bytes accessed | tf_op | source)
XLA Modules:
  0.0 58.1 jit_solution(13023816574689976050)
XLA Ops:
  0.0 0.1 pad_add_fusion.where_ref
  0.1 0.0 copy-start
  0.1 0.0 copy-start.1
  0.1 0.0 copy-start.2
  0.1 0.0 copy-start.4
  0.1 3.9 %driven.1 = (f32[4,49,8,128]{3,2,1,0:T(8,128)S(1)}, f32[4,16,8,128]{3,2,1,0:T(8,128)S(1)}, f32[40,512]{1,0:T(8,128)S(1)}, bf16[8,512,512]{2,1,0:T(8,128)(2,1)S(1)}) custom-call(s32[3]{0:T(128)S(1)} %pad_add_fusion.where_ref, bf16[3,1,384,512]{3,2,1,0:T(8,128)(2,1)} %head_in_ref.1, f32[3,7,512]{2,1,0:T(8,128)} %taps_ref.3, f32[16,512]{1,0:T(8,128)} %decay_ref.3, ...), custom_call_target="tpu_custom_call" | custom-call | flops 1 | bytes 1 | tf_op jit(solution)/shard_map/driven/pallas_call | solution.py:471
  4.0 0.5 collective-permute-start.2
  4.5 2.6 %collective-permute-start = (f32[40,512]{1,0:T(8,128)S(1)}, f32[40,512]{1,0:T(8,128)S(1)}, u32[]{:S(2)}, u32[]{:S(2)}) collective-permute-start(f32[40,512]{1,0:T(8,128)S(1)} %get-tuple-element.42), channel_id=1, source_target_pairs={{0,16},{16,0},{1,17},{17,1},{2,18},{18,2},{3,19},{19,3},{4,20},{20... | collective-permute-start | bytes 245768 | tf_op jit(solution)/shard_map/ppermute | solution.py:432
  7.1 0.0 copy-done
  7.1 0.0 copy-done.1
  7.1 0.0 copy-done.2
  7.2 0.0 copy-done.4
  7.2 0.0 copy-start.3
  7.2 2.9 %response.1 = (f32[4,49,8,128]{3,2,1,0:T(8,128)S(1)}, f32[4,49,8,128]{3,2,1,0:T(8,128)S(1)}, bf16[8,512,512]{2,1,0:T(8,128)(2,1)S(1)}) custom-call(s32[3]{0:T(128)S(1)} %pad_add_fusion.where_ref, bf16[3,1,384,512]{3,2,1,0:T(8,128)(2,1)S(1)} %copy-done, f32[3,7,512]{2,1,0:T(8,128)S(1)} %copy-done.1, f32[16,512]{1,0:T(8,128)S(1)} %copy-done.2, ...), custom_call_target="tpu_custom_call" | custom-call | flops 1 | bytes 1 | tf_op jit(solution)/shard_map/response/pallas_call | solution.py:497
  10.1 0.1 collective-permute-done.message_ref
  10.2 0.0 copy-done.3
  10.2 1.9 %gated.1.own_ref = bf16[384,512]{1,0:T(8,128)(2,1)S(1)} custom-call(s32[3]{0:T(128)S(1)} %pad_add_fusion.where_ref, f32[40,512]{1,0:T(8,128)S(1)} %collective-permute-done.message_ref, bf16[3,1,384,512]{3,2,1,0:T(8,128)(2,1)S(1)} %copy-done, f32[3,7,512]{2,1,0:T(8,128)S(1)} %copy-done.1, f32[16,512]{1,0:T(8,128)S(1)} %copy-done.2, f32[16,512]{1,0:T(8,128)S(1)} %copy-done.4, ...), custom_call_target="tpu_custom_call" | custom-call | flops 1 | bytes 1 | tf_op jit(solution)/shard_map/gated/pallas_call | solution.py:513
  12.1 0.1 collective-permute-start.1
  12.3 1.1 %project_own.1.sum_ref = f32[4,384,256]{2,1,0:T(8,128)S(1)} custom-call(s32[3]{0:T(128)S(1)} %pad_add_fusion.where_ref, bf16[384,512]{1,0:T(8,128)(2,1)S(1)} %gated.1.own_ref, bf16[8,512,512]{2,1,0:T(8,128)(2,1)S(1)} %get-tuple-element.47.mine_ref), custom_call_target="tpu_custom_call" | custom-call | flops 1 | bytes 1 | tf_op jit(solution)/shard_map/project_own/pallas_call | solution.py:346
  13.4 0.5 collective-permute-done.1.other_ref
  13.9 0.0 collective-permute-done.2.theirs_ref
  13.9 1.1 %project_other.1 = (bf16[4,384,128]{2,1,0:T(8,128)(2,1)S(1)}, f32[4,384,128]{2,1,0:T(8,128)S(1)}) custom-call(s32[3]{0:T(128)S(1)} %pad_add_fusion.where_ref, f32[4,384,256]{2,1,0:T(8,128)S(1)} %project_own.1.sum_ref, bf16[384,512]{1,0:T(8,128)(2,1)S(1)} %collective-permute-done.1.other_ref, bf16[8,512,512]{2,1,0:T(8,128)(2,1)S(1)} %collective-permute-done.2.theirs_ref), custom_call_target="tpu_custom_call" | custom-call | flops 1 | bytes 1 | tf_op jit(solution)/shard_map/project_other/pallas_call | solution.py:360
  15.1 1.8 %collective-permute-start.3 = (bf16[4,384,128]{2,1,0:T(8,128)(2,1)S(1)}, bf16[4,384,128]{2,1,0:T(8,128)(2,1)S(1)}, u32[]{:S(2)}, u32[]{:S(2)}) collective-permute-start(bf16[4,384,128]{2,1,0:T(8,128)(2,1)S(1)} %get-tuple-element.50.order_ref), channel_id=1, source_target_pairs={{0,2},{1,3},{2,0},{3,1},{4,6},{5,7},{6,4},{7,5},{8,10},{9,11},{10,... | collective-permute-start | bytes 1179656 | tf_op jit(solution)/shard_map/ppermute | solution.py:427
  16.9 1.5 %project.4 = (bf16[4,384,128]{2,1,0:T(8,128)(2,1)S(1)}, f32[4,384,128]{2,1,0:T(8,128)S(1)}) custom-call(s32[3]{0:T(128)S(1)} %pad_add_fusion.where_ref, bf16[384,512]{1,0:T(8,128)(2,1)S(1)} %gated.1.own_ref, bf16[384,512]{1,0:T(8,128)(2,1)S(1)} %collective-permute-done.1.other_ref, bf16[8,512,512]{2,1,0:T(8,128)(2,1)S(1)} %get-tuple-element.47.mine_ref, ...), custom_call_target="tpu_custom_call" | custom-call | flops 1 | bytes 1 | tf_op jit(solution)/shard_map/project/pallas_call | solution.py:333
  18.4 1.6 %collective-permute-start.6 = (bf16[4,384,128]{2,1,0:T(8,128)(2,1)S(1)}, bf16[4,384,128]{2,1,0:T(8,128)(2,1)S(1)}, u32[]{:S(2)}, u32[]{:S(2)}) collective-permute-start(bf16[4,384,128]{2,1,0:T(8,128)(2,1)S(1)} %get-tuple-element.51.order_ref), channel_id=1, source_target_pairs={{0,4},{1,5},{2,6},{3,7},{4,0},{5,1},{6,2},{7,3},{8,12},{9,13},{10,... | collective-permute-start | bytes 1179656 | tf_op jit(solution)/shard_map/ppermute | solution.py:427
  20.0 1.5 %project.5 = (bf16[4,384,128]{2,1,0:T(8,128)(2,1)S(1)}, f32[4,384,128]{2,1,0:T(8,128)S(1)}) custom-call(s32[3]{0:T(128)S(1)} %pad_add_fusion.where_ref, bf16[384,512]{1,0:T(8,128)(2,1)S(1)} %gated.1.own_ref, bf16[384,512]{1,0:T(8,128)(2,1)S(1)} %collective-permute-done.1.other_ref, bf16[8,512,512]{2,1,0:T(8,128)(2,1)S(1)} %get-tuple-element.47.mine_ref, ...), custom_call_target="tpu_custom_call" | custom-call | flops 1 | bytes 1 | tf_op jit(solution)/shard_map/project/pallas_call | solution.py:333
  21.6 0.6 %collective-permute-start.5 = (bf16[4,384,128]{2,1,0:T(8,128)(2,1)S(1)}, bf16[4,384,128]{2,1,0:T(8,128)(2,1)S(1)}, u32[]{:S(2)}, u32[]{:S(2)}) collective-permute-start(bf16[4,384,128]{2,1,0:T(8,128)(2,1)S(1)} %get-tuple-element.52.order_ref), channel_id=1, source_target_pairs={{0,2},{1,3},{2,0},{3,1},{4,6},{5,7},{6,4},{7,5},{8,10},{9,11},{10,... | collective-permute-start | bytes 1179656 | tf_op jit(solution)/shard_map/ppermute | solution.py:427
  22.2 1.3 %project.6 = (bf16[4,256,128]{2,1,0:T(8,128)(2,1)S(1)}, f32[4,256,128]{2,1,0:T(8,128)S(1)}) custom-call(s32[3]{0:T(128)S(1)} %pad_add_fusion.where_ref, bf16[384,512]{1,0:T(8,128)(2,1)S(1)} %gated.1.own_ref, bf16[384,512]{1,0:T(8,128)(2,1)S(1)} %collective-permute-done.1.other_ref, bf16[8,512,512]{2,1,0:T(8,128)(2,1)S(1)} %get-tuple-element.47.mine_ref, ...), custom_call_target="tpu_custom_call" | custom-call | flops 1 | bytes 1 | tf_op jit(solution)/shard_map/project/pallas_call | solution.py:333
  23.4 1.6 %collective-permute-start.10 = (bf16[4,256,128]{2,1,0:T(8,128)(2,1)S(1)}, bf16[4,256,128]{2,1,0:T(8,128)(2,1)S(1)}, u32[]{:S(2)}, u32[]{:S(2)}) collective-permute-start(bf16[4,256,128]{2,1,0:T(8,128)(2,1)S(1)} %get-tuple-element.53.order_ref), channel_id=1, source_target_pairs={{0,2},{1,3},{2,0},{3,1},{4,6},{5,7},{6,4},{7,5},{8,10},{9,11},{10,... | collective-permute-start | bytes 786440 | tf_op jit(solution)/shard_map/ppermute | solution.py:427
  25.0 2.1 %collective-permute-done.3.received_ref = bf16[4,384,128]{2,1,0:T(8,128)(2,1)S(1)} collective-permute-done((bf16[4,384,128]{2,1,0:T(8,128)(2,1)S(1)}, bf16[4,384,128]{2,1,0:T(8,128)(2,1)S(1)}, u32[]{:S(2)}, u32[]{:S(2)}) %collective-permute-start.3) | collective-permute-done | bytes 393248 | tf_op jit(solution)/shard_map/ppermute | solution.py:427
  27.1 0.1 merge.10
  27.1 1.9 %collective-permute-start.4 = (bf16[2,384,128]{2,1,0:T(8,128)(2,1)S(1)}, bf16[2,384,128]{2,1,0:T(8,128)(2,1)S(1)}, u32[]{:S(2)}, u32[]{:S(2)}) collective-permute-start(bf16[2,384,128]{2,1,0:T(8,128)(2,1)S(1)} %get-tuple-element.55.order_ref), channel_id=1, source_target_pairs={{0,4},{1,5},{2,6},{3,7},{4,0},{5,1},{6,2},{7,3},{8,12},{9,13},{10,... | collective-permute-start | bytes 589832 | tf_op jit(solution)/shard_map/ppermute | solution.py:427
  29.0 1.0 %project.7 = (bf16[4,128,128]{2,1,0:T(8,128)(2,1)S(1)}, f32[4,128,128]{2,1,0:T(8,128)S(1)}) custom-call(s32[3]{0:T(128)S(1)} %pad_add_fusion.where_ref, bf16[384,512]{1,0:T(8,128)(2,1)S(1)} %gated.1.own_ref, bf16[384,512]{1,0:T(8,128)(2,1)S(1)} %collective-permute-done.1.other_ref, bf16[8,512,512]{2,1,0:T(8,128)(2,1)S(1)} %get-tuple-element.47.mine_ref, ...), custom_call_target="tpu_custom_call" | custom-call | flops 1 | bytes 1 | tf_op jit(solution)/shard_map/project/pallas_call | solution.py:333
  30.0 0.2 collective-permute-done.6.received_ref
  30.2 0.1 merge.11
  30.3 2.5 %collective-permute-start.11 = (bf16[2,384,128]{2,1,0:T(8,128)(2,1)S(1)}, bf16[2,384,128]{2,1,0:T(8,128)(2,1)S(1)}, u32[]{:S(2)}, u32[]{:S(2)}) collective-permute-start(bf16[2,384,128]{2,1,0:T(8,128)(2,1)S(1)} %get-tuple-element.59.order_ref), channel_id=1, source_target_pairs={{0,8},{1,9},{2,10},{3,11},{4,12},{5,13},{6,14},{7,15},{8,0},{9,1},... | collective-permute-start | bytes 589832 | tf_op jit(solution)/shard_map/ppermute | solution.py:427
  32.8 2.7 %collective-permute-done.5.received_ref = bf16[4,384,128]{2,1,0:T(8,128)(2,1)S(1)} collective-permute-done((bf16[4,384,128]{2,1,0:T(8,128)(2,1)S(1)}, bf16[4,384,128]{2,1,0:T(8,128)(2,1)S(1)}, u32[]{:S(2)}, u32[]{:S(2)}) %collective-permute-start.5) | collective-permute-done | bytes 393248 | tf_op jit(solution)/shard_map/ppermute | solution.py:427
  35.5 0.1 merge.12
  35.6 1.9 %collective-permute-start.9 = (bf16[2,384,128]{2,1,0:T(8,128)(2,1)S(1)}, bf16[2,384,128]{2,1,0:T(8,128)(2,1)S(1)}, u32[]{:S(2)}, u32[]{:S(2)}) collective-permute-start(bf16[2,384,128]{2,1,0:T(8,128)(2,1)S(1)} %get-tuple-element.60.order_ref), channel_id=1, source_target_pairs={{0,4},{1,5},{2,6},{3,7},{4,0},{5,1},{6,2},{7,3},{8,12},{9,13},{10,... | collective-permute-start | bytes 589832 | tf_op jit(solution)/shard_map/ppermute | solution.py:427
  37.5 1.5 %collective-permute-start.8 = (bf16[4,128,128]{2,1,0:T(8,128)(2,1)S(1)}, bf16[4,128,128]{2,1,0:T(8,128)(2,1)S(1)}, u32[]{:S(2)}, u32[]{:S(2)}) collective-permute-start(bf16[4,128,128]{2,1,0:T(8,128)(2,1)S(1)} %get-tuple-element.58.order_ref), channel_id=1, source_target_pairs={{0,2},{1,3},{2,0},{3,1},{4,6},{5,7},{6,4},{7,5},{8,10},{9,11},{10,... | collective-permute-start | bytes 393224 | tf_op jit(solution)/shard_map/ppermute | solution.py:427
  38.9 0.0 collective-permute-done.4.received_ref
  39.0 1.7 %collective-permute-done.11.received_ref = bf16[2,384,128]{2,1,0:T(8,128)(2,1)S(1)} collective-permute-done((bf16[2,384,128]{2,1,0:T(8,128)(2,1)S(1)}, bf16[2,384,128]{2,1,0:T(8,128)(2,1)S(1)}, u32[]{:S(2)}, u32[]{:S(2)}) %collective-permute-start.11) | collective-permute-done | bytes 196640 | tf_op jit(solution)/shard_map/ppermute | solution.py:427
  40.8 0.3 collective-permute-done.10.received_ref
  41.1 0.1 merge.15
  41.2 1.9 %collective-permute-start.13 = (bf16[2,256,128]{2,1,0:T(8,128)(2,1)S(1)}, bf16[2,256,128]{2,1,0:T(8,128)(2,1)S(1)}, u32[]{:S(2)}, u32[]{:S(2)}) collective-permute-start(bf16[2,256,128]{2,1,0:T(8,128)(2,1)S(1)} %get-tuple-element.68.order_ref), channel_id=1, source_target_pairs={{0,4},{1,5},{2,6},{3,7},{4,0},{5,1},{6,2},{7,3},{8,12},{9,13},{10,... | collective-permute-start | bytes 393224 | tf_op jit(solution)/shard_map/ppermute | solution.py:427
  43.1 2.6 %collective-permute-start.7 = (bf16[1,384,128]{2,1,0:T(8,128)(2,1)S(1)}, bf16[1,384,128]{2,1,0:T(8,128)(2,1)S(1)}, u32[]{:S(2)}, u32[]{:S(2)}) collective-permute-start(bf16[1,384,128]{2,1,0:T(8,128)(2,1)S(1)} %get-tuple-element.62.order_ref), channel_id=1, source_target_pairs={{0,8},{1,9},{2,10},{3,11},{4,12},{5,13},{6,14},{7,15},{8,0},{9,1},... | collective-permute-start | bytes 294920 | tf_op jit(solution)/shard_map/ppermute | solution.py:427
  45.7 0.0 collective-permute-done.9.received_ref
  45.7 1.8 %collective-permute-start.14 = (bf16[1,384,128]{2,1,0:T(8,128)(2,1)S(1)}, bf16[1,384,128]{2,1,0:T(8,128)(2,1)S(1)}, u32[]{:S(2)}, u32[]{:S(2)}) collective-permute-start(bf16[1,384,128]{2,1,0:T(8,128)(2,1)S(1)} %get-tuple-element.69.order_ref), channel_id=1, source_target_pairs={{0,8},{1,9},{2,10},{3,11},{4,12},{5,13},{6,14},{7,15},{8,0},{9,1},... | collective-permute-start | bytes 294920 | tf_op jit(solution)/shard_map/ppermute | solution.py:427
  47.5 0.0 collective-permute-done.8.received_ref
  47.6 2.5 %collective-permute-start.12 = (bf16[2,128,128]{2,1,0:T(8,128)(2,1)S(1)}, bf16[2,128,128]{2,1,0:T(8,128)(2,1)S(1)}, u32[]{:S(2)}, u32[]{:S(2)}) collective-permute-start(bf16[2,128,128]{2,1,0:T(8,128)(2,1)S(1)} %get-tuple-element.71.order_ref), channel_id=1, source_target_pairs={{0,4},{1,5},{2,6},{3,7},{4,0},{5,1},{6,2},{7,3},{8,12},{9,13},{10,... | collective-permute-start | bytes 196616 | tf_op jit(solution)/shard_map/ppermute | solution.py:427
  50.1 0.6 collective-permute-start.16
  50.7 0.0 collective-permute-done.13.received_ref
  50.7 0.2 collective-permute-start.15
  50.9 1.4 %collective-permute-done.12.received_ref = bf16[2,128,128]{2,1,0:T(8,128)(2,1)S(1)} collective-permute-done((bf16[2,128,128]{2,1,0:T(8,128)(2,1)S(1)}, bf16[2,128,128]{2,1,0:T(8,128)(2,1)S(1)}, u32[]{:S(2)}, u32[]{:S(2)}) %collective-permute-start.12) | collective-permute-done | bytes 65568 | tf_op jit(solution)/shard_map/ppermute | solution.py:427
  52.4 2.0 %collective-permute-start.17 = (bf16[1,128,128]{2,1,0:T(8,128)(2,1)S(1)}, bf16[1,128,128]{2,1,0:T(8,128)(2,1)S(1)}, u32[]{:S(2)}, u32[]{:S(2)}) collective-permute-start(bf16[1,128,128]{2,1,0:T(8,128)(2,1)S(1)} %get-tuple-element.74.order_ref), channel_id=1, source_target_pairs={{0,8},{1,9},{2,10},{3,11},{4,12},{5,13},{6,14},{7,15},{8,0},{9,1},... | collective-permute-start | bytes 98312 | tf_op jit(solution)/shard_map/ppermute | solution.py:427
  54.4 0.0 collective-permute-done.7.received_ref
  54.4 1.9 %collective-permute-done.14.received_ref = bf16[1,384,128]{2,1,0:T(8,128)(2,1)S(1)} collective-permute-done((bf16[1,384,128]{2,1,0:T(8,128)(2,1)S(1)}, bf16[1,384,128]{2,1,0:T(8,128)(2,1)S(1)}, u32[]{:S(2)}, u32[]{:S(2)}) %collective-permute-start.14) | collective-permute-done | bytes 98336 | tf_op jit(solution)/shard_map/ppermute | solution.py:427
  56.3 0.7 %collective-permute-done.15.received_ref = bf16[1,256,128]{2,1,0:T(8,128)(2,1)S(1)} collective-permute-done((bf16[1,256,128]{2,1,0:T(8,128)(2,1)S(1)}, bf16[1,256,128]{2,1,0:T(8,128)(2,1)S(1)}, u32[]{:S(2)}, u32[]{:S(2)}) %collective-permute-start.15) | collective-permute-done | bytes 65568 | tf_op jit(solution)/shard_map/ppermute | solution.py:427
  57.0 0.0 collective-permute-done.16.received_ref
  57.1 0.3 collective-permute-done.17.refs_5_
  57.4 0.8 %gather.1 = bf16[1,384,512]{2,1,0:T(8,128)(2,1)} custom-call(bf16[384,128]{1,0:T(8,128)(2,1)S(1)} %finish.4.order_ref.refs_0_, bf16[384,128]{1,0:T(8,128)(2,1)S(1)} %finish.5.order_ref.refs_1_, bf16[256,128]{1,0:T(8,128)(2,1)S(1)} %finish.6.order_ref.refs_2_, bf16[384,128]{1,0:T(8,128)(2,1)S(1)} %finish.7.refs_3_.refs_6_, ...), custom_call_target="tpu_custom_call" | custom-call | flops 1 | bytes 1 | tf_op jit(solution)/shard_map/gather/pallas_call | solution.py:398
  (10 shorter events, 0.3 us)
Async XLA Ops:
  0.1 7.1 %copy-start = (bf16[3,1,384,512]{3,2,1,0:T(8,128)(2,1)S(1)}, bf16[3,1,384,512]{3,2,1,0:T(8,128)(2,1)}, u32[]{:S(2)}) copy-start(bf16[3,1,384,512]{3,2,1,0:T(8,128)(2,1)} %head_in_ref.1) | copy-start | bytes 3538948
  0.1 7.1 %copy-start.1 = (f32[3,7,512]{2,1,0:T(8,128)S(1)}, f32[3,7,512]{2,1,0:T(8,128)}, u32[]{:S(2)}) copy-start(f32[3,7,512]{2,1,0:T(8,128)} %taps_ref.3) | copy-start | bytes 129028
  0.1 7.1 %copy-start.2 = (f32[16,512]{1,0:T(8,128)S(1)}, f32[16,512]{1,0:T(8,128)}, u32[]{:S(2)}) copy-start(f32[16,512]{1,0:T(8,128)} %decay_ref.3) | copy-start | bytes 98308
  0.1 7.1 %copy-start.4 = (f32[16,512]{1,0:T(8,128)S(1)}, f32[16,512]{1,0:T(8,128)}, u32[]{:S(2)}) copy-start(f32[16,512]{1,0:T(8,128)} %residues_ref.3) | copy-start | bytes 98308
  4.0 9.9 %collective-permute-start.2 = (bf16[8,512,512]{2,1,0:T(8,128)(2,1)S(1)}, bf16[8,512,512]{2,1,0:T(8,128)(2,1)S(1)}, u32[]{:S(2)}, u32[]{:S(2)}) collective-permute-start(bf16[8,512,512]{2,1,0:T(8,128)(2,1)S(1)} %get-tuple-element.48), channel_id=1, source_target_pairs={{0,1},{1,0},{2,3},{3,2},{4,5},{5,4},{6,7},{7,6},{8,9},{9,8},{10,11... | collective-permute-start | bytes 12582920 | tf_op jit(solution)/shard_map/ppermute | solution.py:427
  4.5 5.6 %collective-permute-start = (f32[40,512]{1,0:T(8,128)S(1)}, f32[40,512]{1,0:T(8,128)S(1)}, u32[]{:S(2)}, u32[]{:S(2)}) collective-permute-start(f32[40,512]{1,0:T(8,128)S(1)} %get-tuple-element.42), channel_id=1, source_target_pairs={{0,16},{16,0},{1,17},{17,1},{2,18},{18,2},{3,19},{19,3},{4,20},{20... | collective-permute-start | bytes 245768 | tf_op jit(solution)/shard_map/ppermute | solution.py:432
  7.2 3.0 %copy-start.3 = (f32[1,16,512]{2,1,0:T(8,128)S(1)}, f32[1,16,512]{2,1,0:T(8,128)}, u32[]{:S(2)}) copy-start(f32[1,16,512]{2,1,0:T(8,128)} %init_ref.1) | copy-start | bytes 98308
  12.1 1.8 %collective-permute-start.1 = (bf16[384,512]{1,0:T(8,128)(2,1)S(1)}, bf16[384,512]{1,0:T(8,128)(2,1)S(1)}, u32[]{:S(2)}, u32[]{:S(2)}) collective-permute-start(bf16[384,512]{1,0:T(8,128)(2,1)S(1)} %gated.1.own_ref), channel_id=1, source_target_pairs={{0,1},{1,0},{2,3},{3,2},{4,5},{5,4},{6,7},{7,6},{8,9},{9,8},{10,11... | collective-permute-start | bytes 1179656 | tf_op jit(solution)/shard_map/ppermute | solution.py:427
  15.1 12.0 %collective-permute-start.3 = (bf16[4,384,128]{2,1,0:T(8,128)(2,1)S(1)}, bf16[4,384,128]{2,1,0:T(8,128)(2,1)S(1)}, u32[]{:S(2)}, u32[]{:S(2)}) collective-permute-start(bf16[4,384,128]{2,1,0:T(8,128)(2,1)S(1)} %get-tuple-element.50.order_ref), channel_id=1, source_target_pairs={{0,2},{1,3},{2,0},{3,1},{4,6},{5,7},{6,4},{7,5},{8,10},{9,11},{10,... | collective-permute-start | bytes 1179656 | tf_op jit(solution)/shard_map/ppermute | solution.py:427
  18.4 11.8 %collective-permute-start.6 = (bf16[4,384,128]{2,1,0:T(8,128)(2,1)S(1)}, bf16[4,384,128]{2,1,0:T(8,128)(2,1)S(1)}, u32[]{:S(2)}, u32[]{:S(2)}) collective-permute-start(bf16[4,384,128]{2,1,0:T(8,128)(2,1)S(1)} %get-tuple-element.51.order_ref), channel_id=1, source_target_pairs={{0,4},{1,5},{2,6},{3,7},{4,0},{5,1},{6,2},{7,3},{8,12},{9,13},{10,... | collective-permute-start | bytes 1179656 | tf_op jit(solution)/shard_map/ppermute | solution.py:427
  21.6 13.9 %collective-permute-start.5 = (bf16[4,384,128]{2,1,0:T(8,128)(2,1)S(1)}, bf16[4,384,128]{2,1,0:T(8,128)(2,1)S(1)}, u32[]{:S(2)}, u32[]{:S(2)}) collective-permute-start(bf16[4,384,128]{2,1,0:T(8,128)(2,1)S(1)} %get-tuple-element.52.order_ref), channel_id=1, source_target_pairs={{0,2},{1,3},{2,0},{3,1},{4,6},{5,7},{6,4},{7,5},{8,10},{9,11},{10,... | collective-permute-start | bytes 1179656 | tf_op jit(solution)/shard_map/ppermute | solution.py:427
  23.4 17.7 %collective-permute-start.10 = (bf16[4,256,128]{2,1,0:T(8,128)(2,1)S(1)}, bf16[4,256,128]{2,1,0:T(8,128)(2,1)S(1)}, u32[]{:S(2)}, u32[]{:S(2)}) collective-permute-start(bf16[4,256,128]{2,1,0:T(8,128)(2,1)S(1)} %get-tuple-element.53.order_ref), channel_id=1, source_target_pairs={{0,2},{1,3},{2,0},{3,1},{4,6},{5,7},{6,4},{7,5},{8,10},{9,11},{10,... | collective-permute-start | bytes 786440 | tf_op jit(solution)/shard_map/ppermute | solution.py:427
  27.1 11.8 %collective-permute-start.4 = (bf16[2,384,128]{2,1,0:T(8,128)(2,1)S(1)}, bf16[2,384,128]{2,1,0:T(8,128)(2,1)S(1)}, u32[]{:S(2)}, u32[]{:S(2)}) collective-permute-start(bf16[2,384,128]{2,1,0:T(8,128)(2,1)S(1)} %get-tuple-element.55.order_ref), channel_id=1, source_target_pairs={{0,4},{1,5},{2,6},{3,7},{4,0},{5,1},{6,2},{7,3},{8,12},{9,13},{10,... | collective-permute-start | bytes 589832 | tf_op jit(solution)/shard_map/ppermute | solution.py:427
  30.3 10.5 %collective-permute-start.11 = (bf16[2,384,128]{2,1,0:T(8,128)(2,1)S(1)}, bf16[2,384,128]{2,1,0:T(8,128)(2,1)S(1)}, u32[]{:S(2)}, u32[]{:S(2)}) collective-permute-start(bf16[2,384,128]{2,1,0:T(8,128)(2,1)S(1)} %get-tuple-element.59.order_ref), channel_id=1, source_target_pairs={{0,8},{1,9},{2,10},{3,11},{4,12},{5,13},{6,14},{7,15},{8,0},{9,1},... | collective-permute-start | bytes 589832 | tf_op jit(solution)/shard_map/ppermute | solution.py:427
  35.6 10.1 %collective-permute-start.9 = (bf16[2,384,128]{2,1,0:T(8,128)(2,1)S(1)}, bf16[2,384,128]{2,1,0:T(8,128)(2,1)S(1)}, u32[]{:S(2)}, u32[]{:S(2)}) collective-permute-start(bf16[2,384,128]{2,1,0:T(8,128)(2,1)S(1)} %get-tuple-element.60.order_ref), channel_id=1, source_target_pairs={{0,4},{1,5},{2,6},{3,7},{4,0},{5,1},{6,2},{7,3},{8,12},{9,13},{10,... | collective-permute-start | bytes 589832 | tf_op jit(solution)/shard_map/ppermute | solution.py:427
  37.5 10.1 %collective-permute-start.8 = (bf16[4,128,128]{2,1,0:T(8,128)(2,1)S(1)}, bf16[4,128,128]{2,1,0:T(8,128)(2,1)S(1)}, u32[]{:S(2)}, u32[]{:S(2)}) collective-permute-start(bf16[4,128,128]{2,1,0:T(8,128)(2,1)S(1)} %get-tuple-element.58.order_ref), channel_id=1, source_target_pairs={{0,2},{1,3},{2,0},{3,1},{4,6},{5,7},{6,4},{7,5},{8,10},{9,11},{10,... | collective-permute-start | bytes 393224 | tf_op jit(solution)/shard_map/ppermute | solution.py:427
  41.2 9.5 %collective-permute-start.13 = (bf16[2,256,128]{2,1,0:T(8,128)(2,1)S(1)}, bf16[2,256,128]{2,1,0:T(8,128)(2,1)S(1)}, u32[]{:S(2)}, u32[]{:S(2)}) collective-permute-start(bf16[2,256,128]{2,1,0:T(8,128)(2,1)S(1)} %get-tuple-element.68.order_ref), channel_id=1, source_target_pairs={{0,4},{1,5},{2,6},{3,7},{4,0},{5,1},{6,2},{7,3},{8,12},{9,13},{10,... | collective-permute-start | bytes 393224 | tf_op jit(solution)/shard_map/ppermute | solution.py:427
  43.1 11.3 %collective-permute-start.7 = (bf16[1,384,128]{2,1,0:T(8,128)(2,1)S(1)}, bf16[1,384,128]{2,1,0:T(8,128)(2,1)S(1)}, u32[]{:S(2)}, u32[]{:S(2)}) collective-permute-start(bf16[1,384,128]{2,1,0:T(8,128)(2,1)S(1)} %get-tuple-element.62.order_ref), channel_id=1, source_target_pairs={{0,8},{1,9},{2,10},{3,11},{4,12},{5,13},{6,14},{7,15},{8,0},{9,1},... | collective-permute-start | bytes 294920 | tf_op jit(solution)/shard_map/ppermute | solution.py:427
  45.7 10.6 %collective-permute-start.14 = (bf16[1,384,128]{2,1,0:T(8,128)(2,1)S(1)}, bf16[1,384,128]{2,1,0:T(8,128)(2,1)S(1)}, u32[]{:S(2)}, u32[]{:S(2)}) collective-permute-start(bf16[1,384,128]{2,1,0:T(8,128)(2,1)S(1)} %get-tuple-element.69.order_ref), channel_id=1, source_target_pairs={{0,8},{1,9},{2,10},{3,11},{4,12},{5,13},{6,14},{7,15},{8,0},{9,1},... | collective-permute-start | bytes 294920 | tf_op jit(solution)/shard_map/ppermute | solution.py:427
  47.6 4.8 %collective-permute-start.12 = (bf16[2,128,128]{2,1,0:T(8,128)(2,1)S(1)}, bf16[2,128,128]{2,1,0:T(8,128)(2,1)S(1)}, u32[]{:S(2)}, u32[]{:S(2)}) collective-permute-start(bf16[2,128,128]{2,1,0:T(8,128)(2,1)S(1)} %get-tuple-element.71.order_ref), channel_id=1, source_target_pairs={{0,4},{1,5},{2,6},{3,7},{4,0},{5,1},{6,2},{7,3},{8,12},{9,13},{10,... | collective-permute-start | bytes 196616 | tf_op jit(solution)/shard_map/ppermute | solution.py:427
  50.1 6.9 %collective-permute-start.16 = (bf16[1,384,128]{2,1,0:T(8,128)(2,1)S(1)}, bf16[1,384,128]{2,1,0:T(8,128)(2,1)S(1)}, u32[]{:S(2)}, u32[]{:S(2)}) collective-permute-start(bf16[1,384,128]{2,1,0:T(8,128)(2,1)S(1)} %get-tuple-element.67.order_ref), channel_id=1, source_target_pairs={{0,2},{1,3},{2,0},{3,1},{4,6},{5,7},{6,4},{7,5},{8,10},{9,11},{10,... | collective-permute-start | bytes 294920 | tf_op jit(solution)/shard_map/ppermute | solution.py:427
  50.7 6.3 %collective-permute-start.15 = (bf16[1,256,128]{2,1,0:T(8,128)(2,1)S(1)}, bf16[1,256,128]{2,1,0:T(8,128)(2,1)S(1)}, u32[]{:S(2)}, u32[]{:S(2)}) collective-permute-start(bf16[1,256,128]{2,1,0:T(8,128)(2,1)S(1)} %get-tuple-element.73.order_ref), channel_id=1, source_target_pairs={{0,8},{1,9},{2,10},{3,11},{4,12},{5,13},{6,14},{7,15},{8,0},{9,1},... | collective-permute-start | bytes 196616 | tf_op jit(solution)/shard_map/ppermute | solution.py:427
  52.4 5.0 %collective-permute-start.17 = (bf16[1,128,128]{2,1,0:T(8,128)(2,1)S(1)}, bf16[1,128,128]{2,1,0:T(8,128)(2,1)S(1)}, u32[]{:S(2)}, u32[]{:S(2)}) collective-permute-start(bf16[1,128,128]{2,1,0:T(8,128)(2,1)S(1)} %get-tuple-element.74.order_ref), channel_id=1, source_target_pairs={{0,8},{1,9},{2,10},{3,11},{4,12},{5,13},{6,14},{7,15},{8,0},{9,1},... | collective-permute-start | bytes 98312 | tf_op jit(solution)/shard_map/ppermute | solution.py:427

commit v5 on v4

--- a/solution.py
+++ b/solution.py
@@ -415,7 +415,7 @@
         third = length // 3
         boxes = [(0, length, 0, LANES), (0, length, 2 * LANES, LANES), (0, 2 * third, 3 * LANES, LANES), (2 * third, third, 3 * LANES, LANES), (0, length, LANES, LANES)]
         parts = [Part(box, bits) for box in boxes[:4]] + [Part(boxes[4], far)]
-        steps = [(0, -1), (4, -1), (1, -1), (2, -1), (0, 0), (3, -1), (4, 0), (1, 0), (0, 1), (4, 1), (2, 0), (1, 1), (3, 0), (2, 1), (3, 1), (0, 2), (1, 2), (2, 2), (4, 2), (3, 2)]
+        steps = [(0, -1), (4, -1), (1, -1), (2, -1), (3, -1), (0, 0), (4, 0), (1, 0), (0, 1), (4, 1), (2, 0), (1, 1), (3, 0), (2, 1), (3, 1), (0, 2), (1, 2), (2, 2), (4, 2), (3, 2)]
     else:
         parts = [Part((0, length, LANES * at, LANES), far if at == 1 else bits) for at in range(count)]
         steps = [(at, wave - at - 1) for wave in range(count + len(bits)) for at in range(count) if -1 <= wave - at - 1 < len(bits)]

time: 58.3 us -> 58.3 us (level)
  no operation moved by 1% of the time
where the time goes in v5:
time: 58.3 us; the launch traced here: 58.1 us
  starting transfers between devices  28.2 us (48%)
  Pallas kernels  17.6 us (30%)
  waiting for transfers between devices  12.1 us (21%)
    ppermute x17, starting transfers between devices, across(): return lax.ppermute(x, 'tp', [(i, i ^ 1 << bit) for i in range(count)])  25.6 us
    ppermute x17, waiting for transfers between devices, across(): return lax.ppermute(x, 'tp', [(i, i ^ 1 << bit) for i in range(count)])  12 us
    pallas_call x4, Pallas kernels, project(): pl.pallas_call(functools.partial(project_kernel, part), out_shape=(jax.Sh...  5.32 us
    pallas_call x1, Pallas kernels, per_device(): pl.pallas_call(driven_kernel, out_shape=(jax.ShapeDtypeStruct(split, F32)...  3.93 us
    pallas_call x1, Pallas kernels, per_device(): pl.pallas_call(response_kernel, out_shape=(jax.ShapeDtypeStruct(split, F3...  2.89 us
    ppermute x1, starting transfers between devices, after(): return lax.ppermute(x, axis, [(i, (i + 1) % count) for i in range(count)])  2.59 us
    pallas_call x1, Pallas kernels, per_device(): pl.pallas_call(gated_kernel, out_shape=jax.ShapeDtypeStruct((length, chan...  1.93 us
  transfers between devices with their start and end apart: 18, of which 11 were waited for; matrix products, arithmetic and copies ran while one was open for 0% of the time, Pallas kernels for 20%

profile of v5, /device:TPU:0, one launch (start us, length us, event | category | flops | bytes accessed | tf_op | source)
XLA Modules:
  0.0 58.1 jit_solution(12212555857940461407)
XLA Ops:
  0.0 0.1 pad_add_fusion.where_ref
  0.1 0.0 copy-start
  0.1 0.0 copy-start.1
  0.1 0.0 copy-start.2
  0.1 0.0 copy-start.4
  0.1 3.9 %driven.1 = (f32[4,49,8,128]{3,2,1,0:T(8,128)S(1)}, f32[4,16,8,128]{3,2,1,0:T(8,128)S(1)}, f32[40,512]{1,0:T(8,128)S(1)}, bf16[8,512,512]{2,1,0:T(8,128)(2,1)S(1)}) custom-call(s32[3]{0:T(128)S(1)} %pad_add_fusion.where_ref, bf16[3,1,384,512]{3,2,1,0:T(8,128)(2,1)} %head_in_ref.1, f32[3,7,512]{2,1,0:T(8,128)} %taps_ref.3, f32[16,512]{1,0:T(8,128)} %decay_ref.3, ...), custom_call_target="tpu_custom_call" | custom-call | flops 1 | bytes 1 | tf_op jit(solution)/shard_map/driven/pallas_call | solution.py:471
  4.0 0.5 collective-permute-start.2
  4.5 2.6 %collective-permute-start = (f32[40,512]{1,0:T(8,128)S(1)}, f32[40,512]{1,0:T(8,128)S(1)}, u32[]{:S(2)}, u32[]{:S(2)}) collective-permute-start(f32[40,512]{1,0:T(8,128)S(1)} %get-tuple-element.42), channel_id=1, source_target_pairs={{0,16},{16,0},{1,17},{17,1},{2,18},{18,2},{3,19},{19,3},{4,20},{20... | collective-permute-start | bytes 245768 | tf_op jit(solution)/shard_map/ppermute | solution.py:432
  7.1 0.0 copy-done
  7.1 0.0 copy-done.1
  7.1 0.0 copy-done.2
  7.2 0.0 copy-done.4
  7.2 0.0 copy-start.3
  7.2 2.9 %response.1 = (f32[4,49,8,128]{3,2,1,0:T(8,128)S(1)}, f32[4,49,8,128]{3,2,1,0:T(8,128)S(1)}, bf16[8,512,512]{2,1,0:T(8,128)(2,1)S(1)}) custom-call(s32[3]{0:T(128)S(1)} %pad_add_fusion.where_ref, bf16[3,1,384,512]{3,2,1,0:T(8,128)(2,1)S(1)} %copy-done, f32[3,7,512]{2,1,0:T(8,128)S(1)} %copy-done.1, f32[16,512]{1,0:T(8,128)S(1)} %copy-done.2, ...), custom_call_target="tpu_custom_call" | custom-call | flops 1 | bytes 1 | tf_op jit(solution)/shard_map/response/pallas_call | solution.py:497
  10.1 0.1 collective-permute-done.message_ref
  10.2 0.0 copy-done.3
  10.2 1.9 %gated.1.own_ref = bf16[384,512]{1,0:T(8,128)(2,1)S(1)} custom-call(s32[3]{0:T(128)S(1)} %pad_add_fusion.where_ref, f32[40,512]{1,0:T(8,128)S(1)} %collective-permute-done.message_ref, bf16[3,1,384,512]{3,2,1,0:T(8,128)(2,1)S(1)} %copy-done, f32[3,7,512]{2,1,0:T(8,128)S(1)} %copy-done.1, f32[16,512]{1,0:T(8,128)S(1)} %copy-done.2, f32[16,512]{1,0:T(8,128)S(1)} %copy-done.4, ...), custom_call_target="tpu_custom_call" | custom-call | flops 1 | bytes 1 | tf_op jit(solution)/shard_map/gated/pallas_call | solution.py:513
  12.1 0.1 collective-permute-start.1
  12.3 1.1 %project_own.1.sum_ref = f32[4,384,256]{2,1,0:T(8,128)S(1)} custom-call(s32[3]{0:T(128)S(1)} %pad_add_fusion.where_ref, bf16[384,512]{1,0:T(8,128)(2,1)S(1)} %gated.1.own_ref, bf16[8,512,512]{2,1,0:T(8,128)(2,1)S(1)} %get-tuple-element.47.mine_ref), custom_call_target="tpu_custom_call" | custom-call | flops 1 | bytes 1 | tf_op jit(solution)/shard_map/project_own/pallas_call | solution.py:346
  13.4 0.5 collective-permute-done.1.other_ref
  13.9 0.0 collective-permute-done.2.theirs_ref
  13.9 1.1 %project_other.1 = (bf16[4,384,128]{2,1,0:T(8,128)(2,1)S(1)}, f32[4,384,128]{2,1,0:T(8,128)S(1)}) custom-call(s32[3]{0:T(128)S(1)} %pad_add_fusion.where_ref, f32[4,384,256]{2,1,0:T(8,128)S(1)} %project_own.1.sum_ref, bf16[384,512]{1,0:T(8,128)(2,1)S(1)} %collective-permute-done.1.other_ref, bf16[8,512,512]{2,1,0:T(8,128)(2,1)S(1)} %collective-permute-done.2.theirs_ref), custom_call_target="tpu_custom_call" | custom-call | flops 1 | bytes 1 | tf_op jit(solution)/shard_map/project_other/pallas_call | solution.py:360
  15.0 1.8 %collective-permute-start.3 = (bf16[4,384,128]{2,1,0:T(8,128)(2,1)S(1)}, bf16[4,384,128]{2,1,0:T(8,128)(2,1)S(1)}, u32[]{:S(2)}, u32[]{:S(2)}) collective-permute-start(bf16[4,384,128]{2,1,0:T(8,128)(2,1)S(1)} %get-tuple-element.50.order_ref), channel_id=1, source_target_pairs={{0,2},{1,3},{2,0},{3,1},{4,6},{5,7},{6,4},{7,5},{8,10},{9,11},{10,... | collective-permute-start | bytes 1179656 | tf_op jit(solution)/shard_map/ppermute | solution.py:427
  16.8 1.5 %project.4 = (bf16[4,384,128]{2,1,0:T(8,128)(2,1)S(1)}, f32[4,384,128]{2,1,0:T(8,128)S(1)}) custom-call(s32[3]{0:T(128)S(1)} %pad_add_fusion.where_ref, bf16[384,512]{1,0:T(8,128)(2,1)S(1)} %gated.1.own_ref, bf16[384,512]{1,0:T(8,128)(2,1)S(1)} %collective-permute-done.1.other_ref, bf16[8,512,512]{2,1,0:T(8,128)(2,1)S(1)} %get-tuple-element.47.mine_ref, ...), custom_call_target="tpu_custom_call" | custom-call | flops 1 | bytes 1 | tf_op jit(solution)/shard_map/project/pallas_call | solution.py:333
  18.4 1.6 %collective-permute-start.6 = (bf16[4,384,128]{2,1,0:T(8,128)(2,1)S(1)}, bf16[4,384,128]{2,1,0:T(8,128)(2,1)S(1)}, u32[]{:S(2)}, u32[]{:S(2)}) collective-permute-start(bf16[4,384,128]{2,1,0:T(8,128)(2,1)S(1)} %get-tuple-element.51.order_ref), channel_id=1, source_target_pairs={{0,4},{1,5},{2,6},{3,7},{4,0},{5,1},{6,2},{7,3},{8,12},{9,13},{10,... | collective-permute-start | bytes 1179656 | tf_op jit(solution)/shard_map/ppermute | solution.py:427
  20.0 1.5 %project.5 = (bf16[4,384,128]{2,1,0:T(8,128)(2,1)S(1)}, f32[4,384,128]{2,1,0:T(8,128)S(1)}) custom-call(s32[3]{0:T(128)S(1)} %pad_add_fusion.where_ref, bf16[384,512]{1,0:T(8,128)(2,1)S(1)} %gated.1.own_ref, bf16[384,512]{1,0:T(8,128)(2,1)S(1)} %collective-permute-done.1.other_ref, bf16[8,512,512]{2,1,0:T(8,128)(2,1)S(1)} %get-tuple-element.47.mine_ref, ...), custom_call_target="tpu_custom_call" | custom-call | flops 1 | bytes 1 | tf_op jit(solution)/shard_map/project/pallas_call | solution.py:333
  21.5 0.6 %collective-permute-start.5 = (bf16[4,384,128]{2,1,0:T(8,128)(2,1)S(1)}, bf16[4,384,128]{2,1,0:T(8,128)(2,1)S(1)}, u32[]{:S(2)}, u32[]{:S(2)}) collective-permute-start(bf16[4,384,128]{2,1,0:T(8,128)(2,1)S(1)} %get-tuple-element.52.order_ref), channel_id=1, source_target_pairs={{0,2},{1,3},{2,0},{3,1},{4,6},{5,7},{6,4},{7,5},{8,10},{9,11},{10,... | collective-permute-start | bytes 1179656 | tf_op jit(solution)/shard_map/ppermute | solution.py:427
  22.1 1.3 %project.6 = (bf16[4,256,128]{2,1,0:T(8,128)(2,1)S(1)}, f32[4,256,128]{2,1,0:T(8,128)S(1)}) custom-call(s32[3]{0:T(128)S(1)} %pad_add_fusion.where_ref, bf16[384,512]{1,0:T(8,128)(2,1)S(1)} %gated.1.own_ref, bf16[384,512]{1,0:T(8,128)(2,1)S(1)} %collective-permute-done.1.other_ref, bf16[8,512,512]{2,1,0:T(8,128)(2,1)S(1)} %get-tuple-element.47.mine_ref, ...), custom_call_target="tpu_custom_call" | custom-call | flops 1 | bytes 1 | tf_op jit(solution)/shard_map/project/pallas_call | solution.py:333
  23.4 1.6 %collective-permute-start.10 = (bf16[4,256,128]{2,1,0:T(8,128)(2,1)S(1)}, bf16[4,256,128]{2,1,0:T(8,128)(2,1)S(1)}, u32[]{:S(2)}, u32[]{:S(2)}) collective-permute-start(bf16[4,256,128]{2,1,0:T(8,128)(2,1)S(1)} %get-tuple-element.53.order_ref), channel_id=1, source_target_pairs={{0,2},{1,3},{2,0},{3,1},{4,6},{5,7},{6,4},{7,5},{8,10},{9,11},{10,... | collective-permute-start | bytes 786440 | tf_op jit(solution)/shard_map/ppermute | solution.py:427
  25.0 1.0 %project.7 = (bf16[4,128,128]{2,1,0:T(8,128)(2,1)S(1)}, f32[4,128,128]{2,1,0:T(8,128)S(1)}) custom-call(s32[3]{0:T(128)S(1)} %pad_add_fusion.where_ref, bf16[384,512]{1,0:T(8,128)(2,1)S(1)} %gated.1.own_ref, bf16[384,512]{1,0:T(8,128)(2,1)S(1)} %collective-permute-done.1.other_ref, bf16[8,512,512]{2,1,0:T(8,128)(2,1)S(1)} %get-tuple-element.47.mine_ref, ...), custom_call_target="tpu_custom_call" | custom-call | flops 1 | bytes 1 | tf_op jit(solution)/shard_map/project/pallas_call | solution.py:333
  26.0 1.1 %collective-permute-done.3.received_ref = bf16[4,384,128]{2,1,0:T(8,128)(2,1)S(1)} collective-permute-done((bf16[4,384,128]{2,1,0:T(8,128)(2,1)S(1)}, bf16[4,384,128]{2,1,0:T(8,128)(2,1)S(1)}, u32[]{:S(2)}, u32[]{:S(2)}) %collective-permute-start.3) | collective-permute-done | bytes 393248 | tf_op jit(solution)/shard_map/ppermute | solution.py:427
  27.1 0.1 merge.10
  27.1 1.9 %collective-permute-start.4 = (bf16[2,384,128]{2,1,0:T(8,128)(2,1)S(1)}, bf16[2,384,128]{2,1,0:T(8,128)(2,1)S(1)}, u32[]{:S(2)}, u32[]{:S(2)}) collective-permute-start(bf16[2,384,128]{2,1,0:T(8,128)(2,1)S(1)} %get-tuple-element.56.order_ref), channel_id=1, source_target_pairs={{0,4},{1,5},{2,6},{3,7},{4,0},{5,1},{6,2},{7,3},{8,12},{9,13},{10,... | collective-permute-start | bytes 589832 | tf_op jit(solution)/shard_map/ppermute | solution.py:427
  29.0 1.2 %collective-permute-done.6.received_ref = bf16[4,384,128]{2,1,0:T(8,128)(2,1)S(1)} collective-permute-done((bf16[4,384,128]{2,1,0:T(8,128)(2,1)S(1)}, bf16[4,384,128]{2,1,0:T(8,128)(2,1)S(1)}, u32[]{:S(2)}, u32[]{:S(2)}) %collective-permute-start.6) | collective-permute-done | bytes 393248 | tf_op jit(solution)/shard_map/ppermute | solution.py:427
  30.2 0.1 merge.11
  30.2 2.5 %collective-permute-start.11 = (bf16[2,384,128]{2,1,0:T(8,128)(2,1)S(1)}, bf16[2,384,128]{2,1,0:T(8,128)(2,1)S(1)}, u32[]{:S(2)}, u32[]{:S(2)}) collective-permute-start(bf16[2,384,128]{2,1,0:T(8,128)(2,1)S(1)} %get-tuple-element.59.order_ref), channel_id=1, source_target_pairs={{0,8},{1,9},{2,10},{3,11},{4,12},{5,13},{6,14},{7,15},{8,0},{9,1},... | collective-permute-start | bytes 589832 | tf_op jit(solution)/shard_map/ppermute | solution.py:427
  32.7 2.8 %collective-permute-done.5.received_ref = bf16[4,384,128]{2,1,0:T(8,128)(2,1)S(1)} collective-permute-done((bf16[4,384,128]{2,1,0:T(8,128)(2,1)S(1)}, bf16[4,384,128]{2,1,0:T(8,128)(2,1)S(1)}, u32[]{:S(2)}, u32[]{:S(2)}) %collective-permute-start.5) | collective-permute-done | bytes 393248 | tf_op jit(solution)/shard_map/ppermute | solution.py:427
  35.5 0.1 merge.12
  35.6 1.9 %collective-permute-start.9 = (bf16[2,384,128]{2,1,0:T(8,128)(2,1)S(1)}, bf16[2,384,128]{2,1,0:T(8,128)(2,1)S(1)}, u32[]{:S(2)}, u32[]{:S(2)}) collective-permute-start(bf16[2,384,128]{2,1,0:T(8,128)(2,1)S(1)} %get-tuple-element.60.order_ref), channel_id=1, source_target_pairs={{0,4},{1,5},{2,6},{3,7},{4,0},{5,1},{6,2},{7,3},{8,12},{9,13},{10,... | collective-permute-start | bytes 589832 | tf_op jit(solution)/shard_map/ppermute | solution.py:427
  37.4 1.5 %collective-permute-start.8 = (bf16[4,128,128]{2,1,0:T(8,128)(2,1)S(1)}, bf16[4,128,128]{2,1,0:T(8,128)(2,1)S(1)}, u32[]{:S(2)}, u32[]{:S(2)}) collective-permute-start(bf16[4,128,128]{2,1,0:T(8,128)(2,1)S(1)} %get-tuple-element.54.order_ref), channel_id=1, source_target_pairs={{0,2},{1,3},{2,0},{3,1},{4,6},{5,7},{6,4},{7,5},{8,10},{9,11},{10,... | collective-permute-start | bytes 393224 | tf_op jit(solution)/shard_map/ppermute | solution.py:427
  38.9 0.0 collective-permute-done.4.received_ref
  39.0 1.7 %collective-permute-done.11.received_ref = bf16[2,384,128]{2,1,0:T(8,128)(2,1)S(1)} collective-permute-done((bf16[2,384,128]{2,1,0:T(8,128)(2,1)S(1)}, bf16[2,384,128]{2,1,0:T(8,128)(2,1)S(1)}, u32[]{:S(2)}, u32[]{:S(2)}) %collective-permute-start.11) | collective-permute-done | bytes 196640 | tf_op jit(solution)/shard_map/ppermute | solution.py:427
  40.7 0.4 collective-permute-done.10.received_ref
  41.2 1.9 %collective-permute-start.13 = (bf16[2,256,128]{2,1,0:T(8,128)(2,1)S(1)}, bf16[2,256,128]{2,1,0:T(8,128)(2,1)S(1)}, u32[]{:S(2)}, u32[]{:S(2)}) collective-permute-start(bf16[2,256,128]{2,1,0:T(8,128)(2,1)S(1)} %get-tuple-element.68.order_ref), channel_id=1, source_target_pairs={{0,4},{1,5},{2,6},{3,7},{4,0},{5,1},{6,2},{7,3},{8,12},{9,13},{10,... | collective-permute-start | bytes 393224 | tf_op jit(solution)/shard_map/ppermute | solution.py:427
  43.0 2.6 %collective-permute-start.7 = (bf16[1,384,128]{2,1,0:T(8,128)(2,1)S(1)}, bf16[1,384,128]{2,1,0:T(8,128)(2,1)S(1)}, u32[]{:S(2)}, u32[]{:S(2)}) collective-permute-start(bf16[1,384,128]{2,1,0:T(8,128)(2,1)S(1)} %get-tuple-element.62.order_ref), channel_id=1, source_target_pairs={{0,8},{1,9},{2,10},{3,11},{4,12},{5,13},{6,14},{7,15},{8,0},{9,1},... | collective-permute-start | bytes 294920 | tf_op jit(solution)/shard_map/ppermute | solution.py:427
  45.6 0.0 collective-permute-done.9.received_ref
  45.7 1.8 %collective-permute-start.14 = (bf16[1,384,128]{2,1,0:T(8,128)(2,1)S(1)}, bf16[1,384,128]{2,1,0:T(8,128)(2,1)S(1)}, u32[]{:S(2)}, u32[]{:S(2)}) collective-permute-start(bf16[1,384,128]{2,1,0:T(8,128)(2,1)S(1)} %get-tuple-element.69.order_ref), channel_id=1, source_target_pairs={{0,8},{1,9},{2,10},{3,11},{4,12},{5,13},{6,14},{7,15},{8,0},{9,1},... | collective-permute-start | bytes 294920 | tf_op jit(solution)/shard_map/ppermute | solution.py:427
  47.5 0.0 collective-permute-done.8.received_ref
  47.5 2.5 %collective-permute-start.12 = (bf16[2,128,128]{2,1,0:T(8,128)(2,1)S(1)}, bf16[2,128,128]{2,1,0:T(8,128)(2,1)S(1)}, u32[]{:S(2)}, u32[]{:S(2)}) collective-permute-start(bf16[2,128,128]{2,1,0:T(8,128)(2,1)S(1)} %get-tuple-element.71.order_ref), channel_id=1, source_target_pairs={{0,4},{1,5},{2,6},{3,7},{4,0},{5,1},{6,2},{7,3},{8,12},{9,13},{10,... | collective-permute-start | bytes 196616 | tf_op jit(solution)/shard_map/ppermute | solution.py:427
  50.1 0.0 collective-permute-start.16
  50.1 0.0 collective-permute-done.13.received_ref
  50.1 0.7 %collective-permute-start.15 = (bf16[1,256,128]{2,1,0:T(8,128)(2,1)S(1)}, bf16[1,256,128]{2,1,0:T(8,128)(2,1)S(1)}, u32[]{:S(2)}, u32[]{:S(2)}) collective-permute-start(bf16[1,256,128]{2,1,0:T(8,128)(2,1)S(1)} %get-tuple-element.73.order_ref), channel_id=1, source_target_pairs={{0,8},{1,9},{2,10},{3,11},{4,12},{5,13},{6,14},{7,15},{8,0},{9,1},... | collective-permute-start | bytes 196616 | tf_op jit(solution)/shard_map/ppermute | solution.py:427
  50.9 1.5 %collective-permute-done.12.received_ref = bf16[2,128,128]{2,1,0:T(8,128)(2,1)S(1)} collective-permute-done((bf16[2,128,128]{2,1,0:T(8,128)(2,1)S(1)}, bf16[2,128,128]{2,1,0:T(8,128)(2,1)S(1)}, u32[]{:S(2)}, u32[]{:S(2)}) %collective-permute-start.12) | collective-permute-done | bytes 65568 | tf_op jit(solution)/shard_map/ppermute | solution.py:427
  52.3 2.0 %collective-permute-start.17 = (bf16[1,128,128]{2,1,0:T(8,128)(2,1)S(1)}, bf16[1,128,128]{2,1,0:T(8,128)(2,1)S(1)}, u32[]{:S(2)}, u32[]{:S(2)}) collective-permute-start(bf16[1,128,128]{2,1,0:T(8,128)(2,1)S(1)} %get-tuple-element.74.order_ref), channel_id=1, source_target_pairs={{0,8},{1,9},{2,10},{3,11},{4,12},{5,13},{6,14},{7,15},{8,0},{9,1},... | collective-permute-start | bytes 98312 | tf_op jit(solution)/shard_map/ppermute | solution.py:427
  54.4 0.0 collective-permute-done.7.received_ref
  54.4 1.9 %collective-permute-done.14.received_ref = bf16[1,384,128]{2,1,0:T(8,128)(2,1)S(1)} collective-permute-done((bf16[1,384,128]{2,1,0:T(8,128)(2,1)S(1)}, bf16[1,384,128]{2,1,0:T(8,128)(2,1)S(1)}, u32[]{:S(2)}, u32[]{:S(2)}) %collective-permute-start.14) | collective-permute-done | bytes 98336 | tf_op jit(solution)/shard_map/ppermute | solution.py:427
  56.3 0.7 %collective-permute-done.15.received_ref = bf16[1,256,128]{2,1,0:T(8,128)(2,1)S(1)} collective-permute-done((bf16[1,256,128]{2,1,0:T(8,128)(2,1)S(1)}, bf16[1,256,128]{2,1,0:T(8,128)(2,1)S(1)}, u32[]{:S(2)}, u32[]{:S(2)}) %collective-permute-start.15) | collective-permute-done | bytes 65568 | tf_op jit(solution)/shard_map/ppermute | solution.py:427
  57.0 0.0 collective-permute-done.16.received_ref
  57.1 0.3 collective-permute-done.17.refs_5_
  57.4 0.8 %gather.1 = bf16[1,384,512]{2,1,0:T(8,128)(2,1)} custom-call(bf16[384,128]{1,0:T(8,128)(2,1)S(1)} %finish.4.order_ref.refs_0_, bf16[384,128]{1,0:T(8,128)(2,1)S(1)} %finish.5.order_ref.refs_1_, bf16[256,128]{1,0:T(8,128)(2,1)S(1)} %finish.6.order_ref.refs_2_, bf16[384,128]{1,0:T(8,128)(2,1)S(1)} %finish.7.refs_3_.refs_6_, ...), custom_call_target="tpu_custom_call" | custom-call | flops 1 | bytes 1 | tf_op jit(solution)/shard_map/gather/pallas_call | solution.py:398
  (11 shorter events, 0.3 us)
Async XLA Ops:
  0.1 7.1 %copy-start = (bf16[3,1,384,512]{3,2,1,0:T(8,128)(2,1)S(1)}, bf16[3,1,384,512]{3,2,1,0:T(8,128)(2,1)}, u32[]{:S(2)}) copy-start(bf16[3,1,384,512]{3,2,1,0:T(8,128)(2,1)} %head_in_ref.1) | copy-start | bytes 3538948
  0.1 7.1 %copy-start.1 = (f32[3,7,512]{2,1,0:T(8,128)S(1)}, f32[3,7,512]{2,1,0:T(8,128)}, u32[]{:S(2)}) copy-start(f32[3,7,512]{2,1,0:T(8,128)} %taps_ref.3) | copy-start | bytes 129028
  0.1 7.1 %copy-start.2 = (f32[16,512]{1,0:T(8,128)S(1)}, f32[16,512]{1,0:T(8,128)}, u32[]{:S(2)}) copy-start(f32[16,512]{1,0:T(8,128)} %decay_ref.3) | copy-start | bytes 98308
  0.1 7.1 %copy-start.4 = (f32[16,512]{1,0:T(8,128)S(1)}, f32[16,512]{1,0:T(8,128)}, u32[]{:S(2)}) copy-start(f32[16,512]{1,0:T(8,128)} %residues_ref.3) | copy-start | bytes 98308
  4.0 9.9 %collective-permute-start.2 = (bf16[8,512,512]{2,1,0:T(8,128)(2,1)S(1)}, bf16[8,512,512]{2,1,0:T(8,128)(2,1)S(1)}, u32[]{:S(2)}, u32[]{:S(2)}) collective-permute-start(bf16[8,512,512]{2,1,0:T(8,128)(2,1)S(1)} %get-tuple-element.48), channel_id=1, source_target_pairs={{0,1},{1,0},{2,3},{3,2},{4,5},{5,4},{6,7},{7,6},{8,9},{9,8},{10,11... | collective-permute-start | bytes 12582920 | tf_op jit(solution)/shard_map/ppermute | solution.py:427
  4.5 5.6 %collective-permute-start = (f32[40,512]{1,0:T(8,128)S(1)}, f32[40,512]{1,0:T(8,128)S(1)}, u32[]{:S(2)}, u32[]{:S(2)}) collective-permute-start(f32[40,512]{1,0:T(8,128)S(1)} %get-tuple-element.42), channel_id=1, source_target_pairs={{0,16},{16,0},{1,17},{17,1},{2,18},{18,2},{3,19},{19,3},{4,20},{20... | collective-permute-start | bytes 245768 | tf_op jit(solution)/shard_map/ppermute | solution.py:432
  7.2 3.0 %copy-start.3 = (f32[1,16,512]{2,1,0:T(8,128)S(1)}, f32[1,16,512]{2,1,0:T(8,128)}, u32[]{:S(2)}) copy-start(f32[1,16,512]{2,1,0:T(8,128)} %init_ref.1) | copy-start | bytes 98308
  12.1 1.8 %collective-permute-start.1 = (bf16[384,512]{1,0:T(8,128)(2,1)S(1)}, bf16[384,512]{1,0:T(8,128)(2,1)S(1)}, u32[]{:S(2)}, u32[]{:S(2)}) collective-permute-start(bf16[384,512]{1,0:T(8,128)(2,1)S(1)} %gated.1.own_ref), channel_id=1, source_target_pairs={{0,1},{1,0},{2,3},{3,2},{4,5},{5,4},{6,7},{7,6},{8,9},{9,8},{10,11... | collective-permute-start | bytes 1179656 | tf_op jit(solution)/shard_map/ppermute | solution.py:427
  15.0 12.0 %collective-permute-start.3 = (bf16[4,384,128]{2,1,0:T(8,128)(2,1)S(1)}, bf16[4,384,128]{2,1,0:T(8,128)(2,1)S(1)}, u32[]{:S(2)}, u32[]{:S(2)}) collective-permute-start(bf16[4,384,128]{2,1,0:T(8,128)(2,1)S(1)} %get-tuple-element.50.order_ref), channel_id=1, source_target_pairs={{0,2},{1,3},{2,0},{3,1},{4,6},{5,7},{6,4},{7,5},{8,10},{9,11},{10,... | collective-permute-start | bytes 1179656 | tf_op jit(solution)/shard_map/ppermute | solution.py:427
  18.4 11.8 %collective-permute-start.6 = (bf16[4,384,128]{2,1,0:T(8,128)(2,1)S(1)}, bf16[4,384,128]{2,1,0:T(8,128)(2,1)S(1)}, u32[]{:S(2)}, u32[]{:S(2)}) collective-permute-start(bf16[4,384,128]{2,1,0:T(8,128)(2,1)S(1)} %get-tuple-element.51.order_ref), channel_id=1, source_target_pairs={{0,4},{1,5},{2,6},{3,7},{4,0},{5,1},{6,2},{7,3},{8,12},{9,13},{10,... | collective-permute-start | bytes 1179656 | tf_op jit(solution)/shard_map/ppermute | solution.py:427
  21.5 13.9 %collective-permute-start.5 = (bf16[4,384,128]{2,1,0:T(8,128)(2,1)S(1)}, bf16[4,384,128]{2,1,0:T(8,128)(2,1)S(1)}, u32[]{:S(2)}, u32[]{:S(2)}) collective-permute-start(bf16[4,384,128]{2,1,0:T(8,128)(2,1)S(1)} %get-tuple-element.52.order_ref), channel_id=1, source_target_pairs={{0,2},{1,3},{2,0},{3,1},{4,6},{5,7},{6,4},{7,5},{8,10},{9,11},{10,... | collective-permute-start | bytes 1179656 | tf_op jit(solution)/shard_map/ppermute | solution.py:427
  23.4 17.7 %collective-permute-start.10 = (bf16[4,256,128]{2,1,0:T(8,128)(2,1)S(1)}, bf16[4,256,128]{2,1,0:T(8,128)(2,1)S(1)}, u32[]{:S(2)}, u32[]{:S(2)}) collective-permute-start(bf16[4,256,128]{2,1,0:T(8,128)(2,1)S(1)} %get-tuple-element.53.order_ref), channel_id=1, source_target_pairs={{0,2},{1,3},{2,0},{3,1},{4,6},{5,7},{6,4},{7,5},{8,10},{9,11},{10,... | collective-permute-start | bytes 786440 | tf_op jit(solution)/shard_map/ppermute | solution.py:427
  27.1 11.8 %collective-permute-start.4 = (bf16[2,384,128]{2,1,0:T(8,128)(2,1)S(1)}, bf16[2,384,128]{2,1,0:T(8,128)(2,1)S(1)}, u32[]{:S(2)}, u32[]{:S(2)}) collective-permute-start(bf16[2,384,128]{2,1,0:T(8,128)(2,1)S(1)} %get-tuple-element.56.order_ref), channel_id=1, source_target_pairs={{0,4},{1,5},{2,6},{3,7},{4,0},{5,1},{6,2},{7,3},{8,12},{9,13},{10,... | collective-permute-start | bytes 589832 | tf_op jit(solution)/shard_map/ppermute | solution.py:427
  30.2 10.5 %collective-permute-start.11 = (bf16[2,384,128]{2,1,0:T(8,128)(2,1)S(1)}, bf16[2,384,128]{2,1,0:T(8,128)(2,1)S(1)}, u32[]{:S(2)}, u32[]{:S(2)}) collective-permute-start(bf16[2,384,128]{2,1,0:T(8,128)(2,1)S(1)} %get-tuple-element.59.order_ref), channel_id=1, source_target_pairs={{0,8},{1,9},{2,10},{3,11},{4,12},{5,13},{6,14},{7,15},{8,0},{9,1},... | collective-permute-start | bytes 589832 | tf_op jit(solution)/shard_map/ppermute | solution.py:427
  35.6 10.1 %collective-permute-start.9 = (bf16[2,384,128]{2,1,0:T(8,128)(2,1)S(1)}, bf16[2,384,128]{2,1,0:T(8,128)(2,1)S(1)}, u32[]{:S(2)}, u32[]{:S(2)}) collective-permute-start(bf16[2,384,128]{2,1,0:T(8,128)(2,1)S(1)} %get-tuple-element.60.order_ref), channel_id=1, source_target_pairs={{0,4},{1,5},{2,6},{3,7},{4,0},{5,1},{6,2},{7,3},{8,12},{9,13},{10,... | collective-permute-start | bytes 589832 | tf_op jit(solution)/shard_map/ppermute | solution.py:427
  37.4 10.1 %collective-permute-start.8 = (bf16[4,128,128]{2,1,0:T(8,128)(2,1)S(1)}, bf16[4,128,128]{2,1,0:T(8,128)(2,1)S(1)}, u32[]{:S(2)}, u32[]{:S(2)}) collective-permute-start(bf16[4,128,128]{2,1,0:T(8,128)(2,1)S(1)} %get-tuple-element.54.order_ref), channel_id=1, source_target_pairs={{0,2},{1,3},{2,0},{3,1},{4,6},{5,7},{6,4},{7,5},{8,10},{9,11},{10,... | collective-permute-start | bytes 393224 | tf_op jit(solution)/shard_map/ppermute | solution.py:427
  41.2 8.9 %collective-permute-start.13 = (bf16[2,256,128]{2,1,0:T(8,128)(2,1)S(1)}, bf16[2,256,128]{2,1,0:T(8,128)(2,1)S(1)}, u32[]{:S(2)}, u32[]{:S(2)}) collective-permute-start(bf16[2,256,128]{2,1,0:T(8,128)(2,1)S(1)} %get-tuple-element.68.order_ref), channel_id=1, source_target_pairs={{0,4},{1,5},{2,6},{3,7},{4,0},{5,1},{6,2},{7,3},{8,12},{9,13},{10,... | collective-permute-start | bytes 393224 | tf_op jit(solution)/shard_map/ppermute | solution.py:427
  43.0 11.3 %collective-permute-start.7 = (bf16[1,384,128]{2,1,0:T(8,128)(2,1)S(1)}, bf16[1,384,128]{2,1,0:T(8,128)(2,1)S(1)}, u32[]{:S(2)}, u32[]{:S(2)}) collective-permute-start(bf16[1,384,128]{2,1,0:T(8,128)(2,1)S(1)} %get-tuple-element.62.order_ref), channel_id=1, source_target_pairs={{0,8},{1,9},{2,10},{3,11},{4,12},{5,13},{6,14},{7,15},{8,0},{9,1},... | collective-permute-start | bytes 294920 | tf_op jit(solution)/shard_map/ppermute | solution.py:427
  45.7 10.6 %collective-permute-start.14 = (bf16[1,384,128]{2,1,0:T(8,128)(2,1)S(1)}, bf16[1,384,128]{2,1,0:T(8,128)(2,1)S(1)}, u32[]{:S(2)}, u32[]{:S(2)}) collective-permute-start(bf16[1,384,128]{2,1,0:T(8,128)(2,1)S(1)} %get-tuple-element.69.order_ref), channel_id=1, source_target_pairs={{0,8},{1,9},{2,10},{3,11},{4,12},{5,13},{6,14},{7,15},{8,0},{9,1},... | collective-permute-start | bytes 294920 | tf_op jit(solution)/shard_map/ppermute | solution.py:427
  47.5 4.8 %collective-permute-start.12 = (bf16[2,128,128]{2,1,0:T(8,128)(2,1)S(1)}, bf16[2,128,128]{2,1,0:T(8,128)(2,1)S(1)}, u32[]{:S(2)}, u32[]{:S(2)}) collective-permute-start(bf16[2,128,128]{2,1,0:T(8,128)(2,1)S(1)} %get-tuple-element.71.order_ref), channel_id=1, source_target_pairs={{0,4},{1,5},{2,6},{3,7},{4,0},{5,1},{6,2},{7,3},{8,12},{9,13},{10,... | collective-permute-start | bytes 196616 | tf_op jit(solution)/shard_map/ppermute | solution.py:427
  50.1 6.9 %collective-permute-start.16 = (bf16[1,384,128]{2,1,0:T(8,128)(2,1)S(1)}, bf16[1,384,128]{2,1,0:T(8,128)(2,1)S(1)}, u32[]{:S(2)}, u32[]{:S(2)}) collective-permute-start(bf16[1,384,128]{2,1,0:T(8,128)(2,1)S(1)} %get-tuple-element.67.order_ref), channel_id=1, source_target_pairs={{0,2},{1,3},{2,0},{3,1},{4,6},{5,7},{6,4},{7,5},{8,10},{9,11},{10,... | collective-permute-start | bytes 294920 | tf_op jit(solution)/shard_map/ppermute | solution.py:427
  50.1 6.9 %collective-permute-start.15 = (bf16[1,256,128]{2,1,0:T(8,128)(2,1)S(1)}, bf16[1,256,128]{2,1,0:T(8,128)(2,1)S(1)}, u32[]{:S(2)}, u32[]{:S(2)}) collective-permute-start(bf16[1,256,128]{2,1,0:T(8,128)(2,1)S(1)} %get-tuple-element.73.order_ref), channel_id=1, source_target_pairs={{0,8},{1,9},{2,10},{3,11},{4,12},{5,13},{6,14},{7,15},{8,0},{9,1},... | collective-permute-start | bytes 196616 | tf_op jit(solution)/shard_map/ppermute | solution.py:427
  52.3 5.0 %collective-permute-start.17 = (bf16[1,128,128]{2,1,0:T(8,128)(2,1)S(1)}, bf16[1,128,128]{2,1,0:T(8,128)(2,1)S(1)}, u32[]{:S(2)}, u32[]{:S(2)}) collective-permute-start(bf16[1,128,128]{2,1,0:T(8,128)(2,1)S(1)} %get-tuple-element.74.order_ref), channel_id=1, source_target_pairs={{0,8},{1,9},{2,10},{3,11},{4,12},{5,13},{6,14},{7,15},{8,0},{9,1},... | collective-permute-start | bytes 98312 | tf_op jit(solution)/shard_map/ppermute | solution.py:427

commit v6 on v5

--- a/solution.py
+++ b/solution.py
@@ -14,6 +14,7 @@
 SEGS = 8
 PAD = 8
 EDGE = 2 * PAD
+SPARE = 64
 
 
 def power(base, exponent):
@@ -67,11 +68,10 @@
         lanes = pl.ds(tile * LANES, LANES)
         loads.append(pltpu.make_async_copy(streams_hbm.at[1:3, 0, :, lanes], streams_ref.at[tile], sems.at[4 + tile]))
     loads[0].start()
-    for copy in small + loads[1:]:
+    for copy in small[:2] + loads[1:] + small[2:]:
         copy.start()
     copies = weight_columns(weight_hbm, sent_ref, 1 - core, weight_sems)
-    for copy in small:
-        copy.wait()
+    small[0].wait()
     sublane = lax.broadcasted_iota(jnp.int32, (SEGS, LANES), 0)
     for tile in range(tiles):
         lanes = slice(tile * LANES, (tile + 1) * LANES)
@@ -103,6 +103,8 @@
         for j in range(tap_count - 1):
             driven_ref[tile, PAD + j, 0:1, :] = jnp.where(first, driven_ref[tile, PAD + j, 0:1, :], 0.0)
 
+        if tile == 0:
+            small[1].wait()
         decays = [jnp.broadcast_to(decay_ref[n : n + 1, lanes], (SEGS, LANES)) for n in range(poles)]
 
         def scan(b, states):
@@ -122,6 +124,8 @@
                 factor = factor * factor
             inner_ref[tile, n] = total
             message_ref[n : n + 1, lanes] = total[SEGS - 1 : SEGS, :]
+    small[2].wait()
+    small[3].wait()
     carried = power(decay_ref[...], length) * init_ref[0]
     message_ref[0:poles, :] = message_ref[0:poles, :] + jnp.where(first, carried, 0.0)
     for s in range(3):
@@ -230,7 +234,7 @@
         for j in range(lag):
             total = response_ref[tile, PAD + j, 0:1, :] + early_ref[j : j + 1, lanes]
             out_ref[PAD + j : PAD + j + 1, :] = total * head_query[j : j + 1, lanes]
-        gated_ref[:, lanes] = out_ref[PAD:, :].astype(BF16)
+        gated_ref[:, lanes] = out_ref[PAD : PAD + length, :].astype(BF16)
 
 
 def relative(index, high, order):
@@ -479,7 +483,7 @@
         in_specs=[SMEM, HBM, HBM, HBM, HBM, HBM],
         out_specs=(VMEM, VMEM, VMEM, VMEM),
         scratch_shapes=[
-            pltpu.VMEM((2, EDGE + length, LANES), F32),
+            pltpu.VMEM((2, EDGE + length + SPARE, LANES), F32),
             pltpu.VMEM((tiles, 2, length, LANES), BF16),
             pltpu.VMEM((3, 16, channels), BF16),
             pltpu.VMEM(taps.shape, F32),
@@ -503,7 +507,7 @@
         ),
         in_specs=[SMEM] + [VMEM] * 6 + [HBM],
         out_specs=(VMEM, VMEM, VMEM),
-        scratch_shapes=[pltpu.VMEM((EDGE + length, LANES), F32), pltpu.SemaphoreType.DMA((peers // 2,))],
+        scratch_shapes=[pltpu.VMEM((EDGE + length + SPARE, LANES), F32), pltpu.SemaphoreType.DMA((peers // 2,))],
         compiler_params=pltpu.CompilerParams(vmem_limit_bytes=LIMIT),
         cost_estimate=QUICK,
         name="response",
@@ -518,7 +522,7 @@
         scratch_shapes=[
             pltpu.VMEM((PAD + 16, channels), F32),
             pltpu.VMEM((2 * poles, channels), F32),
-            pltpu.VMEM((PAD + length, LANES), F32),
+            pltpu.VMEM((PAD + length + SPARE, LANES), F32),
             pltpu.VMEM((PAD, channels), F32),
         ],
         compiler_params=pltpu.CompilerParams(vmem_limit_bytes=LIMIT),

time: 58.3 us -> 58.2 us (level)
  no operation moved by 1% of the time
where the time goes in v6:
time: 58.2 us; the launch traced here: 58.1 us
  starting transfers between devices  28.2 us (48%)
  Pallas kernels  17.5 us (30%)
  waiting for transfers between devices  12.1 us (21%)
    ppermute x17, starting transfers between devices, across(): return lax.ppermute(x, 'tp', [(i, i ^ 1 << bit) for i in range(count)])  25.6 us
    ppermute x17, waiting for transfers between devices, across(): return lax.ppermute(x, 'tp', [(i, i ^ 1 << bit) for i in range(count)])  12 us
    pallas_call x4, Pallas kernels, project(): pl.pallas_call(functools.partial(project_kernel, part), out_shape=(jax.Sh...  5.32 us
    pallas_call x1, Pallas kernels, per_device(): pl.pallas_call(driven_kernel, out_shape=(jax.ShapeDtypeStruct(split, F32)...  3.9 us
    pallas_call x1, Pallas kernels, per_device(): pl.pallas_call(response_kernel, out_shape=(jax.ShapeDtypeStruct(split, F3...  2.89 us
    ppermute x1, starting transfers between devices, after(): return lax.ppermute(x, axis, [(i, (i + 1) % count) for i in range(count)])  2.59 us
    pallas_call x1, Pallas kernels, per_device(): pl.pallas_call(gated_kernel, out_shape=jax.ShapeDtypeStruct((length, chan...  1.93 us
  transfers between devices with their start and end apart: 18, of which 11 were waited for; matrix products, arithmetic and copies ran while one was open for 0% of the time, Pallas kernels for 20%

profile of v6, /device:TPU:0, one launch (start us, length us, event | category | flops | bytes accessed | tf_op | source)
XLA Modules:
  0.0 58.1 jit_solution(8132471488022025057)
XLA Ops:
  0.0 0.1 pad_add_fusion.where_ref
  0.1 0.0 copy-start
  0.1 0.0 copy-start.1
  0.1 0.0 copy-start.2
  0.1 0.0 copy-start.4
  0.1 3.9 %driven.1 = (f32[4,49,8,128]{3,2,1,0:T(8,128)S(1)}, f32[4,16,8,128]{3,2,1,0:T(8,128)S(1)}, f32[40,512]{1,0:T(8,128)S(1)}, bf16[8,512,512]{2,1,0:T(8,128)(2,1)S(1)}) custom-call(s32[3]{0:T(128)S(1)} %pad_add_fusion.where_ref, bf16[3,1,384,512]{3,2,1,0:T(8,128)(2,1)} %head_in_ref.1, f32[3,7,512]{2,1,0:T(8,128)} %taps_ref.3, f32[16,512]{1,0:T(8,128)} %decay_ref.3, ...), custom_call_target="tpu_custom_call" | custom-call | flops 1 | bytes 1 | tf_op jit(solution)/shard_map/driven/pallas_call | solution.py:475
  4.0 0.5 collective-permute-start.2
  4.5 2.6 %collective-permute-start = (f32[40,512]{1,0:T(8,128)S(1)}, f32[40,512]{1,0:T(8,128)S(1)}, u32[]{:S(2)}, u32[]{:S(2)}) collective-permute-start(f32[40,512]{1,0:T(8,128)S(1)} %get-tuple-element.42), channel_id=1, source_target_pairs={{0,16},{16,0},{1,17},{17,1},{2,18},{18,2},{3,19},{19,3},{4,20},{20... | collective-permute-start | bytes 245768 | tf_op jit(solution)/shard_map/ppermute | solution.py:436
  7.1 0.0 copy-done
  7.1 0.0 copy-done.1
  7.1 0.0 copy-done.2
  7.1 0.0 copy-done.4
  7.1 0.0 copy-start.3
  7.1 2.9 %response.1 = (f32[4,49,8,128]{3,2,1,0:T(8,128)S(1)}, f32[4,49,8,128]{3,2,1,0:T(8,128)S(1)}, bf16[8,512,512]{2,1,0:T(8,128)(2,1)S(1)}) custom-call(s32[3]{0:T(128)S(1)} %pad_add_fusion.where_ref, bf16[3,1,384,512]{3,2,1,0:T(8,128)(2,1)S(1)} %copy-done, f32[3,7,512]{2,1,0:T(8,128)S(1)} %copy-done.1, f32[16,512]{1,0:T(8,128)S(1)} %copy-done.2, ...), custom_call_target="tpu_custom_call" | custom-call | flops 1 | bytes 1 | tf_op jit(solution)/shard_map/response/pallas_call | solution.py:501
  10.0 0.1 collective-permute-done.message_ref
  10.1 0.0 copy-done.3
  10.2 1.9 %gated.1.own_ref = bf16[384,512]{1,0:T(8,128)(2,1)S(1)} custom-call(s32[3]{0:T(128)S(1)} %pad_add_fusion.where_ref, f32[40,512]{1,0:T(8,128)S(1)} %collective-permute-done.message_ref, bf16[3,1,384,512]{3,2,1,0:T(8,128)(2,1)S(1)} %copy-done, f32[3,7,512]{2,1,0:T(8,128)S(1)} %copy-done.1, f32[16,512]{1,0:T(8,128)S(1)} %copy-done.2, f32[16,512]{1,0:T(8,128)S(1)} %copy-done.4, ...), custom_call_target="tpu_custom_call" | custom-call | flops 1 | bytes 1 | tf_op jit(solution)/shard_map/gated/pallas_call | solution.py:517
  12.1 0.1 collective-permute-start.1
  12.2 1.1 %project_own.1.sum_ref = f32[4,384,256]{2,1,0:T(8,128)S(1)} custom-call(s32[3]{0:T(128)S(1)} %pad_add_fusion.where_ref, bf16[384,512]{1,0:T(8,128)(2,1)S(1)} %gated.1.own_ref, bf16[8,512,512]{2,1,0:T(8,128)(2,1)S(1)} %get-tuple-element.47.mine_ref), custom_call_target="tpu_custom_call" | custom-call | flops 1 | bytes 1 | tf_op jit(solution)/shard_map/project_own/pallas_call | solution.py:350
  13.4 0.5 collective-permute-done.1.other_ref
  13.9 0.0 collective-permute-done.2.theirs_ref
  13.9 1.1 %project_other.1 = (bf16[4,384,128]{2,1,0:T(8,128)(2,1)S(1)}, f32[4,384,128]{2,1,0:T(8,128)S(1)}) custom-call(s32[3]{0:T(128)S(1)} %pad_add_fusion.where_ref, f32[4,384,256]{2,1,0:T(8,128)S(1)} %project_own.1.sum_ref, bf16[384,512]{1,0:T(8,128)(2,1)S(1)} %collective-permute-done.1.other_ref, bf16[8,512,512]{2,1,0:T(8,128)(2,1)S(1)} %collective-permute-done.2.theirs_ref), custom_call_target="tpu_custom_call" | custom-call | flops 1 | bytes 1 | tf_op jit(solution)/shard_map/project_other/pallas_call | solution.py:364
  15.0 1.8 %collective-permute-start.3 = (bf16[4,384,128]{2,1,0:T(8,128)(2,1)S(1)}, bf16[4,384,128]{2,1,0:T(8,128)(2,1)S(1)}, u32[]{:S(2)}, u32[]{:S(2)}) collective-permute-start(bf16[4,384,128]{2,1,0:T(8,128)(2,1)S(1)} %get-tuple-element.50.order_ref), channel_id=1, source_target_pairs={{0,2},{1,3},{2,0},{3,1},{4,6},{5,7},{6,4},{7,5},{8,10},{9,11},{10,... | collective-permute-start | bytes 1179656 | tf_op jit(solution)/shard_map/ppermute | solution.py:431
  16.8 1.5 %project.4 = (bf16[4,384,128]{2,1,0:T(8,128)(2,1)S(1)}, f32[4,384,128]{2,1,0:T(8,128)S(1)}) custom-call(s32[3]{0:T(128)S(1)} %pad_add_fusion.where_ref, bf16[384,512]{1,0:T(8,128)(2,1)S(1)} %gated.1.own_ref, bf16[384,512]{1,0:T(8,128)(2,1)S(1)} %collective-permute-done.1.other_ref, bf16[8,512,512]{2,1,0:T(8,128)(2,1)S(1)} %get-tuple-element.47.mine_ref, ...), custom_call_target="tpu_custom_call" | custom-call | flops 1 | bytes 1 | tf_op jit(solution)/shard_map/project/pallas_call | solution.py:337
  18.3 1.6 %collective-permute-start.6 = (bf16[4,384,128]{2,1,0:T(8,128)(2,1)S(1)}, bf16[4,384,128]{2,1,0:T(8,128)(2,1)S(1)}, u32[]{:S(2)}, u32[]{:S(2)}) collective-permute-start(bf16[4,384,128]{2,1,0:T(8,128)(2,1)S(1)} %get-tuple-element.51.order_ref), channel_id=1, source_target_pairs={{0,4},{1,5},{2,6},{3,7},{4,0},{5,1},{6,2},{7,3},{8,12},{9,13},{10,... | collective-permute-start | bytes 1179656 | tf_op jit(solution)/shard_map/ppermute | solution.py:431
  20.0 1.5 %project.5 = (bf16[4,384,128]{2,1,0:T(8,128)(2,1)S(1)}, f32[4,384,128]{2,1,0:T(8,128)S(1)}) custom-call(s32[3]{0:T(128)S(1)} %pad_add_fusion.where_ref, bf16[384,512]{1,0:T(8,128)(2,1)S(1)} %gated.1.own_ref, bf16[384,512]{1,0:T(8,128)(2,1)S(1)} %collective-permute-done.1.other_ref, bf16[8,512,512]{2,1,0:T(8,128)(2,1)S(1)} %get-tuple-element.47.mine_ref, ...), custom_call_target="tpu_custom_call" | custom-call | flops 1 | bytes 1 | tf_op jit(solution)/shard_map/project/pallas_call | solution.py:337
  21.5 0.6 %collective-permute-start.5 = (bf16[4,384,128]{2,1,0:T(8,128)(2,1)S(1)}, bf16[4,384,128]{2,1,0:T(8,128)(2,1)S(1)}, u32[]{:S(2)}, u32[]{:S(2)}) collective-permute-start(bf16[4,384,128]{2,1,0:T(8,128)(2,1)S(1)} %get-tuple-element.52.order_ref), channel_id=1, source_target_pairs={{0,2},{1,3},{2,0},{3,1},{4,6},{5,7},{6,4},{7,5},{8,10},{9,11},{10,... | collective-permute-start | bytes 1179656 | tf_op jit(solution)/shard_map/ppermute | solution.py:431
  22.1 1.3 %project.6 = (bf16[4,256,128]{2,1,0:T(8,128)(2,1)S(1)}, f32[4,256,128]{2,1,0:T(8,128)S(1)}) custom-call(s32[3]{0:T(128)S(1)} %pad_add_fusion.where_ref, bf16[384,512]{1,0:T(8,128)(2,1)S(1)} %gated.1.own_ref, bf16[384,512]{1,0:T(8,128)(2,1)S(1)} %collective-permute-done.1.other_ref, bf16[8,512,512]{2,1,0:T(8,128)(2,1)S(1)} %get-tuple-element.47.mine_ref, ...), custom_call_target="tpu_custom_call" | custom-call | flops 1 | bytes 1 | tf_op jit(solution)/shard_map/project/pallas_call | solution.py:337
  23.4 1.6 %collective-permute-start.10 = (bf16[4,256,128]{2,1,0:T(8,128)(2,1)S(1)}, bf16[4,256,128]{2,1,0:T(8,128)(2,1)S(1)}, u32[]{:S(2)}, u32[]{:S(2)}) collective-permute-start(bf16[4,256,128]{2,1,0:T(8,128)(2,1)S(1)} %get-tuple-element.53.order_ref), channel_id=1, source_target_pairs={{0,2},{1,3},{2,0},{3,1},{4,6},{5,7},{6,4},{7,5},{8,10},{9,11},{10,... | collective-permute-start | bytes 786440 | tf_op jit(solution)/shard_map/ppermute | solution.py:431
  24.9 1.0 %project.7 = (bf16[4,128,128]{2,1,0:T(8,128)(2,1)S(1)}, f32[4,128,128]{2,1,0:T(8,128)S(1)}) custom-call(s32[3]{0:T(128)S(1)} %pad_add_fusion.where_ref, bf16[384,512]{1,0:T(8,128)(2,1)S(1)} %gated.1.own_ref, bf16[384,512]{1,0:T(8,128)(2,1)S(1)} %collective-permute-done.1.other_ref, bf16[8,512,512]{2,1,0:T(8,128)(2,1)S(1)} %get-tuple-element.47.mine_ref, ...), custom_call_target="tpu_custom_call" | custom-call | flops 1 | bytes 1 | tf_op jit(solution)/shard_map/project/pallas_call | solution.py:337
  26.0 1.1 %collective-permute-done.3.received_ref = bf16[4,384,128]{2,1,0:T(8,128)(2,1)S(1)} collective-permute-done((bf16[4,384,128]{2,1,0:T(8,128)(2,1)S(1)}, bf16[4,384,128]{2,1,0:T(8,128)(2,1)S(1)}, u32[]{:S(2)}, u32[]{:S(2)}) %collective-permute-start.3) | collective-permute-done | bytes 393248 | tf_op jit(solution)/shard_map/ppermute | solution.py:431
  27.0 0.1 merge.10
  27.1 1.9 %collective-permute-start.4 = (bf16[2,384,128]{2,1,0:T(8,128)(2,1)S(1)}, bf16[2,384,128]{2,1,0:T(8,128)(2,1)S(1)}, u32[]{:S(2)}, u32[]{:S(2)}) collective-permute-start(bf16[2,384,128]{2,1,0:T(8,128)(2,1)S(1)} %get-tuple-element.56.order_ref), channel_id=1, source_target_pairs={{0,4},{1,5},{2,6},{3,7},{4,0},{5,1},{6,2},{7,3},{8,12},{9,13},{10,... | collective-permute-start | bytes 589832 | tf_op jit(solution)/shard_map/ppermute | solution.py:431
  29.0 1.2 %collective-permute-done.6.received_ref = bf16[4,384,128]{2,1,0:T(8,128)(2,1)S(1)} collective-permute-done((bf16[4,384,128]{2,1,0:T(8,128)(2,1)S(1)}, bf16[4,384,128]{2,1,0:T(8,128)(2,1)S(1)}, u32[]{:S(2)}, u32[]{:S(2)}) %collective-permute-start.6) | collective-permute-done | bytes 393248 | tf_op jit(solution)/shard_map/ppermute | solution.py:431
  30.2 0.1 merge.11
  30.2 2.5 %collective-permute-start.11 = (bf16[2,384,128]{2,1,0:T(8,128)(2,1)S(1)}, bf16[2,384,128]{2,1,0:T(8,128)(2,1)S(1)}, u32[]{:S(2)}, u32[]{:S(2)}) collective-permute-start(bf16[2,384,128]{2,1,0:T(8,128)(2,1)S(1)} %get-tuple-element.59.order_ref), channel_id=1, source_target_pairs={{0,8},{1,9},{2,10},{3,11},{4,12},{5,13},{6,14},{7,15},{8,0},{9,1},... | collective-permute-start | bytes 589832 | tf_op jit(solution)/shard_map/ppermute | solution.py:431
  32.7 2.8 %collective-permute-done.5.received_ref = bf16[4,384,128]{2,1,0:T(8,128)(2,1)S(1)} collective-permute-done((bf16[4,384,128]{2,1,0:T(8,128)(2,1)S(1)}, bf16[4,384,128]{2,1,0:T(8,128)(2,1)S(1)}, u32[]{:S(2)}, u32[]{:S(2)}) %collective-permute-start.5) | collective-permute-done | bytes 393248 | tf_op jit(solution)/shard_map/ppermute | solution.py:431
  35.5 0.1 merge.12
  35.5 1.9 %collective-permute-start.9 = (bf16[2,384,128]{2,1,0:T(8,128)(2,1)S(1)}, bf16[2,384,128]{2,1,0:T(8,128)(2,1)S(1)}, u32[]{:S(2)}, u32[]{:S(2)}) collective-permute-start(bf16[2,384,128]{2,1,0:T(8,128)(2,1)S(1)} %get-tuple-element.60.order_ref), channel_id=1, source_target_pairs={{0,4},{1,5},{2,6},{3,7},{4,0},{5,1},{6,2},{7,3},{8,12},{9,13},{10,... | collective-permute-start | bytes 589832 | tf_op jit(solution)/shard_map/ppermute | solution.py:431
  37.4 1.5 %collective-permute-start.8 = (bf16[4,128,128]{2,1,0:T(8,128)(2,1)S(1)}, bf16[4,128,128]{2,1,0:T(8,128)(2,1)S(1)}, u32[]{:S(2)}, u32[]{:S(2)}) collective-permute-start(bf16[4,128,128]{2,1,0:T(8,128)(2,1)S(1)} %get-tuple-element.54.order_ref), channel_id=1, source_target_pairs={{0,2},{1,3},{2,0},{3,1},{4,6},{5,7},{6,4},{7,5},{8,10},{9,11},{10,... | collective-permute-start | bytes 393224 | tf_op jit(solution)/shard_map/ppermute | solution.py:431
  38.9 0.0 collective-permute-done.4.received_ref
  39.0 1.7 %collective-permute-done.11.received_ref = bf16[2,384,128]{2,1,0:T(8,128)(2,1)S(1)} collective-permute-done((bf16[2,384,128]{2,1,0:T(8,128)(2,1)S(1)}, bf16[2,384,128]{2,1,0:T(8,128)(2,1)S(1)}, u32[]{:S(2)}, u32[]{:S(2)}) %collective-permute-start.11) | collective-permute-done | bytes 196640 | tf_op jit(solution)/shard_map/ppermute | solution.py:431
  40.7 0.4 collective-permute-done.10.received_ref
  41.1 1.9 %collective-permute-start.13 = (bf16[2,256,128]{2,1,0:T(8,128)(2,1)S(1)}, bf16[2,256,128]{2,1,0:T(8,128)(2,1)S(1)}, u32[]{:S(2)}, u32[]{:S(2)}) collective-permute-start(bf16[2,256,128]{2,1,0:T(8,128)(2,1)S(1)} %get-tuple-element.68.order_ref), channel_id=1, source_target_pairs={{0,4},{1,5},{2,6},{3,7},{4,0},{5,1},{6,2},{7,3},{8,12},{9,13},{10,... | collective-permute-start | bytes 393224 | tf_op jit(solution)/shard_map/ppermute | solution.py:431
  43.0 2.6 %collective-permute-start.7 = (bf16[1,384,128]{2,1,0:T(8,128)(2,1)S(1)}, bf16[1,384,128]{2,1,0:T(8,128)(2,1)S(1)}, u32[]{:S(2)}, u32[]{:S(2)}) collective-permute-start(bf16[1,384,128]{2,1,0:T(8,128)(2,1)S(1)} %get-tuple-element.62.order_ref), channel_id=1, source_target_pairs={{0,8},{1,9},{2,10},{3,11},{4,12},{5,13},{6,14},{7,15},{8,0},{9,1},... | collective-permute-start | bytes 294920 | tf_op jit(solution)/shard_map/ppermute | solution.py:431
  45.6 0.0 collective-permute-done.9.received_ref
  45.6 1.8 %collective-permute-start.14 = (bf16[1,384,128]{2,1,0:T(8,128)(2,1)S(1)}, bf16[1,384,128]{2,1,0:T(8,128)(2,1)S(1)}, u32[]{:S(2)}, u32[]{:S(2)}) collective-permute-start(bf16[1,384,128]{2,1,0:T(8,128)(2,1)S(1)} %get-tuple-element.69.order_ref), channel_id=1, source_target_pairs={{0,8},{1,9},{2,10},{3,11},{4,12},{5,13},{6,14},{7,15},{8,0},{9,1},... | collective-permute-start | bytes 294920 | tf_op jit(solution)/shard_map/ppermute | solution.py:431
  47.5 0.0 collective-permute-done.8.received_ref
  47.5 2.5 %collective-permute-start.12 = (bf16[2,128,128]{2,1,0:T(8,128)(2,1)S(1)}, bf16[2,128,128]{2,1,0:T(8,128)(2,1)S(1)}, u32[]{:S(2)}, u32[]{:S(2)}) collective-permute-start(bf16[2,128,128]{2,1,0:T(8,128)(2,1)S(1)} %get-tuple-element.71.order_ref), channel_id=1, source_target_pairs={{0,4},{1,5},{2,6},{3,7},{4,0},{5,1},{6,2},{7,3},{8,12},{9,13},{10,... | collective-permute-start | bytes 196616 | tf_op jit(solution)/shard_map/ppermute | solution.py:431
  50.0 0.0 collective-permute-start.16
  50.0 0.0 collective-permute-done.13.received_ref
  50.1 0.8 %collective-permute-start.15 = (bf16[1,256,128]{2,1,0:T(8,128)(2,1)S(1)}, bf16[1,256,128]{2,1,0:T(8,128)(2,1)S(1)}, u32[]{:S(2)}, u32[]{:S(2)}) collective-permute-start(bf16[1,256,128]{2,1,0:T(8,128)(2,1)S(1)} %get-tuple-element.73.order_ref), channel_id=1, source_target_pairs={{0,8},{1,9},{2,10},{3,11},{4,12},{5,13},{6,14},{7,15},{8,0},{9,1},... | collective-permute-start | bytes 196616 | tf_op jit(solution)/shard_map/ppermute | solution.py:431
  50.8 1.5 %collective-permute-done.12.received_ref = bf16[2,128,128]{2,1,0:T(8,128)(2,1)S(1)} collective-permute-done((bf16[2,128,128]{2,1,0:T(8,128)(2,1)S(1)}, bf16[2,128,128]{2,1,0:T(8,128)(2,1)S(1)}, u32[]{:S(2)}, u32[]{:S(2)}) %collective-permute-start.12) | collective-permute-done | bytes 65568 | tf_op jit(solution)/shard_map/ppermute | solution.py:431
  52.3 2.0 %collective-permute-start.17 = (bf16[1,128,128]{2,1,0:T(8,128)(2,1)S(1)}, bf16[1,128,128]{2,1,0:T(8,128)(2,1)S(1)}, u32[]{:S(2)}, u32[]{:S(2)}) collective-permute-start(bf16[1,128,128]{2,1,0:T(8,128)(2,1)S(1)} %get-tuple-element.74.order_ref), channel_id=1, source_target_pairs={{0,8},{1,9},{2,10},{3,11},{4,12},{5,13},{6,14},{7,15},{8,0},{9,1},... | collective-permute-start | bytes 98312 | tf_op jit(solution)/shard_map/ppermute | solution.py:431
  54.3 0.0 collective-permute-done.7.received_ref
  54.4 1.9 %collective-permute-done.14.received_ref = bf16[1,384,128]{2,1,0:T(8,128)(2,1)S(1)} collective-permute-done((bf16[1,384,128]{2,1,0:T(8,128)(2,1)S(1)}, bf16[1,384,128]{2,1,0:T(8,128)(2,1)S(1)}, u32[]{:S(2)}, u32[]{:S(2)}) %collective-permute-start.14) | collective-permute-done | bytes 98336 | tf_op jit(solution)/shard_map/ppermute | solution.py:431
  56.3 0.7 %collective-permute-done.15.received_ref = bf16[1,256,128]{2,1,0:T(8,128)(2,1)S(1)} collective-permute-done((bf16[1,256,128]{2,1,0:T(8,128)(2,1)S(1)}, bf16[1,256,128]{2,1,0:T(8,128)(2,1)S(1)}, u32[]{:S(2)}, u32[]{:S(2)}) %collective-permute-start.15) | collective-permute-done | bytes 65568 | tf_op jit(solution)/shard_map/ppermute | solution.py:431
  57.0 0.0 collective-permute-done.16.received_ref
  57.0 0.3 collective-permute-done.17.refs_5_
  57.3 0.8 %gather.1 = bf16[1,384,512]{2,1,0:T(8,128)(2,1)} custom-call(bf16[384,128]{1,0:T(8,128)(2,1)S(1)} %finish.4.order_ref.refs_0_, bf16[384,128]{1,0:T(8,128)(2,1)S(1)} %finish.5.order_ref.refs_1_, bf16[256,128]{1,0:T(8,128)(2,1)S(1)} %finish.6.order_ref.refs_2_, bf16[384,128]{1,0:T(8,128)(2,1)S(1)} %finish.7.refs_3_.refs_6_, ...), custom_call_target="tpu_custom_call" | custom-call | flops 1 | bytes 1 | tf_op jit(solution)/shard_map/gather/pallas_call | solution.py:402
  (11 shorter events, 0.3 us)
Async XLA Ops:
  0.1 7.0 %copy-start = (bf16[3,1,384,512]{3,2,1,0:T(8,128)(2,1)S(1)}, bf16[3,1,384,512]{3,2,1,0:T(8,128)(2,1)}, u32[]{:S(2)}) copy-start(bf16[3,1,384,512]{3,2,1,0:T(8,128)(2,1)} %head_in_ref.1) | copy-start | bytes 3538948
  0.1 7.0 %copy-start.1 = (f32[3,7,512]{2,1,0:T(8,128)S(1)}, f32[3,7,512]{2,1,0:T(8,128)}, u32[]{:S(2)}) copy-start(f32[3,7,512]{2,1,0:T(8,128)} %taps_ref.3) | copy-start | bytes 129028
  0.1 7.0 %copy-start.2 = (f32[16,512]{1,0:T(8,128)S(1)}, f32[16,512]{1,0:T(8,128)}, u32[]{:S(2)}) copy-start(f32[16,512]{1,0:T(8,128)} %decay_ref.3) | copy-start | bytes 98308
  0.1 7.0 %copy-start.4 = (f32[16,512]{1,0:T(8,128)S(1)}, f32[16,512]{1,0:T(8,128)}, u32[]{:S(2)}) copy-start(f32[16,512]{1,0:T(8,128)} %residues_ref.3) | copy-start | bytes 98308
  4.0 9.9 %collective-permute-start.2 = (bf16[8,512,512]{2,1,0:T(8,128)(2,1)S(1)}, bf16[8,512,512]{2,1,0:T(8,128)(2,1)S(1)}, u32[]{:S(2)}, u32[]{:S(2)}) collective-permute-start(bf16[8,512,512]{2,1,0:T(8,128)(2,1)S(1)} %get-tuple-element.48), channel_id=1, source_target_pairs={{0,1},{1,0},{2,3},{3,2},{4,5},{5,4},{6,7},{7,6},{8,9},{9,8},{10,11... | collective-permute-start | bytes 12582920 | tf_op jit(solution)/shard_map/ppermute | solution.py:431
  4.5 5.6 %collective-permute-start = (f32[40,512]{1,0:T(8,128)S(1)}, f32[40,512]{1,0:T(8,128)S(1)}, u32[]{:S(2)}, u32[]{:S(2)}) collective-permute-start(f32[40,512]{1,0:T(8,128)S(1)} %get-tuple-element.42), channel_id=1, source_target_pairs={{0,16},{16,0},{1,17},{17,1},{2,18},{18,2},{3,19},{19,3},{4,20},{20... | collective-permute-start | bytes 245768 | tf_op jit(solution)/shard_map/ppermute | solution.py:436
  7.1 3.0 %copy-start.3 = (f32[1,16,512]{2,1,0:T(8,128)S(1)}, f32[1,16,512]{2,1,0:T(8,128)}, u32[]{:S(2)}) copy-start(f32[1,16,512]{2,1,0:T(8,128)} %init_ref.1) | copy-start | bytes 98308
  12.1 1.8 %collective-permute-start.1 = (bf16[384,512]{1,0:T(8,128)(2,1)S(1)}, bf16[384,512]{1,0:T(8,128)(2,1)S(1)}, u32[]{:S(2)}, u32[]{:S(2)}) collective-permute-start(bf16[384,512]{1,0:T(8,128)(2,1)S(1)} %gated.1.own_ref), channel_id=1, source_target_pairs={{0,1},{1,0},{2,3},{3,2},{4,5},{5,4},{6,7},{7,6},{8,9},{9,8},{10,11... | collective-permute-start | bytes 1179656 | tf_op jit(solution)/shard_map/ppermute | solution.py:431
  15.0 12.0 %collective-permute-start.3 = (bf16[4,384,128]{2,1,0:T(8,128)(2,1)S(1)}, bf16[4,384,128]{2,1,0:T(8,128)(2,1)S(1)}, u32[]{:S(2)}, u32[]{:S(2)}) collective-permute-start(bf16[4,384,128]{2,1,0:T(8,128)(2,1)S(1)} %get-tuple-element.50.order_ref), channel_id=1, source_target_pairs={{0,2},{1,3},{2,0},{3,1},{4,6},{5,7},{6,4},{7,5},{8,10},{9,11},{10,... | collective-permute-start | bytes 1179656 | tf_op jit(solution)/shard_map/ppermute | solution.py:431
  18.3 11.8 %collective-permute-start.6 = (bf16[4,384,128]{2,1,0:T(8,128)(2,1)S(1)}, bf16[4,384,128]{2,1,0:T(8,128)(2,1)S(1)}, u32[]{:S(2)}, u32[]{:S(2)}) collective-permute-start(bf16[4,384,128]{2,1,0:T(8,128)(2,1)S(1)} %get-tuple-element.51.order_ref), channel_id=1, source_target_pairs={{0,4},{1,5},{2,6},{3,7},{4,0},{5,1},{6,2},{7,3},{8,12},{9,13},{10,... | collective-permute-start | bytes 1179656 | tf_op jit(solution)/shard_map/ppermute | solution.py:431
  21.5 13.9 %collective-permute-start.5 = (bf16[4,384,128]{2,1,0:T(8,128)(2,1)S(1)}, bf16[4,384,128]{2,1,0:T(8,128)(2,1)S(1)}, u32[]{:S(2)}, u32[]{:S(2)}) collective-permute-start(bf16[4,384,128]{2,1,0:T(8,128)(2,1)S(1)} %get-tuple-element.52.order_ref), channel_id=1, source_target_pairs={{0,2},{1,3},{2,0},{3,1},{4,6},{5,7},{6,4},{7,5},{8,10},{9,11},{10,... | collective-permute-start | bytes 1179656 | tf_op jit(solution)/shard_map/ppermute | solution.py:431
  23.4 17.7 %collective-permute-start.10 = (bf16[4,256,128]{2,1,0:T(8,128)(2,1)S(1)}, bf16[4,256,128]{2,1,0:T(8,128)(2,1)S(1)}, u32[]{:S(2)}, u32[]{:S(2)}) collective-permute-start(bf16[4,256,128]{2,1,0:T(8,128)(2,1)S(1)} %get-tuple-element.53.order_ref), channel_id=1, source_target_pairs={{0,2},{1,3},{2,0},{3,1},{4,6},{5,7},{6,4},{7,5},{8,10},{9,11},{10,... | collective-permute-start | bytes 786440 | tf_op jit(solution)/shard_map/ppermute | solution.py:431
  27.1 11.8 %collective-permute-start.4 = (bf16[2,384,128]{2,1,0:T(8,128)(2,1)S(1)}, bf16[2,384,128]{2,1,0:T(8,128)(2,1)S(1)}, u32[]{:S(2)}, u32[]{:S(2)}) collective-permute-start(bf16[2,384,128]{2,1,0:T(8,128)(2,1)S(1)} %get-tuple-element.56.order_ref), channel_id=1, source_target_pairs={{0,4},{1,5},{2,6},{3,7},{4,0},{5,1},{6,2},{7,3},{8,12},{9,13},{10,... | collective-permute-start | bytes 589832 | tf_op jit(solution)/shard_map/ppermute | solution.py:431
  30.2 10.5 %collective-permute-start.11 = (bf16[2,384,128]{2,1,0:T(8,128)(2,1)S(1)}, bf16[2,384,128]{2,1,0:T(8,128)(2,1)S(1)}, u32[]{:S(2)}, u32[]{:S(2)}) collective-permute-start(bf16[2,384,128]{2,1,0:T(8,128)(2,1)S(1)} %get-tuple-element.59.order_ref), channel_id=1, source_target_pairs={{0,8},{1,9},{2,10},{3,11},{4,12},{5,13},{6,14},{7,15},{8,0},{9,1},... | collective-permute-start | bytes 589832 | tf_op jit(solution)/shard_map/ppermute | solution.py:431
  35.5 10.1 %collective-permute-start.9 = (bf16[2,384,128]{2,1,0:T(8,128)(2,1)S(1)}, bf16[2,384,128]{2,1,0:T(8,128)(2,1)S(1)}, u32[]{:S(2)}, u32[]{:S(2)}) collective-permute-start(bf16[2,384,128]{2,1,0:T(8,128)(2,1)S(1)} %get-tuple-element.60.order_ref), channel_id=1, source_target_pairs={{0,4},{1,5},{2,6},{3,7},{4,0},{5,1},{6,2},{7,3},{8,12},{9,13},{10,... | collective-permute-start | bytes 589832 | tf_op jit(solution)/shard_map/ppermute | solution.py:431
  37.4 10.1 %collective-permute-start.8 = (bf16[4,128,128]{2,1,0:T(8,128)(2,1)S(1)}, bf16[4,128,128]{2,1,0:T(8,128)(2,1)S(1)}, u32[]{:S(2)}, u32[]{:S(2)}) collective-permute-start(bf16[4,128,128]{2,1,0:T(8,128)(2,1)S(1)} %get-tuple-element.54.order_ref), channel_id=1, source_target_pairs={{0,2},{1,3},{2,0},{3,1},{4,6},{5,7},{6,4},{7,5},{8,10},{9,11},{10,... | collective-permute-start | bytes 393224 | tf_op jit(solution)/shard_map/ppermute | solution.py:431
  41.1 8.9 %collective-permute-start.13 = (bf16[2,256,128]{2,1,0:T(8,128)(2,1)S(1)}, bf16[2,256,128]{2,1,0:T(8,128)(2,1)S(1)}, u32[]{:S(2)}, u32[]{:S(2)}) collective-permute-start(bf16[2,256,128]{2,1,0:T(8,128)(2,1)S(1)} %get-tuple-element.68.order_ref), channel_id=1, source_target_pairs={{0,4},{1,5},{2,6},{3,7},{4,0},{5,1},{6,2},{7,3},{8,12},{9,13},{10,... | collective-permute-start | bytes 393224 | tf_op jit(solution)/shard_map/ppermute | solution.py:431
  43.0 11.3 %collective-permute-start.7 = (bf16[1,384,128]{2,1,0:T(8,128)(2,1)S(1)}, bf16[1,384,128]{2,1,0:T(8,128)(2,1)S(1)}, u32[]{:S(2)}, u32[]{:S(2)}) collective-permute-start(bf16[1,384,128]{2,1,0:T(8,128)(2,1)S(1)} %get-tuple-element.62.order_ref), channel_id=1, source_target_pairs={{0,8},{1,9},{2,10},{3,11},{4,12},{5,13},{6,14},{7,15},{8,0},{9,1},... | collective-permute-start | bytes 294920 | tf_op jit(solution)/shard_map/ppermute | solution.py:431
  45.6 10.6 %collective-permute-start.14 = (bf16[1,384,128]{2,1,0:T(8,128)(2,1)S(1)}, bf16[1,384,128]{2,1,0:T(8,128)(2,1)S(1)}, u32[]{:S(2)}, u32[]{:S(2)}) collective-permute-start(bf16[1,384,128]{2,1,0:T(8,128)(2,1)S(1)} %get-tuple-element.69.order_ref), channel_id=1, source_target_pairs={{0,8},{1,9},{2,10},{3,11},{4,12},{5,13},{6,14},{7,15},{8,0},{9,1},... | collective-permute-start | bytes 294920 | tf_op jit(solution)/shard_map/ppermute | solution.py:431
  47.5 4.8 %collective-permute-start.12 = (bf16[2,128,128]{2,1,0:T(8,128)(2,1)S(1)}, bf16[2,128,128]{2,1,0:T(8,128)(2,1)S(1)}, u32[]{:S(2)}, u32[]{:S(2)}) collective-permute-start(bf16[2,128,128]{2,1,0:T(8,128)(2,1)S(1)} %get-tuple-element.71.order_ref), channel_id=1, source_target_pairs={{0,4},{1,5},{2,6},{3,7},{4,0},{5,1},{6,2},{7,3},{8,12},{9,13},{10,... | collective-permute-start | bytes 196616 | tf_op jit(solution)/shard_map/ppermute | solution.py:431
  50.0 6.9 %collective-permute-start.16 = (bf16[1,384,128]{2,1,0:T(8,128)(2,1)S(1)}, bf16[1,384,128]{2,1,0:T(8,128)(2,1)S(1)}, u32[]{:S(2)}, u32[]{:S(2)}) collective-permute-start(bf16[1,384,128]{2,1,0:T(8,128)(2,1)S(1)} %get-tuple-element.67.order_ref), channel_id=1, source_target_pairs={{0,2},{1,3},{2,0},{3,1},{4,6},{5,7},{6,4},{7,5},{8,10},{9,11},{10,... | collective-permute-start | bytes 294920 | tf_op jit(solution)/shard_map/ppermute | solution.py:431
  50.1 6.9 %collective-permute-start.15 = (bf16[1,256,128]{2,1,0:T(8,128)(2,1)S(1)}, bf16[1,256,128]{2,1,0:T(8,128)(2,1)S(1)}, u32[]{:S(2)}, u32[]{:S(2)}) collective-permute-start(bf16[1,256,128]{2,1,0:T(8,128)(2,1)S(1)} %get-tuple-element.73.order_ref), channel_id=1, source_target_pairs={{0,8},{1,9},{2,10},{3,11},{4,12},{5,13},{6,14},{7,15},{8,0},{9,1},... | collective-permute-start | bytes 196616 | tf_op jit(solution)/shard_map/ppermute | solution.py:431
  52.3 5.0 %collective-permute-start.17 = (bf16[1,128,128]{2,1,0:T(8,128)(2,1)S(1)}, bf16[1,128,128]{2,1,0:T(8,128)(2,1)S(1)}, u32[]{:S(2)}, u32[]{:S(2)}) collective-permute-start(bf16[1,128,128]{2,1,0:T(8,128)(2,1)S(1)} %get-tuple-element.74.order_ref), channel_id=1, source_target_pairs={{0,8},{1,9},{2,10},{3,11},{4,12},{5,13},{6,14},{7,15},{8,0},{9,1},... | collective-permute-start | bytes 98312 | tf_op jit(solution)/shard_map/ppermute | solution.py:431

commit v7 on v6

--- a/solution.py
+++ b/solution.py
@@ -176,7 +176,8 @@
                 response_ref[tile, b * turn + step] = tree_sum([r * s for r, s in zip(weights, states)])
             return tuple(states)
 
-        lax.fori_loop(0, seg_len // turn, scan, tuple(states))
+        for b in range(seg_len // turn):
+            states = scan(b, states)
     for copy in copies:
         copy.wait()
 
@@ -230,7 +231,8 @@
                 out_ref[pl.ds(at, SEGS, stride=seg_len), :] = total * query_ref[tile, at]
             return tuple(states)
 
-        lax.fori_loop(0, seg_len // turn, block, tuple(states))
+        for b in range(seg_len // turn):
+            states = block(b, states)
         for j in range(lag):
             total = response_ref[tile, PAD + j, 0:1, :] + early_ref[j : j + 1, lanes]
             out_ref[PAD + j : PAD + j + 1, :] = total * head_query[j : j + 1, lanes]

time: 58.2 us -> 58.1 us (level)
  no operation moved by 1% of the time
where the time goes in v7:
time: 58.1 us; the launch traced here: 57.9 us
  starting transfers between devices  28.1 us (48%)
  Pallas kernels  17.3 us (30%)
  waiting for transfers between devices  12.2 us (21%)
    ppermute x17, starting transfers between devices, across(): return lax.ppermute(x, 'tp', [(i, i ^ 1 << bit) for i in range(count)])  25.5 us
    ppermute x17, waiting for transfers between devices, across(): return lax.ppermute(x, 'tp', [(i, i ^ 1 << bit) for i in range(count)])  12 us
    pallas_call x4, Pallas kernels, project(): pl.pallas_call(functools.partial(project_kernel, part), out_shape=(jax.Sh...  5.32 us
    pallas_call x1, Pallas kernels, per_device(): pl.pallas_call(driven_kernel, out_shape=(jax.ShapeDtypeStruct(split, F32)...  3.9 us
    pallas_call x1, Pallas kernels, per_device(): pl.pallas_call(response_kernel, out_shape=(jax.ShapeDtypeStruct(split, F3...  2.82 us
    ppermute x1, starting transfers between devices, after(): return lax.ppermute(x, axis, [(i, (i + 1) % count) for i in range(count)])  2.59 us
    pallas_call x1, Pallas kernels, per_device(): pl.pallas_call(gated_kernel, out_shape=jax.ShapeDtypeStruct((length, chan...  1.76 us
  transfers between devices with their start and end apart: 18, of which 11 were waited for; matrix products, arithmetic and copies ran while one was open for 0% of the time, Pallas kernels for 20%

profile of v7, /device:TPU:0, one launch (start us, length us, event | category | flops | bytes accessed | tf_op | source)
XLA Modules:
  0.0 57.9 jit_solution(15238570959651935906)
XLA Ops:
  0.0 0.1 pad_add_fusion.where_ref
  0.1 0.0 copy-start
  0.1 0.0 copy-start.1
  0.1 0.0 copy-start.2
  0.1 0.0 copy-start.4
  0.1 3.9 %driven.1 = (f32[4,49,8,128]{3,2,1,0:T(8,128)S(1)}, f32[4,16,8,128]{3,2,1,0:T(8,128)S(1)}, f32[40,512]{1,0:T(8,128)S(1)}, bf16[8,512,512]{2,1,0:T(8,128)(2,1)S(1)}) custom-call(s32[3]{0:T(128)S(1)} %pad_add_fusion.where_ref, bf16[3,1,384,512]{3,2,1,0:T(8,128)(2,1)} %head_in_ref.1, f32[3,7,512]{2,1,0:T(8,128)} %taps_ref.3, f32[16,512]{1,0:T(8,128)} %decay_ref.3, ...), custom_call_target="tpu_custom_call" | custom-call | flops 1 | bytes 1 | tf_op jit(solution)/shard_map/driven/pallas_call | solution.py:477
  4.0 0.5 collective-permute-start.2
  4.5 2.6 %collective-permute-start = (f32[40,512]{1,0:T(8,128)S(1)}, f32[40,512]{1,0:T(8,128)S(1)}, u32[]{:S(2)}, u32[]{:S(2)}) collective-permute-start(f32[40,512]{1,0:T(8,128)S(1)} %get-tuple-element.42), channel_id=1, source_target_pairs={{0,16},{16,0},{1,17},{17,1},{2,18},{18,2},{3,19},{19,3},{4,20},{20... | collective-permute-start | bytes 245768 | tf_op jit(solution)/shard_map/ppermute | solution.py:438
  7.1 0.0 copy-done
  7.1 0.0 copy-done.1
  7.1 0.0 copy-done.2
  7.1 0.0 copy-done.4
  7.1 0.0 copy-start.3
  7.1 2.8 %response.1 = (f32[4,49,8,128]{3,2,1,0:T(8,128)S(1)}, f32[4,49,8,128]{3,2,1,0:T(8,128)S(1)}, bf16[8,512,512]{2,1,0:T(8,128)(2,1)S(1)}) custom-call(s32[3]{0:T(128)S(1)} %pad_add_fusion.where_ref, bf16[3,1,384,512]{3,2,1,0:T(8,128)(2,1)S(1)} %copy-done, f32[3,7,512]{2,1,0:T(8,128)S(1)} %copy-done.1, f32[16,512]{1,0:T(8,128)S(1)} %copy-done.2, ...), custom_call_target="tpu_custom_call" | custom-call | flops 1 | bytes 1 | tf_op jit(solution)/shard_map/response/pallas_call | solution.py:503
  10.0 0.2 collective-permute-done.message_ref
  10.1 0.0 copy-done.3
  10.2 1.8 %gated.1.own_ref = bf16[384,512]{1,0:T(8,128)(2,1)S(1)} custom-call(s32[3]{0:T(128)S(1)} %pad_add_fusion.where_ref, f32[40,512]{1,0:T(8,128)S(1)} %collective-permute-done.message_ref, bf16[3,1,384,512]{3,2,1,0:T(8,128)(2,1)S(1)} %copy-done, f32[3,7,512]{2,1,0:T(8,128)S(1)} %copy-done.1, f32[16,512]{1,0:T(8,128)S(1)} %copy-done.2, f32[16,512]{1,0:T(8,128)S(1)} %copy-done.4, ...), custom_call_target="tpu_custom_call" | custom-call | flops 1 | bytes 1 | tf_op jit(solution)/shard_map/gated/pallas_call | solution.py:519
  11.9 0.1 collective-permute-start.1
  12.0 1.1 %project_own.1.sum_ref = f32[4,384,256]{2,1,0:T(8,128)S(1)} custom-call(s32[3]{0:T(128)S(1)} %pad_add_fusion.where_ref, bf16[384,512]{1,0:T(8,128)(2,1)S(1)} %gated.1.own_ref, bf16[8,512,512]{2,1,0:T(8,128)(2,1)S(1)} %get-tuple-element.47.mine_ref), custom_call_target="tpu_custom_call" | custom-call | flops 1 | bytes 1 | tf_op jit(solution)/shard_map/project_own/pallas_call | solution.py:352
  13.1 0.6 collective-permute-done.1.other_ref
  13.7 0.0 collective-permute-done.2.theirs_ref
  13.7 1.1 %project_other.1 = (bf16[4,384,128]{2,1,0:T(8,128)(2,1)S(1)}, f32[4,384,128]{2,1,0:T(8,128)S(1)}) custom-call(s32[3]{0:T(128)S(1)} %pad_add_fusion.where_ref, f32[4,384,256]{2,1,0:T(8,128)S(1)} %project_own.1.sum_ref, bf16[384,512]{1,0:T(8,128)(2,1)S(1)} %collective-permute-done.1.other_ref, bf16[8,512,512]{2,1,0:T(8,128)(2,1)S(1)} %collective-permute-done.2.theirs_ref), custom_call_target="tpu_custom_call" | custom-call | flops 1 | bytes 1 | tf_op jit(solution)/shard_map/project_other/pallas_call | solution.py:366
  14.8 1.8 %collective-permute-start.3 = (bf16[4,384,128]{2,1,0:T(8,128)(2,1)S(1)}, bf16[4,384,128]{2,1,0:T(8,128)(2,1)S(1)}, u32[]{:S(2)}, u32[]{:S(2)}) collective-permute-start(bf16[4,384,128]{2,1,0:T(8,128)(2,1)S(1)} %get-tuple-element.50.order_ref), channel_id=1, source_target_pairs={{0,2},{1,3},{2,0},{3,1},{4,6},{5,7},{6,4},{7,5},{8,10},{9,11},{10,... | collective-permute-start | bytes 1179656 | tf_op jit(solution)/shard_map/ppermute | solution.py:433
  16.6 1.5 %project.4 = (bf16[4,384,128]{2,1,0:T(8,128)(2,1)S(1)}, f32[4,384,128]{2,1,0:T(8,128)S(1)}) custom-call(s32[3]{0:T(128)S(1)} %pad_add_fusion.where_ref, bf16[384,512]{1,0:T(8,128)(2,1)S(1)} %gated.1.own_ref, bf16[384,512]{1,0:T(8,128)(2,1)S(1)} %collective-permute-done.1.other_ref, bf16[8,512,512]{2,1,0:T(8,128)(2,1)S(1)} %get-tuple-element.47.mine_ref, ...), custom_call_target="tpu_custom_call" | custom-call | flops 1 | bytes 1 | tf_op jit(solution)/shard_map/project/pallas_call | solution.py:339
  18.2 1.6 %collective-permute-start.6 = (bf16[4,384,128]{2,1,0:T(8,128)(2,1)S(1)}, bf16[4,384,128]{2,1,0:T(8,128)(2,1)S(1)}, u32[]{:S(2)}, u32[]{:S(2)}) collective-permute-start(bf16[4,384,128]{2,1,0:T(8,128)(2,1)S(1)} %get-tuple-element.51.order_ref), channel_id=1, source_target_pairs={{0,4},{1,5},{2,6},{3,7},{4,0},{5,1},{6,2},{7,3},{8,12},{9,13},{10,... | collective-permute-start | bytes 1179656 | tf_op jit(solution)/shard_map/ppermute | solution.py:433
  19.8 1.5 %project.5 = (bf16[4,384,128]{2,1,0:T(8,128)(2,1)S(1)}, f32[4,384,128]{2,1,0:T(8,128)S(1)}) custom-call(s32[3]{0:T(128)S(1)} %pad_add_fusion.where_ref, bf16[384,512]{1,0:T(8,128)(2,1)S(1)} %gated.1.own_ref, bf16[384,512]{1,0:T(8,128)(2,1)S(1)} %collective-permute-done.1.other_ref, bf16[8,512,512]{2,1,0:T(8,128)(2,1)S(1)} %get-tuple-element.47.mine_ref, ...), custom_call_target="tpu_custom_call" | custom-call | flops 1 | bytes 1 | tf_op jit(solution)/shard_map/project/pallas_call | solution.py:339
  21.3 0.6 %collective-permute-start.5 = (bf16[4,384,128]{2,1,0:T(8,128)(2,1)S(1)}, bf16[4,384,128]{2,1,0:T(8,128)(2,1)S(1)}, u32[]{:S(2)}, u32[]{:S(2)}) collective-permute-start(bf16[4,384,128]{2,1,0:T(8,128)(2,1)S(1)} %get-tuple-element.52.order_ref), channel_id=1, source_target_pairs={{0,2},{1,3},{2,0},{3,1},{4,6},{5,7},{6,4},{7,5},{8,10},{9,11},{10,... | collective-permute-start | bytes 1179656 | tf_op jit(solution)/shard_map/ppermute | solution.py:433
  21.9 1.3 %project.6 = (bf16[4,256,128]{2,1,0:T(8,128)(2,1)S(1)}, f32[4,256,128]{2,1,0:T(8,128)S(1)}) custom-call(s32[3]{0:T(128)S(1)} %pad_add_fusion.where_ref, bf16[384,512]{1,0:T(8,128)(2,1)S(1)} %gated.1.own_ref, bf16[384,512]{1,0:T(8,128)(2,1)S(1)} %collective-permute-done.1.other_ref, bf16[8,512,512]{2,1,0:T(8,128)(2,1)S(1)} %get-tuple-element.47.mine_ref, ...), custom_call_target="tpu_custom_call" | custom-call | flops 1 | bytes 1 | tf_op jit(solution)/shard_map/project/pallas_call | solution.py:339
  23.2 1.6 %collective-permute-start.10 = (bf16[4,256,128]{2,1,0:T(8,128)(2,1)S(1)}, bf16[4,256,128]{2,1,0:T(8,128)(2,1)S(1)}, u32[]{:S(2)}, u32[]{:S(2)}) collective-permute-start(bf16[4,256,128]{2,1,0:T(8,128)(2,1)S(1)} %get-tuple-element.53.order_ref), channel_id=1, source_target_pairs={{0,2},{1,3},{2,0},{3,1},{4,6},{5,7},{6,4},{7,5},{8,10},{9,11},{10,... | collective-permute-start | bytes 786440 | tf_op jit(solution)/shard_map/ppermute | solution.py:433
  24.8 1.0 %project.7 = (bf16[4,128,128]{2,1,0:T(8,128)(2,1)S(1)}, f32[4,128,128]{2,1,0:T(8,128)S(1)}) custom-call(s32[3]{0:T(128)S(1)} %pad_add_fusion.where_ref, bf16[384,512]{1,0:T(8,128)(2,1)S(1)} %gated.1.own_ref, bf16[384,512]{1,0:T(8,128)(2,1)S(1)} %collective-permute-done.1.other_ref, bf16[8,512,512]{2,1,0:T(8,128)(2,1)S(1)} %get-tuple-element.47.mine_ref, ...), custom_call_target="tpu_custom_call" | custom-call | flops 1 | bytes 1 | tf_op jit(solution)/shard_map/project/pallas_call | solution.py:339
  25.8 1.1 %collective-permute-done.3.received_ref = bf16[4,384,128]{2,1,0:T(8,128)(2,1)S(1)} collective-permute-done((bf16[4,384,128]{2,1,0:T(8,128)(2,1)S(1)}, bf16[4,384,128]{2,1,0:T(8,128)(2,1)S(1)}, u32[]{:S(2)}, u32[]{:S(2)}) %collective-permute-start.3) | collective-permute-done | bytes 393248 | tf_op jit(solution)/shard_map/ppermute | solution.py:433
  26.9 0.1 merge.10
  26.9 1.9 %collective-permute-start.4 = (bf16[2,384,128]{2,1,0:T(8,128)(2,1)S(1)}, bf16[2,384,128]{2,1,0:T(8,128)(2,1)S(1)}, u32[]{:S(2)}, u32[]{:S(2)}) collective-permute-start(bf16[2,384,128]{2,1,0:T(8,128)(2,1)S(1)} %get-tuple-element.56.order_ref), channel_id=1, source_target_pairs={{0,4},{1,5},{2,6},{3,7},{4,0},{5,1},{6,2},{7,3},{8,12},{9,13},{10,... | collective-permute-start | bytes 589832 | tf_op jit(solution)/shard_map/ppermute | solution.py:433
  28.8 1.2 %collective-permute-done.6.received_ref = bf16[4,384,128]{2,1,0:T(8,128)(2,1)S(1)} collective-permute-done((bf16[4,384,128]{2,1,0:T(8,128)(2,1)S(1)}, bf16[4,384,128]{2,1,0:T(8,128)(2,1)S(1)}, u32[]{:S(2)}, u32[]{:S(2)}) %collective-permute-start.6) | collective-permute-done | bytes 393248 | tf_op jit(solution)/shard_map/ppermute | solution.py:433
  30.0 0.1 merge.11
  30.0 2.5 %collective-permute-start.11 = (bf16[2,384,128]{2,1,0:T(8,128)(2,1)S(1)}, bf16[2,384,128]{2,1,0:T(8,128)(2,1)S(1)}, u32[]{:S(2)}, u32[]{:S(2)}) collective-permute-start(bf16[2,384,128]{2,1,0:T(8,128)(2,1)S(1)} %get-tuple-element.59.order_ref), channel_id=1, source_target_pairs={{0,8},{1,9},{2,10},{3,11},{4,12},{5,13},{6,14},{7,15},{8,0},{9,1},... | collective-permute-start | bytes 589832 | tf_op jit(solution)/shard_map/ppermute | solution.py:433
  32.5 2.7 %collective-permute-done.5.received_ref = bf16[4,384,128]{2,1,0:T(8,128)(2,1)S(1)} collective-permute-done((bf16[4,384,128]{2,1,0:T(8,128)(2,1)S(1)}, bf16[4,384,128]{2,1,0:T(8,128)(2,1)S(1)}, u32[]{:S(2)}, u32[]{:S(2)}) %collective-permute-start.5) | collective-permute-done | bytes 393248 | tf_op jit(solution)/shard_map/ppermute | solution.py:433
  35.3 0.1 merge.12
  35.4 1.9 %collective-permute-start.9 = (bf16[2,384,128]{2,1,0:T(8,128)(2,1)S(1)}, bf16[2,384,128]{2,1,0:T(8,128)(2,1)S(1)}, u32[]{:S(2)}, u32[]{:S(2)}) collective-permute-start(bf16[2,384,128]{2,1,0:T(8,128)(2,1)S(1)} %get-tuple-element.60.order_ref), channel_id=1, source_target_pairs={{0,4},{1,5},{2,6},{3,7},{4,0},{5,1},{6,2},{7,3},{8,12},{9,13},{10,... | collective-permute-start | bytes 589832 | tf_op jit(solution)/shard_map/ppermute | solution.py:433
  37.2 1.5 %collective-permute-start.8 = (bf16[4,128,128]{2,1,0:T(8,128)(2,1)S(1)}, bf16[4,128,128]{2,1,0:T(8,128)(2,1)S(1)}, u32[]{:S(2)}, u32[]{:S(2)}) collective-permute-start(bf16[4,128,128]{2,1,0:T(8,128)(2,1)S(1)} %get-tuple-element.54.order_ref), channel_id=1, source_target_pairs={{0,2},{1,3},{2,0},{3,1},{4,6},{5,7},{6,4},{7,5},{8,10},{9,11},{10,... | collective-permute-start | bytes 393224 | tf_op jit(solution)/shard_map/ppermute | solution.py:433
  38.7 0.0 collective-permute-done.4.received_ref
  38.8 1.7 %collective-permute-done.11.received_ref = bf16[2,384,128]{2,1,0:T(8,128)(2,1)S(1)} collective-permute-done((bf16[2,384,128]{2,1,0:T(8,128)(2,1)S(1)}, bf16[2,384,128]{2,1,0:T(8,128)(2,1)S(1)}, u32[]{:S(2)}, u32[]{:S(2)}) %collective-permute-start.11) | collective-permute-done | bytes 196640 | tf_op jit(solution)/shard_map/ppermute | solution.py:433
  40.5 0.4 collective-permute-done.10.received_ref
  41.0 1.9 %collective-permute-start.13 = (bf16[2,256,128]{2,1,0:T(8,128)(2,1)S(1)}, bf16[2,256,128]{2,1,0:T(8,128)(2,1)S(1)}, u32[]{:S(2)}, u32[]{:S(2)}) collective-permute-start(bf16[2,256,128]{2,1,0:T(8,128)(2,1)S(1)} %get-tuple-element.68.order_ref), channel_id=1, source_target_pairs={{0,4},{1,5},{2,6},{3,7},{4,0},{5,1},{6,2},{7,3},{8,12},{9,13},{10,... | collective-permute-start | bytes 393224 | tf_op jit(solution)/shard_map/ppermute | solution.py:433
  42.8 2.6 %collective-permute-start.7 = (bf16[1,384,128]{2,1,0:T(8,128)(2,1)S(1)}, bf16[1,384,128]{2,1,0:T(8,128)(2,1)S(1)}, u32[]{:S(2)}, u32[]{:S(2)}) collective-permute-start(bf16[1,384,128]{2,1,0:T(8,128)(2,1)S(1)} %get-tuple-element.62.order_ref), channel_id=1, source_target_pairs={{0,8},{1,9},{2,10},{3,11},{4,12},{5,13},{6,14},{7,15},{8,0},{9,1},... | collective-permute-start | bytes 294920 | tf_op jit(solution)/shard_map/ppermute | solution.py:433
  45.4 0.0 collective-permute-done.9.received_ref
  45.5 1.8 %collective-permute-start.14 = (bf16[1,384,128]{2,1,0:T(8,128)(2,1)S(1)}, bf16[1,384,128]{2,1,0:T(8,128)(2,1)S(1)}, u32[]{:S(2)}, u32[]{:S(2)}) collective-permute-start(bf16[1,384,128]{2,1,0:T(8,128)(2,1)S(1)} %get-tuple-element.69.order_ref), channel_id=1, source_target_pairs={{0,8},{1,9},{2,10},{3,11},{4,12},{5,13},{6,14},{7,15},{8,0},{9,1},... | collective-permute-start | bytes 294920 | tf_op jit(solution)/shard_map/ppermute | solution.py:433
  47.3 0.0 collective-permute-done.8.received_ref
  47.3 2.5 %collective-permute-start.12 = (bf16[2,128,128]{2,1,0:T(8,128)(2,1)S(1)}, bf16[2,128,128]{2,1,0:T(8,128)(2,1)S(1)}, u32[]{:S(2)}, u32[]{:S(2)}) collective-permute-start(bf16[2,128,128]{2,1,0:T(8,128)(2,1)S(1)} %get-tuple-element.71.order_ref), channel_id=1, source_target_pairs={{0,4},{1,5},{2,6},{3,7},{4,0},{5,1},{6,2},{7,3},{8,12},{9,13},{10,... | collective-permute-start | bytes 196616 | tf_op jit(solution)/shard_map/ppermute | solution.py:433
  49.9 0.0 collective-permute-start.16
  49.9 0.0 collective-permute-done.13.received_ref
  49.9 0.7 %collective-permute-start.15 = (bf16[1,256,128]{2,1,0:T(8,128)(2,1)S(1)}, bf16[1,256,128]{2,1,0:T(8,128)(2,1)S(1)}, u32[]{:S(2)}, u32[]{:S(2)}) collective-permute-start(bf16[1,256,128]{2,1,0:T(8,128)(2,1)S(1)} %get-tuple-element.73.order_ref), channel_id=1, source_target_pairs={{0,8},{1,9},{2,10},{3,11},{4,12},{5,13},{6,14},{7,15},{8,0},{9,1},... | collective-permute-start | bytes 196616 | tf_op jit(solution)/shard_map/ppermute | solution.py:433
  50.7 1.5 %collective-permute-done.12.received_ref = bf16[2,128,128]{2,1,0:T(8,128)(2,1)S(1)} collective-permute-done((bf16[2,128,128]{2,1,0:T(8,128)(2,1)S(1)}, bf16[2,128,128]{2,1,0:T(8,128)(2,1)S(1)}, u32[]{:S(2)}, u32[]{:S(2)}) %collective-permute-start.12) | collective-permute-done | bytes 65568 | tf_op jit(solution)/shard_map/ppermute | solution.py:433
  52.1 2.0 %collective-permute-start.17 = (bf16[1,128,128]{2,1,0:T(8,128)(2,1)S(1)}, bf16[1,128,128]{2,1,0:T(8,128)(2,1)S(1)}, u32[]{:S(2)}, u32[]{:S(2)}) collective-permute-start(bf16[1,128,128]{2,1,0:T(8,128)(2,1)S(1)} %get-tuple-element.74.order_ref), channel_id=1, source_target_pairs={{0,8},{1,9},{2,10},{3,11},{4,12},{5,13},{6,14},{7,15},{8,0},{9,1},... | collective-permute-start | bytes 98312 | tf_op jit(solution)/shard_map/ppermute | solution.py:433
  54.2 0.0 collective-permute-done.7.received_ref
  54.2 1.9 %collective-permute-done.14.received_ref = bf16[1,384,128]{2,1,0:T(8,128)(2,1)S(1)} collective-permute-done((bf16[1,384,128]{2,1,0:T(8,128)(2,1)S(1)}, bf16[1,384,128]{2,1,0:T(8,128)(2,1)S(1)}, u32[]{:S(2)}, u32[]{:S(2)}) %collective-permute-start.14) | collective-permute-done | bytes 98336 | tf_op jit(solution)/shard_map/ppermute | solution.py:433
  56.1 0.7 %collective-permute-done.15.received_ref = bf16[1,256,128]{2,1,0:T(8,128)(2,1)S(1)} collective-permute-done((bf16[1,256,128]{2,1,0:T(8,128)(2,1)S(1)}, bf16[1,256,128]{2,1,0:T(8,128)(2,1)S(1)}, u32[]{:S(2)}, u32[]{:S(2)}) %collective-permute-start.15) | collective-permute-done | bytes 65568 | tf_op jit(solution)/shard_map/ppermute | solution.py:433
  56.8 0.0 collective-permute-done.16.received_ref
  56.9 0.3 collective-permute-done.17.refs_5_
  57.2 0.8 %gather.1 = bf16[1,384,512]{2,1,0:T(8,128)(2,1)} custom-call(bf16[384,128]{1,0:T(8,128)(2,1)S(1)} %finish.4.order_ref.refs_0_, bf16[384,128]{1,0:T(8,128)(2,1)S(1)} %finish.5.order_ref.refs_1_, bf16[256,128]{1,0:T(8,128)(2,1)S(1)} %finish.6.order_ref.refs_2_, bf16[384,128]{1,0:T(8,128)(2,1)S(1)} %finish.7.refs_3_.refs_6_, ...), custom_call_target="tpu_custom_call" | custom-call | flops 1 | bytes 1 | tf_op jit(solution)/shard_map/gather/pallas_call | solution.py:404
  (11 shorter events, 0.3 us)
Async XLA Ops:
  0.1 7.0 %copy-start = (bf16[3,1,384,512]{3,2,1,0:T(8,128)(2,1)S(1)}, bf16[3,1,384,512]{3,2,1,0:T(8,128)(2,1)}, u32[]{:S(2)}) copy-start(bf16[3,1,384,512]{3,2,1,0:T(8,128)(2,1)} %head_in_ref.1) | copy-start | bytes 3538948
  0.1 7.0 %copy-start.1 = (f32[3,7,512]{2,1,0:T(8,128)S(1)}, f32[3,7,512]{2,1,0:T(8,128)}, u32[]{:S(2)}) copy-start(f32[3,7,512]{2,1,0:T(8,128)} %taps_ref.3) | copy-start | bytes 129028
  0.1 7.0 %copy-start.2 = (f32[16,512]{1,0:T(8,128)S(1)}, f32[16,512]{1,0:T(8,128)}, u32[]{:S(2)}) copy-start(f32[16,512]{1,0:T(8,128)} %decay_ref.3) | copy-start | bytes 98308
  0.1 7.0 %copy-start.4 = (f32[16,512]{1,0:T(8,128)S(1)}, f32[16,512]{1,0:T(8,128)}, u32[]{:S(2)}) copy-start(f32[16,512]{1,0:T(8,128)} %residues_ref.3) | copy-start | bytes 98308
  4.0 9.7 %collective-permute-start.2 = (bf16[8,512,512]{2,1,0:T(8,128)(2,1)S(1)}, bf16[8,512,512]{2,1,0:T(8,128)(2,1)S(1)}, u32[]{:S(2)}, u32[]{:S(2)}) collective-permute-start(bf16[8,512,512]{2,1,0:T(8,128)(2,1)S(1)} %get-tuple-element.48), channel_id=1, source_target_pairs={{0,1},{1,0},{2,3},{3,2},{4,5},{5,4},{6,7},{7,6},{8,9},{9,8},{10,11... | collective-permute-start | bytes 12582920 | tf_op jit(solution)/shard_map/ppermute | solution.py:433
  4.5 5.6 %collective-permute-start = (f32[40,512]{1,0:T(8,128)S(1)}, f32[40,512]{1,0:T(8,128)S(1)}, u32[]{:S(2)}, u32[]{:S(2)}) collective-permute-start(f32[40,512]{1,0:T(8,128)S(1)} %get-tuple-element.42), channel_id=1, source_target_pairs={{0,16},{16,0},{1,17},{17,1},{2,18},{18,2},{3,19},{19,3},{4,20},{20... | collective-permute-start | bytes 245768 | tf_op jit(solution)/shard_map/ppermute | solution.py:438
  7.1 3.0 %copy-start.3 = (f32[1,16,512]{2,1,0:T(8,128)S(1)}, f32[1,16,512]{2,1,0:T(8,128)}, u32[]{:S(2)}) copy-start(f32[1,16,512]{2,1,0:T(8,128)} %init_ref.1) | copy-start | bytes 98308
  11.9 1.8 %collective-permute-start.1 = (bf16[384,512]{1,0:T(8,128)(2,1)S(1)}, bf16[384,512]{1,0:T(8,128)(2,1)S(1)}, u32[]{:S(2)}, u32[]{:S(2)}) collective-permute-start(bf16[384,512]{1,0:T(8,128)(2,1)S(1)} %gated.1.own_ref), channel_id=1, source_target_pairs={{0,1},{1,0},{2,3},{3,2},{4,5},{5,4},{6,7},{7,6},{8,9},{9,8},{10,11... | collective-permute-start | bytes 1179656 | tf_op jit(solution)/shard_map/ppermute | solution.py:433
  14.8 12.0 %collective-permute-start.3 = (bf16[4,384,128]{2,1,0:T(8,128)(2,1)S(1)}, bf16[4,384,128]{2,1,0:T(8,128)(2,1)S(1)}, u32[]{:S(2)}, u32[]{:S(2)}) collective-permute-start(bf16[4,384,128]{2,1,0:T(8,128)(2,1)S(1)} %get-tuple-element.50.order_ref), channel_id=1, source_target_pairs={{0,2},{1,3},{2,0},{3,1},{4,6},{5,7},{6,4},{7,5},{8,10},{9,11},{10,... | collective-permute-start | bytes 1179656 | tf_op jit(solution)/shard_map/ppermute | solution.py:433
  18.2 11.8 %collective-permute-start.6 = (bf16[4,384,128]{2,1,0:T(8,128)(2,1)S(1)}, bf16[4,384,128]{2,1,0:T(8,128)(2,1)S(1)}, u32[]{:S(2)}, u32[]{:S(2)}) collective-permute-start(bf16[4,384,128]{2,1,0:T(8,128)(2,1)S(1)} %get-tuple-element.51.order_ref), channel_id=1, source_target_pairs={{0,4},{1,5},{2,6},{3,7},{4,0},{5,1},{6,2},{7,3},{8,12},{9,13},{10,... | collective-permute-start | bytes 1179656 | tf_op jit(solution)/shard_map/ppermute | solution.py:433
  21.3 13.9 %collective-permute-start.5 = (bf16[4,384,128]{2,1,0:T(8,128)(2,1)S(1)}, bf16[4,384,128]{2,1,0:T(8,128)(2,1)S(1)}, u32[]{:S(2)}, u32[]{:S(2)}) collective-permute-start(bf16[4,384,128]{2,1,0:T(8,128)(2,1)S(1)} %get-tuple-element.52.order_ref), channel_id=1, source_target_pairs={{0,2},{1,3},{2,0},{3,1},{4,6},{5,7},{6,4},{7,5},{8,10},{9,11},{10,... | collective-permute-start | bytes 1179656 | tf_op jit(solution)/shard_map/ppermute | solution.py:433
  23.2 17.7 %collective-permute-start.10 = (bf16[4,256,128]{2,1,0:T(8,128)(2,1)S(1)}, bf16[4,256,128]{2,1,0:T(8,128)(2,1)S(1)}, u32[]{:S(2)}, u32[]{:S(2)}) collective-permute-start(bf16[4,256,128]{2,1,0:T(8,128)(2,1)S(1)} %get-tuple-element.53.order_ref), channel_id=1, source_target_pairs={{0,2},{1,3},{2,0},{3,1},{4,6},{5,7},{6,4},{7,5},{8,10},{9,11},{10,... | collective-permute-start | bytes 786440 | tf_op jit(solution)/shard_map/ppermute | solution.py:433
  26.9 11.8 %collective-permute-start.4 = (bf16[2,384,128]{2,1,0:T(8,128)(2,1)S(1)}, bf16[2,384,128]{2,1,0:T(8,128)(2,1)S(1)}, u32[]{:S(2)}, u32[]{:S(2)}) collective-permute-start(bf16[2,384,128]{2,1,0:T(8,128)(2,1)S(1)} %get-tuple-element.56.order_ref), channel_id=1, source_target_pairs={{0,4},{1,5},{2,6},{3,7},{4,0},{5,1},{6,2},{7,3},{8,12},{9,13},{10,... | collective-permute-start | bytes 589832 | tf_op jit(solution)/shard_map/ppermute | solution.py:433
  30.0 10.5 %collective-permute-start.11 = (bf16[2,384,128]{2,1,0:T(8,128)(2,1)S(1)}, bf16[2,384,128]{2,1,0:T(8,128)(2,1)S(1)}, u32[]{:S(2)}, u32[]{:S(2)}) collective-permute-start(bf16[2,384,128]{2,1,0:T(8,128)(2,1)S(1)} %get-tuple-element.59.order_ref), channel_id=1, source_target_pairs={{0,8},{1,9},{2,10},{3,11},{4,12},{5,13},{6,14},{7,15},{8,0},{9,1},... | collective-permute-start | bytes 589832 | tf_op jit(solution)/shard_map/ppermute | solution.py:433
  35.4 10.1 %collective-permute-start.9 = (bf16[2,384,128]{2,1,0:T(8,128)(2,1)S(1)}, bf16[2,384,128]{2,1,0:T(8,128)(2,1)S(1)}, u32[]{:S(2)}, u32[]{:S(2)}) collective-permute-start(bf16[2,384,128]{2,1,0:T(8,128)(2,1)S(1)} %get-tuple-element.60.order_ref), channel_id=1, source_target_pairs={{0,4},{1,5},{2,6},{3,7},{4,0},{5,1},{6,2},{7,3},{8,12},{9,13},{10,... | collective-permute-start | bytes 589832 | tf_op jit(solution)/shard_map/ppermute | solution.py:433
  37.2 10.1 %collective-permute-start.8 = (bf16[4,128,128]{2,1,0:T(8,128)(2,1)S(1)}, bf16[4,128,128]{2,1,0:T(8,128)(2,1)S(1)}, u32[]{:S(2)}, u32[]{:S(2)}) collective-permute-start(bf16[4,128,128]{2,1,0:T(8,128)(2,1)S(1)} %get-tuple-element.54.order_ref), channel_id=1, source_target_pairs={{0,2},{1,3},{2,0},{3,1},{4,6},{5,7},{6,4},{7,5},{8,10},{9,11},{10,... | collective-permute-start | bytes 393224 | tf_op jit(solution)/shard_map/ppermute | solution.py:433
  41.0 8.9 %collective-permute-start.13 = (bf16[2,256,128]{2,1,0:T(8,128)(2,1)S(1)}, bf16[2,256,128]{2,1,0:T(8,128)(2,1)S(1)}, u32[]{:S(2)}, u32[]{:S(2)}) collective-permute-start(bf16[2,256,128]{2,1,0:T(8,128)(2,1)S(1)} %get-tuple-element.68.order_ref), channel_id=1, source_target_pairs={{0,4},{1,5},{2,6},{3,7},{4,0},{5,1},{6,2},{7,3},{8,12},{9,13},{10,... | collective-permute-start | bytes 393224 | tf_op jit(solution)/shard_map/ppermute | solution.py:433
  42.8 11.3 %collective-permute-start.7 = (bf16[1,384,128]{2,1,0:T(8,128)(2,1)S(1)}, bf16[1,384,128]{2,1,0:T(8,128)(2,1)S(1)}, u32[]{:S(2)}, u32[]{:S(2)}) collective-permute-start(bf16[1,384,128]{2,1,0:T(8,128)(2,1)S(1)} %get-tuple-element.62.order_ref), channel_id=1, source_target_pairs={{0,8},{1,9},{2,10},{3,11},{4,12},{5,13},{6,14},{7,15},{8,0},{9,1},... | collective-permute-start | bytes 294920 | tf_op jit(solution)/shard_map/ppermute | solution.py:433
  45.5 10.6 %collective-permute-start.14 = (bf16[1,384,128]{2,1,0:T(8,128)(2,1)S(1)}, bf16[1,384,128]{2,1,0:T(8,128)(2,1)S(1)}, u32[]{:S(2)}, u32[]{:S(2)}) collective-permute-start(bf16[1,384,128]{2,1,0:T(8,128)(2,1)S(1)} %get-tuple-element.69.order_ref), channel_id=1, source_target_pairs={{0,8},{1,9},{2,10},{3,11},{4,12},{5,13},{6,14},{7,15},{8,0},{9,1},... | collective-permute-start | bytes 294920 | tf_op jit(solution)/shard_map/ppermute | solution.py:433
  47.3 4.8 %collective-permute-start.12 = (bf16[2,128,128]{2,1,0:T(8,128)(2,1)S(1)}, bf16[2,128,128]{2,1,0:T(8,128)(2,1)S(1)}, u32[]{:S(2)}, u32[]{:S(2)}) collective-permute-start(bf16[2,128,128]{2,1,0:T(8,128)(2,1)S(1)} %get-tuple-element.71.order_ref), channel_id=1, source_target_pairs={{0,4},{1,5},{2,6},{3,7},{4,0},{5,1},{6,2},{7,3},{8,12},{9,13},{10,... | collective-permute-start | bytes 196616 | tf_op jit(solution)/shard_map/ppermute | solution.py:433
  49.9 6.9 %collective-permute-start.16 = (bf16[1,384,128]{2,1,0:T(8,128)(2,1)S(1)}, bf16[1,384,128]{2,1,0:T(8,128)(2,1)S(1)}, u32[]{:S(2)}, u32[]{:S(2)}) collective-permute-start(bf16[1,384,128]{2,1,0:T(8,128)(2,1)S(1)} %get-tuple-element.67.order_ref), channel_id=1, source_target_pairs={{0,2},{1,3},{2,0},{3,1},{4,6},{5,7},{6,4},{7,5},{8,10},{9,11},{10,... | collective-permute-start | bytes 294920 | tf_op jit(solution)/shard_map/ppermute | solution.py:433
  49.9 6.9 %collective-permute-start.15 = (bf16[1,256,128]{2,1,0:T(8,128)(2,1)S(1)}, bf16[1,256,128]{2,1,0:T(8,128)(2,1)S(1)}, u32[]{:S(2)}, u32[]{:S(2)}) collective-permute-start(bf16[1,256,128]{2,1,0:T(8,128)(2,1)S(1)} %get-tuple-element.73.order_ref), channel_id=1, source_target_pairs={{0,8},{1,9},{2,10},{3,11},{4,12},{5,13},{6,14},{7,15},{8,0},{9,1},... | collective-permute-start | bytes 196616 | tf_op jit(solution)/shard_map/ppermute | solution.py:433
  52.1 5.0 %collective-permute-start.17 = (bf16[1,128,128]{2,1,0:T(8,128)(2,1)S(1)}, bf16[1,128,128]{2,1,0:T(8,128)(2,1)S(1)}, u32[]{:S(2)}, u32[]{:S(2)}) collective-permute-start(bf16[1,128,128]{2,1,0:T(8,128)(2,1)S(1)} %get-tuple-element.74.order_ref), channel_id=1, source_target_pairs={{0,8},{1,9},{2,10},{3,11},{4,12},{5,13},{6,14},{7,15},{8,0},{9,1},... | collective-permute-start | bytes 98312 | tf_op jit(solution)/shard_map/ppermute | solution.py:433

commit v8 on v7

--- a/solution.py
+++ b/solution.py
@@ -269,24 +269,22 @@
 
 def project_own_kernel(part, where_ref, own_ref, mine_ref, out_ref):
     row, rows, _, _ = part.box
-
-    def step(index):
-        out_ref[index] = jnp.dot(own_ref[row : row + rows, :], sides(part, where_ref, mine_ref, index), preferred_element_type=F32)
-
-    for index in range(out_ref.shape[0]):
-        step(index)
+    count, _, wide = out_ref.shape
+    blocks = jnp.concatenate([sides(part, where_ref, mine_ref, index) for index in range(count)], axis=1)
+    total = jnp.dot(own_ref[row : row + rows, :], blocks, preferred_element_type=F32)
+    for index in range(count):
+        out_ref[index] = total[:, index * wide : (index + 1) * wide]
 
 
 def project_other_kernel(part, where_ref, sum_ref, other_ref, theirs_ref, send_ref, keep_ref):
     row, rows, _, columns = part.box
-
-    def step(index):
-        total = sum_ref[index] + jnp.dot(other_ref[row : row + rows, :], sides(part, where_ref, theirs_ref, index), preferred_element_type=F32)
+    count, _, wide = sum_ref.shape
+    blocks = jnp.concatenate([sides(part, where_ref, theirs_ref, index) for index in range(count)], axis=1)
+    product = jnp.dot(other_ref[row : row + rows, :], blocks, preferred_element_type=F32)
+    for index in range(count):
+        total = sum_ref[index] + product[:, index * wide : (index + 1) * wide]
         send_ref[index] = total[:, :columns].astype(BF16)
         keep_ref[index] = total[:, columns:]
-
-    for index in range(send_ref.shape[0]):
-        step(index)
 
 
 def merge_kernel(keep_ref, received_ref, order_ref, send_ref, kept_ref):

time: 58.1 us -> 58.1 us (level)
  no operation moved by 1% of the time
where the time goes in v8:
time: 58.1 us; the launch traced here: 57.9 us
  starting transfers between devices  28.1 us (48%)
  Pallas kernels  17.3 us (30%)
  waiting for transfers between devices  12.2 us (21%)
    ppermute x17, starting transfers between devices, across(): return lax.ppermute(x, 'tp', [(i, i ^ 1 << bit) for i in range(count)])  25.5 us
    ppermute x17, waiting for transfers between devices, across(): return lax.ppermute(x, 'tp', [(i, i ^ 1 << bit) for i in range(count)])  12 us
    pallas_call x4, Pallas kernels, project(): pl.pallas_call(functools.partial(project_kernel, part), out_shape=(jax.Sh...  5.32 us
    pallas_call x1, Pallas kernels, per_device(): pl.pallas_call(driven_kernel, out_shape=(jax.ShapeDtypeStruct(split, F32)...  3.9 us
    pallas_call x1, Pallas kernels, per_device(): pl.pallas_call(response_kernel, out_shape=(jax.ShapeDtypeStruct(split, F3...  2.82 us
    ppermute x1, starting transfers between devices, after(): return lax.ppermute(x, axis, [(i, (i + 1) % count) for i in range(count)])  2.59 us
    pallas_call x1, Pallas kernels, per_device(): pl.pallas_call(gated_kernel, out_shape=jax.ShapeDtypeStruct((length, chan...  1.76 us
  transfers between devices with their start and end apart: 18, of which 11 were waited for; matrix products, arithmetic and copies ran while one was open for 0% of the time, Pallas kernels for 20%

profile of v8, /device:TPU:0, one launch (start us, length us, event | category | flops | bytes accessed | tf_op | source)
XLA Modules:
  0.0 57.9 jit_solution(956267574048701398)
XLA Ops:
  0.0 0.1 pad_add_fusion.where_ref
  0.1 0.0 copy-start
  0.1 0.0 copy-start.1
  0.1 0.0 copy-start.2
  0.1 0.0 copy-start.4
  0.1 3.9 %driven.1 = (f32[4,49,8,128]{3,2,1,0:T(8,128)S(1)}, f32[4,16,8,128]{3,2,1,0:T(8,128)S(1)}, f32[40,512]{1,0:T(8,128)S(1)}, bf16[8,512,512]{2,1,0:T(8,128)(2,1)S(1)}) custom-call(s32[3]{0:T(128)S(1)} %pad_add_fusion.where_ref, bf16[3,1,384,512]{3,2,1,0:T(8,128)(2,1)} %head_in_ref.1, f32[3,7,512]{2,1,0:T(8,128)} %taps_ref.3, f32[16,512]{1,0:T(8,128)} %decay_ref.3, ...), custom_call_target="tpu_custom_call" | custom-call | flops 1 | bytes 1 | tf_op jit(solution)/shard_map/driven/pallas_call | solution.py:475
  4.0 0.5 collective-permute-start.2
  4.5 2.6 %collective-permute-start = (f32[40,512]{1,0:T(8,128)S(1)}, f32[40,512]{1,0:T(8,128)S(1)}, u32[]{:S(2)}, u32[]{:S(2)}) collective-permute-start(f32[40,512]{1,0:T(8,128)S(1)} %get-tuple-element.42), channel_id=1, source_target_pairs={{0,16},{16,0},{1,17},{17,1},{2,18},{18,2},{3,19},{19,3},{4,20},{20... | collective-permute-start | bytes 245768 | tf_op jit(solution)/shard_map/ppermute | solution.py:436
  7.1 0.0 copy-done
  7.1 0.0 copy-done.1
  7.1 0.0 copy-done.2
  7.1 0.0 copy-done.4
  7.1 0.0 copy-start.3
  7.1 2.8 %response.1 = (f32[4,49,8,128]{3,2,1,0:T(8,128)S(1)}, f32[4,49,8,128]{3,2,1,0:T(8,128)S(1)}, bf16[8,512,512]{2,1,0:T(8,128)(2,1)S(1)}) custom-call(s32[3]{0:T(128)S(1)} %pad_add_fusion.where_ref, bf16[3,1,384,512]{3,2,1,0:T(8,128)(2,1)S(1)} %copy-done, f32[3,7,512]{2,1,0:T(8,128)S(1)} %copy-done.1, f32[16,512]{1,0:T(8,128)S(1)} %copy-done.2, ...), custom_call_target="tpu_custom_call" | custom-call | flops 1 | bytes 1 | tf_op jit(solution)/shard_map/response/pallas_call | solution.py:501
  10.0 0.2 collective-permute-done.message_ref
  10.1 0.0 copy-done.3
  10.2 1.8 %gated.1.own_ref = bf16[384,512]{1,0:T(8,128)(2,1)S(1)} custom-call(s32[3]{0:T(128)S(1)} %pad_add_fusion.where_ref, f32[40,512]{1,0:T(8,128)S(1)} %collective-permute-done.message_ref, bf16[3,1,384,512]{3,2,1,0:T(8,128)(2,1)S(1)} %copy-done, f32[3,7,512]{2,1,0:T(8,128)S(1)} %copy-done.1, f32[16,512]{1,0:T(8,128)S(1)} %copy-done.2, f32[16,512]{1,0:T(8,128)S(1)} %copy-done.4, ...), custom_call_target="tpu_custom_call" | custom-call | flops 1 | bytes 1 | tf_op jit(solution)/shard_map/gated/pallas_call | solution.py:517
  11.9 0.1 collective-permute-start.1
  12.0 1.1 %project_own.1.sum_ref = f32[4,384,256]{2,1,0:T(8,128)S(1)} custom-call(s32[3]{0:T(128)S(1)} %pad_add_fusion.where_ref, bf16[384,512]{1,0:T(8,128)(2,1)S(1)} %gated.1.own_ref, bf16[8,512,512]{2,1,0:T(8,128)(2,1)S(1)} %get-tuple-element.47.mine_ref), custom_call_target="tpu_custom_call" | custom-call | flops 1 | bytes 1 | tf_op jit(solution)/shard_map/project_own/pallas_call | solution.py:350
  13.1 0.6 collective-permute-done.1.other_ref
  13.7 0.0 collective-permute-done.2.theirs_ref
  13.7 1.1 %project_other.1 = (bf16[4,384,128]{2,1,0:T(8,128)(2,1)S(1)}, f32[4,384,128]{2,1,0:T(8,128)S(1)}) custom-call(s32[3]{0:T(128)S(1)} %pad_add_fusion.where_ref, f32[4,384,256]{2,1,0:T(8,128)S(1)} %project_own.1.sum_ref, bf16[384,512]{1,0:T(8,128)(2,1)S(1)} %collective-permute-done.1.other_ref, bf16[8,512,512]{2,1,0:T(8,128)(2,1)S(1)} %collective-permute-done.2.theirs_ref), custom_call_target="tpu_custom_call" | custom-call | flops 1 | bytes 1 | tf_op jit(solution)/shard_map/project_other/pallas_call | solution.py:364
  14.8 1.8 %collective-permute-start.3 = (bf16[4,384,128]{2,1,0:T(8,128)(2,1)S(1)}, bf16[4,384,128]{2,1,0:T(8,128)(2,1)S(1)}, u32[]{:S(2)}, u32[]{:S(2)}) collective-permute-start(bf16[4,384,128]{2,1,0:T(8,128)(2,1)S(1)} %get-tuple-element.50.order_ref), channel_id=1, source_target_pairs={{0,2},{1,3},{2,0},{3,1},{4,6},{5,7},{6,4},{7,5},{8,10},{9,11},{10,... | collective-permute-start | bytes 1179656 | tf_op jit(solution)/shard_map/ppermute | solution.py:431
  16.6 1.5 %project.4 = (bf16[4,384,128]{2,1,0:T(8,128)(2,1)S(1)}, f32[4,384,128]{2,1,0:T(8,128)S(1)}) custom-call(s32[3]{0:T(128)S(1)} %pad_add_fusion.where_ref, bf16[384,512]{1,0:T(8,128)(2,1)S(1)} %gated.1.own_ref, bf16[384,512]{1,0:T(8,128)(2,1)S(1)} %collective-permute-done.1.other_ref, bf16[8,512,512]{2,1,0:T(8,128)(2,1)S(1)} %get-tuple-element.47.mine_ref, ...), custom_call_target="tpu_custom_call" | custom-call | flops 1 | bytes 1 | tf_op jit(solution)/shard_map/project/pallas_call | solution.py:337
  18.2 1.6 %collective-permute-start.6 = (bf16[4,384,128]{2,1,0:T(8,128)(2,1)S(1)}, bf16[4,384,128]{2,1,0:T(8,128)(2,1)S(1)}, u32[]{:S(2)}, u32[]{:S(2)}) collective-permute-start(bf16[4,384,128]{2,1,0:T(8,128)(2,1)S(1)} %get-tuple-element.51.order_ref), channel_id=1, source_target_pairs={{0,4},{1,5},{2,6},{3,7},{4,0},{5,1},{6,2},{7,3},{8,12},{9,13},{10,... | collective-permute-start | bytes 1179656 | tf_op jit(solution)/shard_map/ppermute | solution.py:431
  19.8 1.5 %project.5 = (bf16[4,384,128]{2,1,0:T(8,128)(2,1)S(1)}, f32[4,384,128]{2,1,0:T(8,128)S(1)}) custom-call(s32[3]{0:T(128)S(1)} %pad_add_fusion.where_ref, bf16[384,512]{1,0:T(8,128)(2,1)S(1)} %gated.1.own_ref, bf16[384,512]{1,0:T(8,128)(2,1)S(1)} %collective-permute-done.1.other_ref, bf16[8,512,512]{2,1,0:T(8,128)(2,1)S(1)} %get-tuple-element.47.mine_ref, ...), custom_call_target="tpu_custom_call" | custom-call | flops 1 | bytes 1 | tf_op jit(solution)/shard_map/project/pallas_call | solution.py:337
  21.3 0.6 %collective-permute-start.5 = (bf16[4,384,128]{2,1,0:T(8,128)(2,1)S(1)}, bf16[4,384,128]{2,1,0:T(8,128)(2,1)S(1)}, u32[]{:S(2)}, u32[]{:S(2)}) collective-permute-start(bf16[4,384,128]{2,1,0:T(8,128)(2,1)S(1)} %get-tuple-element.52.order_ref), channel_id=1, source_target_pairs={{0,2},{1,3},{2,0},{3,1},{4,6},{5,7},{6,4},{7,5},{8,10},{9,11},{10,... | collective-permute-start | bytes 1179656 | tf_op jit(solution)/shard_map/ppermute | solution.py:431
  21.9 1.3 %project.6 = (bf16[4,256,128]{2,1,0:T(8,128)(2,1)S(1)}, f32[4,256,128]{2,1,0:T(8,128)S(1)}) custom-call(s32[3]{0:T(128)S(1)} %pad_add_fusion.where_ref, bf16[384,512]{1,0:T(8,128)(2,1)S(1)} %gated.1.own_ref, bf16[384,512]{1,0:T(8,128)(2,1)S(1)} %collective-permute-done.1.other_ref, bf16[8,512,512]{2,1,0:T(8,128)(2,1)S(1)} %get-tuple-element.47.mine_ref, ...), custom_call_target="tpu_custom_call" | custom-call | flops 1 | bytes 1 | tf_op jit(solution)/shard_map/project/pallas_call | solution.py:337
  23.2 1.6 %collective-permute-start.10 = (bf16[4,256,128]{2,1,0:T(8,128)(2,1)S(1)}, bf16[4,256,128]{2,1,0:T(8,128)(2,1)S(1)}, u32[]{:S(2)}, u32[]{:S(2)}) collective-permute-start(bf16[4,256,128]{2,1,0:T(8,128)(2,1)S(1)} %get-tuple-element.53.order_ref), channel_id=1, source_target_pairs={{0,2},{1,3},{2,0},{3,1},{4,6},{5,7},{6,4},{7,5},{8,10},{9,11},{10,... | collective-permute-start | bytes 786440 | tf_op jit(solution)/shard_map/ppermute | solution.py:431
  24.8 1.0 %project.7 = (bf16[4,128,128]{2,1,0:T(8,128)(2,1)S(1)}, f32[4,128,128]{2,1,0:T(8,128)S(1)}) custom-call(s32[3]{0:T(128)S(1)} %pad_add_fusion.where_ref, bf16[384,512]{1,0:T(8,128)(2,1)S(1)} %gated.1.own_ref, bf16[384,512]{1,0:T(8,128)(2,1)S(1)} %collective-permute-done.1.other_ref, bf16[8,512,512]{2,1,0:T(8,128)(2,1)S(1)} %get-tuple-element.47.mine_ref, ...), custom_call_target="tpu_custom_call" | custom-call | flops 1 | bytes 1 | tf_op jit(solution)/shard_map/project/pallas_call | solution.py:337
  25.8 1.1 %collective-permute-done.3.received_ref = bf16[4,384,128]{2,1,0:T(8,128)(2,1)S(1)} collective-permute-done((bf16[4,384,128]{2,1,0:T(8,128)(2,1)S(1)}, bf16[4,384,128]{2,1,0:T(8,128)(2,1)S(1)}, u32[]{:S(2)}, u32[]{:S(2)}) %collective-permute-start.3) | collective-permute-done | bytes 393248 | tf_op jit(solution)/shard_map/ppermute | solution.py:431
  26.9 0.1 merge.10
  26.9 1.9 %collective-permute-start.4 = (bf16[2,384,128]{2,1,0:T(8,128)(2,1)S(1)}, bf16[2,384,128]{2,1,0:T(8,128)(2,1)S(1)}, u32[]{:S(2)}, u32[]{:S(2)}) collective-permute-start(bf16[2,384,128]{2,1,0:T(8,128)(2,1)S(1)} %get-tuple-element.56.order_ref), channel_id=1, source_target_pairs={{0,4},{1,5},{2,6},{3,7},{4,0},{5,1},{6,2},{7,3},{8,12},{9,13},{10,... | collective-permute-start | bytes 589832 | tf_op jit(solution)/shard_map/ppermute | solution.py:431
  28.8 1.2 %collective-permute-done.6.received_ref = bf16[4,384,128]{2,1,0:T(8,128)(2,1)S(1)} collective-permute-done((bf16[4,384,128]{2,1,0:T(8,128)(2,1)S(1)}, bf16[4,384,128]{2,1,0:T(8,128)(2,1)S(1)}, u32[]{:S(2)}, u32[]{:S(2)}) %collective-permute-start.6) | collective-permute-done | bytes 393248 | tf_op jit(solution)/shard_map/ppermute | solution.py:431
  30.0 0.1 merge.11
  30.0 2.5 %collective-permute-start.11 = (bf16[2,384,128]{2,1,0:T(8,128)(2,1)S(1)}, bf16[2,384,128]{2,1,0:T(8,128)(2,1)S(1)}, u32[]{:S(2)}, u32[]{:S(2)}) collective-permute-start(bf16[2,384,128]{2,1,0:T(8,128)(2,1)S(1)} %get-tuple-element.59.order_ref), channel_id=1, source_target_pairs={{0,8},{1,9},{2,10},{3,11},{4,12},{5,13},{6,14},{7,15},{8,0},{9,1},... | collective-permute-start | bytes 589832 | tf_op jit(solution)/shard_map/ppermute | solution.py:431
  32.5 2.7 %collective-permute-done.5.received_ref = bf16[4,384,128]{2,1,0:T(8,128)(2,1)S(1)} collective-permute-done((bf16[4,384,128]{2,1,0:T(8,128)(2,1)S(1)}, bf16[4,384,128]{2,1,0:T(8,128)(2,1)S(1)}, u32[]{:S(2)}, u32[]{:S(2)}) %collective-permute-start.5) | collective-permute-done | bytes 393248 | tf_op jit(solution)/shard_map/ppermute | solution.py:431
  35.3 0.1 merge.12
  35.4 1.9 %collective-permute-start.9 = (bf16[2,384,128]{2,1,0:T(8,128)(2,1)S(1)}, bf16[2,384,128]{2,1,0:T(8,128)(2,1)S(1)}, u32[]{:S(2)}, u32[]{:S(2)}) collective-permute-start(bf16[2,384,128]{2,1,0:T(8,128)(2,1)S(1)} %get-tuple-element.60.order_ref), channel_id=1, source_target_pairs={{0,4},{1,5},{2,6},{3,7},{4,0},{5,1},{6,2},{7,3},{8,12},{9,13},{10,... | collective-permute-start | bytes 589832 | tf_op jit(solution)/shard_map/ppermute | solution.py:431
  37.2 1.5 %collective-permute-start.8 = (bf16[4,128,128]{2,1,0:T(8,128)(2,1)S(1)}, bf16[4,128,128]{2,1,0:T(8,128)(2,1)S(1)}, u32[]{:S(2)}, u32[]{:S(2)}) collective-permute-start(bf16[4,128,128]{2,1,0:T(8,128)(2,1)S(1)} %get-tuple-element.54.order_ref), channel_id=1, source_target_pairs={{0,2},{1,3},{2,0},{3,1},{4,6},{5,7},{6,4},{7,5},{8,10},{9,11},{10,... | collective-permute-start | bytes 393224 | tf_op jit(solution)/shard_map/ppermute | solution.py:431
  38.7 0.0 collective-permute-done.4.received_ref
  38.8 1.7 %collective-permute-done.11.received_ref = bf16[2,384,128]{2,1,0:T(8,128)(2,1)S(1)} collective-permute-done((bf16[2,384,128]{2,1,0:T(8,128)(2,1)S(1)}, bf16[2,384,128]{2,1,0:T(8,128)(2,1)S(1)}, u32[]{:S(2)}, u32[]{:S(2)}) %collective-permute-start.11) | collective-permute-done | bytes 196640 | tf_op jit(solution)/shard_map/ppermute | solution.py:431
  40.5 0.4 collective-permute-done.10.received_ref
  41.0 1.9 %collective-permute-start.13 = (bf16[2,256,128]{2,1,0:T(8,128)(2,1)S(1)}, bf16[2,256,128]{2,1,0:T(8,128)(2,1)S(1)}, u32[]{:S(2)}, u32[]{:S(2)}) collective-permute-start(bf16[2,256,128]{2,1,0:T(8,128)(2,1)S(1)} %get-tuple-element.68.order_ref), channel_id=1, source_target_pairs={{0,4},{1,5},{2,6},{3,7},{4,0},{5,1},{6,2},{7,3},{8,12},{9,13},{10,... | collective-permute-start | bytes 393224 | tf_op jit(solution)/shard_map/ppermute | solution.py:431
  42.8 2.6 %collective-permute-start.7 = (bf16[1,384,128]{2,1,0:T(8,128)(2,1)S(1)}, bf16[1,384,128]{2,1,0:T(8,128)(2,1)S(1)}, u32[]{:S(2)}, u32[]{:S(2)}) collective-permute-start(bf16[1,384,128]{2,1,0:T(8,128)(2,1)S(1)} %get-tuple-element.62.order_ref), channel_id=1, source_target_pairs={{0,8},{1,9},{2,10},{3,11},{4,12},{5,13},{6,14},{7,15},{8,0},{9,1},... | collective-permute-start | bytes 294920 | tf_op jit(solution)/shard_map/ppermute | solution.py:431
  45.4 0.0 collective-permute-done.9.received_ref
  45.5 1.8 %collective-permute-start.14 = (bf16[1,384,128]{2,1,0:T(8,128)(2,1)S(1)}, bf16[1,384,128]{2,1,0:T(8,128)(2,1)S(1)}, u32[]{:S(2)}, u32[]{:S(2)}) collective-permute-start(bf16[1,384,128]{2,1,0:T(8,128)(2,1)S(1)} %get-tuple-element.69.order_ref), channel_id=1, source_target_pairs={{0,8},{1,9},{2,10},{3,11},{4,12},{5,13},{6,14},{7,15},{8,0},{9,1},... | collective-permute-start | bytes 294920 | tf_op jit(solution)/shard_map/ppermute | solution.py:431
  47.3 0.0 collective-permute-done.8.received_ref
  47.3 2.5 %collective-permute-start.12 = (bf16[2,128,128]{2,1,0:T(8,128)(2,1)S(1)}, bf16[2,128,128]{2,1,0:T(8,128)(2,1)S(1)}, u32[]{:S(2)}, u32[]{:S(2)}) collective-permute-start(bf16[2,128,128]{2,1,0:T(8,128)(2,1)S(1)} %get-tuple-element.71.order_ref), channel_id=1, source_target_pairs={{0,4},{1,5},{2,6},{3,7},{4,0},{5,1},{6,2},{7,3},{8,12},{9,13},{10,... | collective-permute-start | bytes 196616 | tf_op jit(solution)/shard_map/ppermute | solution.py:431
  49.9 0.0 collective-permute-start.16
  49.9 0.0 collective-permute-done.13.received_ref
  49.9 0.7 %collective-permute-start.15 = (bf16[1,256,128]{2,1,0:T(8,128)(2,1)S(1)}, bf16[1,256,128]{2,1,0:T(8,128)(2,1)S(1)}, u32[]{:S(2)}, u32[]{:S(2)}) collective-permute-start(bf16[1,256,128]{2,1,0:T(8,128)(2,1)S(1)} %get-tuple-element.73.order_ref), channel_id=1, source_target_pairs={{0,8},{1,9},{2,10},{3,11},{4,12},{5,13},{6,14},{7,15},{8,0},{9,1},... | collective-permute-start | bytes 196616 | tf_op jit(solution)/shard_map/ppermute | solution.py:431
  50.7 1.5 %collective-permute-done.12.received_ref = bf16[2,128,128]{2,1,0:T(8,128)(2,1)S(1)} collective-permute-done((bf16[2,128,128]{2,1,0:T(8,128)(2,1)S(1)}, bf16[2,128,128]{2,1,0:T(8,128)(2,1)S(1)}, u32[]{:S(2)}, u32[]{:S(2)}) %collective-permute-start.12) | collective-permute-done | bytes 65568 | tf_op jit(solution)/shard_map/ppermute | solution.py:431
  52.1 2.0 %collective-permute-start.17 = (bf16[1,128,128]{2,1,0:T(8,128)(2,1)S(1)}, bf16[1,128,128]{2,1,0:T(8,128)(2,1)S(1)}, u32[]{:S(2)}, u32[]{:S(2)}) collective-permute-start(bf16[1,128,128]{2,1,0:T(8,128)(2,1)S(1)} %get-tuple-element.74.order_ref), channel_id=1, source_target_pairs={{0,8},{1,9},{2,10},{3,11},{4,12},{5,13},{6,14},{7,15},{8,0},{9,1},... | collective-permute-start | bytes 98312 | tf_op jit(solution)/shard_map/ppermute | solution.py:431
  54.2 0.0 collective-permute-done.7.received_ref
  54.2 1.9 %collective-permute-done.14.received_ref = bf16[1,384,128]{2,1,0:T(8,128)(2,1)S(1)} collective-permute-done((bf16[1,384,128]{2,1,0:T(8,128)(2,1)S(1)}, bf16[1,384,128]{2,1,0:T(8,128)(2,1)S(1)}, u32[]{:S(2)}, u32[]{:S(2)}) %collective-permute-start.14) | collective-permute-done | bytes 98336 | tf_op jit(solution)/shard_map/ppermute | solution.py:431
  56.1 0.7 %collective-permute-done.15.received_ref = bf16[1,256,128]{2,1,0:T(8,128)(2,1)S(1)} collective-permute-done((bf16[1,256,128]{2,1,0:T(8,128)(2,1)S(1)}, bf16[1,256,128]{2,1,0:T(8,128)(2,1)S(1)}, u32[]{:S(2)}, u32[]{:S(2)}) %collective-permute-start.15) | collective-permute-done | bytes 65568 | tf_op jit(solution)/shard_map/ppermute | solution.py:431
  56.8 0.0 collective-permute-done.16.received_ref
  56.9 0.3 collective-permute-done.17.refs_5_
  57.2 0.8 %gather.1 = bf16[1,384,512]{2,1,0:T(8,128)(2,1)} custom-call(bf16[384,128]{1,0:T(8,128)(2,1)S(1)} %finish.4.order_ref.refs_0_, bf16[384,128]{1,0:T(8,128)(2,1)S(1)} %finish.5.order_ref.refs_1_, bf16[256,128]{1,0:T(8,128)(2,1)S(1)} %finish.6.order_ref.refs_2_, bf16[384,128]{1,0:T(8,128)(2,1)S(1)} %finish.7.refs_3_.refs_6_, ...), custom_call_target="tpu_custom_call" | custom-call | flops 1 | bytes 1 | tf_op jit(solution)/shard_map/gather/pallas_call | solution.py:402
  (11 shorter events, 0.3 us)
Async XLA Ops:
  0.1 7.0 %copy-start = (bf16[3,1,384,512]{3,2,1,0:T(8,128)(2,1)S(1)}, bf16[3,1,384,512]{3,2,1,0:T(8,128)(2,1)}, u32[]{:S(2)}) copy-start(bf16[3,1,384,512]{3,2,1,0:T(8,128)(2,1)} %head_in_ref.1) | copy-start | bytes 3538948
  0.1 7.0 %copy-start.1 = (f32[3,7,512]{2,1,0:T(8,128)S(1)}, f32[3,7,512]{2,1,0:T(8,128)}, u32[]{:S(2)}) copy-start(f32[3,7,512]{2,1,0:T(8,128)} %taps_ref.3) | copy-start | bytes 129028
  0.1 7.0 %copy-start.2 = (f32[16,512]{1,0:T(8,128)S(1)}, f32[16,512]{1,0:T(8,128)}, u32[]{:S(2)}) copy-start(f32[16,512]{1,0:T(8,128)} %decay_ref.3) | copy-start | bytes 98308
  0.1 7.0 %copy-start.4 = (f32[16,512]{1,0:T(8,128)S(1)}, f32[16,512]{1,0:T(8,128)}, u32[]{:S(2)}) copy-start(f32[16,512]{1,0:T(8,128)} %residues_ref.3) | copy-start | bytes 98308
  4.0 9.7 %collective-permute-start.2 = (bf16[8,512,512]{2,1,0:T(8,128)(2,1)S(1)}, bf16[8,512,512]{2,1,0:T(8,128)(2,1)S(1)}, u32[]{:S(2)}, u32[]{:S(2)}) collective-permute-start(bf16[8,512,512]{2,1,0:T(8,128)(2,1)S(1)} %get-tuple-element.48), channel_id=1, source_target_pairs={{0,1},{1,0},{2,3},{3,2},{4,5},{5,4},{6,7},{7,6},{8,9},{9,8},{10,11... | collective-permute-start | bytes 12582920 | tf_op jit(solution)/shard_map/ppermute | solution.py:431
  4.5 5.6 %collective-permute-start = (f32[40,512]{1,0:T(8,128)S(1)}, f32[40,512]{1,0:T(8,128)S(1)}, u32[]{:S(2)}, u32[]{:S(2)}) collective-permute-start(f32[40,512]{1,0:T(8,128)S(1)} %get-tuple-element.42), channel_id=1, source_target_pairs={{0,16},{16,0},{1,17},{17,1},{2,18},{18,2},{3,19},{19,3},{4,20},{20... | collective-permute-start | bytes 245768 | tf_op jit(solution)/shard_map/ppermute | solution.py:436
  7.1 3.0 %copy-start.3 = (f32[1,16,512]{2,1,0:T(8,128)S(1)}, f32[1,16,512]{2,1,0:T(8,128)}, u32[]{:S(2)}) copy-start(f32[1,16,512]{2,1,0:T(8,128)} %init_ref.1) | copy-start | bytes 98308
  11.9 1.8 %collective-permute-start.1 = (bf16[384,512]{1,0:T(8,128)(2,1)S(1)}, bf16[384,512]{1,0:T(8,128)(2,1)S(1)}, u32[]{:S(2)}, u32[]{:S(2)}) collective-permute-start(bf16[384,512]{1,0:T(8,128)(2,1)S(1)} %gated.1.own_ref), channel_id=1, source_target_pairs={{0,1},{1,0},{2,3},{3,2},{4,5},{5,4},{6,7},{7,6},{8,9},{9,8},{10,11... | collective-permute-start | bytes 1179656 | tf_op jit(solution)/shard_map/ppermute | solution.py:431
  14.8 12.0 %collective-permute-start.3 = (bf16[4,384,128]{2,1,0:T(8,128)(2,1)S(1)}, bf16[4,384,128]{2,1,0:T(8,128)(2,1)S(1)}, u32[]{:S(2)}, u32[]{:S(2)}) collective-permute-start(bf16[4,384,128]{2,1,0:T(8,128)(2,1)S(1)} %get-tuple-element.50.order_ref), channel_id=1, source_target_pairs={{0,2},{1,3},{2,0},{3,1},{4,6},{5,7},{6,4},{7,5},{8,10},{9,11},{10,... | collective-permute-start | bytes 1179656 | tf_op jit(solution)/shard_map/ppermute | solution.py:431
  18.2 11.8 %collective-permute-start.6 = (bf16[4,384,128]{2,1,0:T(8,128)(2,1)S(1)}, bf16[4,384,128]{2,1,0:T(8,128)(2,1)S(1)}, u32[]{:S(2)}, u32[]{:S(2)}) collective-permute-start(bf16[4,384,128]{2,1,0:T(8,128)(2,1)S(1)} %get-tuple-element.51.order_ref), channel_id=1, source_target_pairs={{0,4},{1,5},{2,6},{3,7},{4,0},{5,1},{6,2},{7,3},{8,12},{9,13},{10,... | collective-permute-start | bytes 1179656 | tf_op jit(solution)/shard_map/ppermute | solution.py:431
  21.3 13.9 %collective-permute-start.5 = (bf16[4,384,128]{2,1,0:T(8,128)(2,1)S(1)}, bf16[4,384,128]{2,1,0:T(8,128)(2,1)S(1)}, u32[]{:S(2)}, u32[]{:S(2)}) collective-permute-start(bf16[4,384,128]{2,1,0:T(8,128)(2,1)S(1)} %get-tuple-element.52.order_ref), channel_id=1, source_target_pairs={{0,2},{1,3},{2,0},{3,1},{4,6},{5,7},{6,4},{7,5},{8,10},{9,11},{10,... | collective-permute-start | bytes 1179656 | tf_op jit(solution)/shard_map/ppermute | solution.py:431
  23.2 17.7 %collective-permute-start.10 = (bf16[4,256,128]{2,1,0:T(8,128)(2,1)S(1)}, bf16[4,256,128]{2,1,0:T(8,128)(2,1)S(1)}, u32[]{:S(2)}, u32[]{:S(2)}) collective-permute-start(bf16[4,256,128]{2,1,0:T(8,128)(2,1)S(1)} %get-tuple-element.53.order_ref), channel_id=1, source_target_pairs={{0,2},{1,3},{2,0},{3,1},{4,6},{5,7},{6,4},{7,5},{8,10},{9,11},{10,... | collective-permute-start | bytes 786440 | tf_op jit(solution)/shard_map/ppermute | solution.py:431
  26.9 11.8 %collective-permute-start.4 = (bf16[2,384,128]{2,1,0:T(8,128)(2,1)S(1)}, bf16[2,384,128]{2,1,0:T(8,128)(2,1)S(1)}, u32[]{:S(2)}, u32[]{:S(2)}) collective-permute-start(bf16[2,384,128]{2,1,0:T(8,128)(2,1)S(1)} %get-tuple-element.56.order_ref), channel_id=1, source_target_pairs={{0,4},{1,5},{2,6},{3,7},{4,0},{5,1},{6,2},{7,3},{8,12},{9,13},{10,... | collective-permute-start | bytes 589832 | tf_op jit(solution)/shard_map/ppermute | solution.py:431
  30.0 10.5 %collective-permute-start.11 = (bf16[2,384,128]{2,1,0:T(8,128)(2,1)S(1)}, bf16[2,384,128]{2,1,0:T(8,128)(2,1)S(1)}, u32[]{:S(2)}, u32[]{:S(2)}) collective-permute-start(bf16[2,384,128]{2,1,0:T(8,128)(2,1)S(1)} %get-tuple-element.59.order_ref), channel_id=1, source_target_pairs={{0,8},{1,9},{2,10},{3,11},{4,12},{5,13},{6,14},{7,15},{8,0},{9,1},... | collective-permute-start | bytes 589832 | tf_op jit(solution)/shard_map/ppermute | solution.py:431
  35.4 10.1 %collective-permute-start.9 = (bf16[2,384,128]{2,1,0:T(8,128)(2,1)S(1)}, bf16[2,384,128]{2,1,0:T(8,128)(2,1)S(1)}, u32[]{:S(2)}, u32[]{:S(2)}) collective-permute-start(bf16[2,384,128]{2,1,0:T(8,128)(2,1)S(1)} %get-tuple-element.60.order_ref), channel_id=1, source_target_pairs={{0,4},{1,5},{2,6},{3,7},{4,0},{5,1},{6,2},{7,3},{8,12},{9,13},{10,... | collective-permute-start | bytes 589832 | tf_op jit(solution)/shard_map/ppermute | solution.py:431
  37.2 10.1 %collective-permute-start.8 = (bf16[4,128,128]{2,1,0:T(8,128)(2,1)S(1)}, bf16[4,128,128]{2,1,0:T(8,128)(2,1)S(1)}, u32[]{:S(2)}, u32[]{:S(2)}) collective-permute-start(bf16[4,128,128]{2,1,0:T(8,128)(2,1)S(1)} %get-tuple-element.54.order_ref), channel_id=1, source_target_pairs={{0,2},{1,3},{2,0},{3,1},{4,6},{5,7},{6,4},{7,5},{8,10},{9,11},{10,... | collective-permute-start | bytes 393224 | tf_op jit(solution)/shard_map/ppermute | solution.py:431
  41.0 8.9 %collective-permute-start.13 = (bf16[2,256,128]{2,1,0:T(8,128)(2,1)S(1)}, bf16[2,256,128]{2,1,0:T(8,128)(2,1)S(1)}, u32[]{:S(2)}, u32[]{:S(2)}) collective-permute-start(bf16[2,256,128]{2,1,0:T(8,128)(2,1)S(1)} %get-tuple-element.68.order_ref), channel_id=1, source_target_pairs={{0,4},{1,5},{2,6},{3,7},{4,0},{5,1},{6,2},{7,3},{8,12},{9,13},{10,... | collective-permute-start | bytes 393224 | tf_op jit(solution)/shard_map/ppermute | solution.py:431
  42.8 11.3 %collective-permute-start.7 = (bf16[1,384,128]{2,1,0:T(8,128)(2,1)S(1)}, bf16[1,384,128]{2,1,0:T(8,128)(2,1)S(1)}, u32[]{:S(2)}, u32[]{:S(2)}) collective-permute-start(bf16[1,384,128]{2,1,0:T(8,128)(2,1)S(1)} %get-tuple-element.62.order_ref), channel_id=1, source_target_pairs={{0,8},{1,9},{2,10},{3,11},{4,12},{5,13},{6,14},{7,15},{8,0},{9,1},... | collective-permute-start | bytes 294920 | tf_op jit(solution)/shard_map/ppermute | solution.py:431
  45.5 10.6 %collective-permute-start.14 = (bf16[1,384,128]{2,1,0:T(8,128)(2,1)S(1)}, bf16[1,384,128]{2,1,0:T(8,128)(2,1)S(1)}, u32[]{:S(2)}, u32[]{:S(2)}) collective-permute-start(bf16[1,384,128]{2,1,0:T(8,128)(2,1)S(1)} %get-tuple-element.69.order_ref), channel_id=1, source_target_pairs={{0,8},{1,9},{2,10},{3,11},{4,12},{5,13},{6,14},{7,15},{8,0},{9,1},... | collective-permute-start | bytes 294920 | tf_op jit(solution)/shard_map/ppermute | solution.py:431
  47.3 4.8 %collective-permute-start.12 = (bf16[2,128,128]{2,1,0:T(8,128)(2,1)S(1)}, bf16[2,128,128]{2,1,0:T(8,128)(2,1)S(1)}, u32[]{:S(2)}, u32[]{:S(2)}) collective-permute-start(bf16[2,128,128]{2,1,0:T(8,128)(2,1)S(1)} %get-tuple-element.71.order_ref), channel_id=1, source_target_pairs={{0,4},{1,5},{2,6},{3,7},{4,0},{5,1},{6,2},{7,3},{8,12},{9,13},{10,... | collective-permute-start | bytes 196616 | tf_op jit(solution)/shard_map/ppermute | solution.py:431
  49.9 6.9 %collective-permute-start.16 = (bf16[1,384,128]{2,1,0:T(8,128)(2,1)S(1)}, bf16[1,384,128]{2,1,0:T(8,128)(2,1)S(1)}, u32[]{:S(2)}, u32[]{:S(2)}) collective-permute-start(bf16[1,384,128]{2,1,0:T(8,128)(2,1)S(1)} %get-tuple-element.67.order_ref), channel_id=1, source_target_pairs={{0,2},{1,3},{2,0},{3,1},{4,6},{5,7},{6,4},{7,5},{8,10},{9,11},{10,... | collective-permute-start | bytes 294920 | tf_op jit(solution)/shard_map/ppermute | solution.py:431
  49.9 6.9 %collective-permute-start.15 = (bf16[1,256,128]{2,1,0:T(8,128)(2,1)S(1)}, bf16[1,256,128]{2,1,0:T(8,128)(2,1)S(1)}, u32[]{:S(2)}, u32[]{:S(2)}) collective-permute-start(bf16[1,256,128]{2,1,0:T(8,128)(2,1)S(1)} %get-tuple-element.73.order_ref), channel_id=1, source_target_pairs={{0,8},{1,9},{2,10},{3,11},{4,12},{5,13},{6,14},{7,15},{8,0},{9,1},... | collective-permute-start | bytes 196616 | tf_op jit(solution)/shard_map/ppermute | solution.py:431
  52.1 5.0 %collective-permute-start.17 = (bf16[1,128,128]{2,1,0:T(8,128)(2,1)S(1)}, bf16[1,128,128]{2,1,0:T(8,128)(2,1)S(1)}, u32[]{:S(2)}, u32[]{:S(2)}) collective-permute-start(bf16[1,128,128]{2,1,0:T(8,128)(2,1)S(1)} %get-tuple-element.74.order_ref), channel_id=1, source_target_pairs={{0,8},{1,9},{2,10},{3,11},{4,12},{5,13},{6,14},{7,15},{8,0},{9,1},... | collective-permute-start | bytes 98312 | tf_op jit(solution)/shard_map/ppermute | solution.py:431
